TPU v7x, 32 devices: a whole 2x2x4 slice. The times are simulated.
32 devices in a mesh: grp: 2 (over x), ctx: 16 (over z, y, core).
Axes of the slice: x: 2, y: 2, z: 4, core: 2. Of those that a mesh axis runs over, the one named last changes fastest.
Arguments:
- queries: bfloat16 [4, 4, 128, 576], P('grp', None, 'ctx'), parts along dimension 0, may hold values from -40 to 40
- latent_cache: bfloat16 [4, 32768, 576], P('grp', 'ctx'), parts along dimension 0, may hold values from -64 to 64
- lengths: int32 [4], P('grp'), parts along dimension 0, may hold values from 16384 to 32768
- draft_mask: int32 [4, 4], P('grp'), parts along dimension 0, may hold values 0 or 1
- value_up: bfloat16 [128, 512, 128], P('ctx'), may hold values from -0.8984375 to 0.8984375
- output_weight: bfloat16 [16384, 7168], P('ctx'), may hold values from -0.046875 to 0.046875
Outputs:
- reduced: bfloat16 [4, 4, 7168], P('grp', None, 'ctx'), parts along dimension 0
There are 2 independent parts, one for each index of `grp`. A program takes and returns all parts, laid end to end along the dimension named above; an argument that names none is the same for every part. Nothing has to cross between parts.
Inputs may be any that keep to these rules, and one draw needn't show every extreme that they name: `lengths`: each request has at least 16384 cached positions, so every row sees some position.
All inputs are finite; a program needn't handle non-finite values.
Results may differ from a plain program's by a relative error of at most 0.015.
Values may be sent and summed in bfloat16 or wider, within the bound.
No kernel may reach another device: no remote copies, remote signals or barrier semaphores. Data moves between devices by JAX's collectives and lax.ppermute only.
A program may use at most 64 MiB of HBM per device.

v0:
```python
import jax
import jax.numpy as jnp
from jax import lax
from jax.sharding import PartitionSpec as P

SOFTMAX_SCALE = 192.0 ** (-0.5)
SCORE_FLOOR = -1e30


def on_device(queries, latent_cache, lengths, draft_mask, value_up, output_weight):
    gathered = lax.all_gather(queries, "ctx", axis=2, tiled=True)
    requests, drafts, head_count, feature = gathered.shape
    ctx_local = latent_cache.shape[1]
    latent = value_up.shape[1]
    offset = lax.axis_index("ctx") * ctx_local
    stacked = gathered.reshape(requests, drafts * head_count, feature)
    scores = (
        jnp.einsum("rqw,rcw->rqc", stacked, latent_cache, preferred_element_type=jnp.float32)
        * SOFTMAX_SCALE
    )
    scores = scores.reshape(requests, drafts, head_count, ctx_local)
    position = offset + jnp.arange(ctx_local, dtype=jnp.int32)
    horizon = lengths[:, None] - drafts + 1 + jnp.arange(drafts, dtype=jnp.int32)[None, :]
    visible = (position[None, None, :] < horizon[:, :, None])[:, :, None, :]
    peak = jnp.max(jnp.where(visible, scores, SCORE_FLOOR), axis=-1)
    weights = jnp.where(visible, jnp.exp(scores - peak[..., None]), 0.0)
    denominator = jnp.sum(weights, axis=-1)
    weights_low = weights.astype(jnp.bfloat16).reshape(requests, drafts * head_count, ctx_local)
    numerator = jnp.einsum(
        "rqc,rcl->rql", weights_low, latent_cache[:, :, :latent], preferred_element_type=jnp.float32
    )
    numerator = numerator.reshape(requests, drafts, head_count, latent)
    received = (
        lax.all_to_all(numerator[None], "ctx", split_axis=3, concat_axis=0, tiled=True),
        lax.all_to_all(peak[None], "ctx", split_axis=3, concat_axis=0, tiled=True),
        lax.all_to_all(denominator[None], "ctx", split_axis=3, concat_axis=0, tiled=True),
    )
    numer_all, peak_all, denom_all = received
    largest = jnp.max(peak_all, axis=0)
    factor = jnp.exp(peak_all - largest)
    upper = jnp.sum(factor[..., None] * numer_all, axis=0)
    lower = jnp.sum(factor * denom_all, axis=0)
    attended = (upper / lower[..., None]).astype(jnp.bfloat16)
    values = jnp.einsum(
        "rshc,hcd->rshd", attended, value_up, preferred_element_type=jnp.float32
    ).astype(jnp.bfloat16)
    values = values.reshape(requests * drafts, -1)
    partial_out = jnp.dot(values, output_weight, preferred_element_type=jnp.float32).reshape(
        requests, drafts, -1
    )
    reduced = lax.psum_scatter(partial_out, "ctx", scatter_dimension=2, tiled=True)
    return (reduced * draft_mask[..., None].astype(jnp.float32)).astype(jnp.bfloat16)


def solution(mesh):
    return jax.shard_map(
        on_device,
        mesh=mesh,
        in_specs=(
            P("grp", None, "ctx", None),
            P("grp", "ctx", None),
            P("grp"),
            P("grp", None),
            P("ctx", None, None),
            P("ctx", None),
        ),
        out_specs=P("grp", None, "ctx"),
        check_vma=False,
    )
```

profile of v0, /device:TPU:0, one launch (start us, length us, event | category | flops | bytes accessed | tf_op | source)
XLA Modules:
  0.0 240.2 jit_solution(5961044993891589604)
XLA Ops:
  6.5 0.0 all-gather.2.cloned.1.call-start
  6.5 0.7 all-gather.2.cloned.1.call-update
  7.3 0.7 broadcast_add_fusion
  7.9 0.1 iota_add_fusion.1
  8.0 0.1 broadcast_compare_fusion
  8.1 43.1 %all-gather.2.cloned.1.call-done = bf16[2,4,128,576]{3,2,1,0:T(8,128)(2,1)} async-done(((bf16[2,4,8,576]{3,2,1,0:T(8,128)(2,1)}), bf16[2,4,128,576]{3,2,1,0:T(8,128)(2,1)}) %all-gather.2.cloned.1.call-update) | async-done | bytes 1179664 | tf_op jit(solution)/shard_map/all_gather | solution.py:11
  51.2 6.1 %fusion.2 = (f32[2,512]{1,0:T(2,128)S(1)}, f32[2,512,2048]{2,1,0:T(8,128)S(1)}) fusion(pred[2,4,2048]{2,1,0:T(4,128)(4,1)S(1)} %broadcast_compare_fusion, bf16[2,512,576]{2,1,0:T(8,128)(2,1)} %bitcast.57, bf16[2,2048,576]{1,2,0:T(8,128)(2,1)} %param.7), kind=kOutput, calls=%fused_computation.4 | convolution fusion | flops 2422209536 | bytes 14307328 | tf_op jit(solution)/shard_map/rqw,rcw->rqc/dot_general | solution.py:18
  57.3 3.4 %fusion.3 = (f32[2,512]{1,0:T(2,128)S(1)}, bf16[2,512,2048]{2,1,0:T(8,128)(2,1)}) fusion(f32[2,512,2048]{2,1,0:T(8,128)S(1)} %get-tuple-element.10, f32[2,512]{1,0:T(2,128)S(1)} %get-tuple-element.9, pred[2,4,2048]{2,1,0:T(4,128)(4,1)S(1)} %broadcast_compare_fusion), kind=kLoop, calls=%fused_computation.5 | loop fusion | flops 10484736 | bytes 12607488 | tf_op jit(solution)/shard_map/reduce_sum | solution.py:27
  60.8 0.8 copy.26
  61.6 3.7 %all-to-all-start.2 = ((f32[1,2,4,128]{2,1,0,3:T(2,128)}), f32[1,2,4,128]{2,1,0,3:T(2,128)S(1)}, u32[]{:S(2)}, u32[]{:S(2)}) async-start(f32[1,2,4,128]{2,1,0,3:T(2,128)} %copy.26), calls=%async_computation.2 | async-start | bytes 262144 | tf_op jit(solution)/shard_map/all_to_all | solution.py:36
  65.3 0.8 copy.21
  66.1 7.1 %all-to-all-done.2 = f32[1,2,4,128]{2,1,0,3:T(2,128)S(1)} async-done(((f32[1,2,4,128]{2,1,0,3:T(2,128)}), f32[1,2,4,128]{2,1,0,3:T(2,128)S(1)}, u32[]{:S(2)}, u32[]{:S(2)}) %all-to-all-start.2) | async-done | bytes 4128 | tf_op jit(solution)/shard_map/all_to_all | solution.py:36
  73.2 3.5 %all-to-all-start = ((f32[1,2,4,128]{2,1,0,3:T(2,128)}), f32[1,2,4,128]{2,1,0,3:T(2,128)S(1)}, u32[]{:S(2)}, u32[]{:S(2)}) async-start(f32[1,2,4,128]{2,1,0,3:T(2,128)} %copy.21), calls=%async_computation | async-start | bytes 262144 | tf_op jit(solution)/shard_map/all_to_all | solution.py:35
  76.7 5.8 %fusion.5 = f32[2,512,512]{2,1,0:T(8,128)S(1)} fusion(bf16[2,512,2048]{2,1,0:T(8,128)(2,1)} %get-tuple-element.8, bf16[2,2048,576]{1,2,0:T(8,128)(2,1)} %param.7), kind=kOutput, calls=%fused_computation.7 | convolution fusion | flops 2147483648 | bytes 10485760 | tf_op jit(solution)/shard_map/rqc,rcl->rql/dot_general | solution.py:29
  82.6 2.7 %copy.24 = f32[1,2,4,128,512]{4,2,1,0,3:T(4,128)} copy(f32[1,2,4,128,512]{4,3,2,1,0:T(8,128)S(1)} %bitcast.55) | data formatting | bytes 4194304 | tf_op jit(solution)/shard_map/broadcast_in_dim;reshape | solution.py:34
  85.3 0.0 all-to-all-done
  85.3 6.0 %all-to-all-start.1 = ((f32[1,2,4,128,512]{4,2,1,0,3:T(4,128)}), f32[1,2,4,128,512]{4,2,1,0,3:T(4,128)S(1)}, u32[]{:S(2)}, u32[]{:S(2)}) async-start(f32[1,2,4,128,512]{4,2,1,0,3:T(4,128)} %copy.24), calls=%async_computation.1 | async-start | bytes 4194304 | tf_op jit(solution)/shard_map/all_to_all | solution.py:34
  91.3 0.2 reduce-scatter.4.cloned.1.call-start
  91.5 0.3 copy.33
  91.8 0.3 copy.32
  92.1 40.2 %all-to-all-done.1 = f32[1,2,4,128,512]{4,2,1,0,3:T(4,128)S(1)} async-done(((f32[1,2,4,128,512]{4,2,1,0,3:T(4,128)}), f32[1,2,4,128,512]{4,2,1,0,3:T(4,128)S(1)}, u32[]{:S(2)}, u32[]{:S(2)}) %all-to-all-start.1) | async-done | bytes 2097184 | tf_op jit(solution)/shard_map/all_to_all | solution.py:34
  132.4 1.1 fusion.7
  133.5 0.1 divide_convert_fusion
  133.6 0.3 fusion.8
  133.9 7.3 %fusion = f32[2,4,7168]{2,1,0:T(4,128)S(1)} fusion(bf16[1024,7168]{1,0:T(8,128)(2,1)} %param.11, bf16[8,2,1,4,128]{4,3,2,1,0:T(4,128)(2,1)S(1)} %fusion.8), kind=kOutput, calls=%fused_computation | convolution fusion | flops 117440512 | bytes 14925824 | tf_op jit(solution)/shard_map/dot_general | solution.py:48
  141.1 6.9 %copy.34 = f32[2,4,7168]{1,0,2:T(2,128)} copy(f32[2,4,7168]{2,1,0:T(4,128)S(1)} %fusion) | data formatting | bytes 458752
  148.0 7.9 %reshape.63 = f32[7168,8]{1,0:T(8,128)} reshape(f32[7168,2,4]{2,1,0:T(2,128)} %bitcast.53) | data formatting | bytes 458752
  156.0 0.0 reduce-scatter.4.cloned.1.call-update
  156.0 75.3 %reduce-scatter.4.cloned.1.call-done = f32[448,8]{1,0:T(8,128)} async-done(((f32[7168,8]{1,0:T(8,128)}), f32[448,8]{1,0:T(8,128)}) %reduce-scatter.4.cloned.1.call-update) | async-done | bytes 14352
  231.3 1.2 reshape.64
  232.5 0.2 copy.35
  232.7 0.7 multiply_convert_fusion
  (10 shorter events, 0.1 us)
Async XLA Ops:
  6.5 127.1 %copy-start = (bf16[8,512,128]{2,1,0:T(8,128)(2,1)S(1)}, bf16[8,512,128]{2,1,0:T(8,128)(2,1)}, u32[]{:S(2)}) copy-start(bf16[8,512,128]{2,1,0:T(8,128)(2,1)} %param.10) | copy-start | bytes 3145732
  6.5 44.7 %all-gather.2.cloned.1.call-start = ((), (), s32[]{:S(2)}) async-start(), calls=%async_computation.4 | async-start | bytes 1392640 | tf_op jit(solution)/shard_map/all_gather | solution.py:11
  61.6 11.6 %all-to-all-start.2 = ((f32[1,2,4,128]{2,1,0,3:T(2,128)}), f32[1,2,4,128]{2,1,0,3:T(2,128)S(1)}, u32[]{:S(2)}, u32[]{:S(2)}) async-start(f32[1,2,4,128]{2,1,0,3:T(2,128)} %copy.26), calls=%async_computation.2 | async-start | bytes 262144 | tf_op jit(solution)/shard_map/all_to_all | solution.py:36
  73.2 12.1 %all-to-all-start = ((f32[1,2,4,128]{2,1,0,3:T(2,128)}), f32[1,2,4,128]{2,1,0,3:T(2,128)S(1)}, u32[]{:S(2)}, u32[]{:S(2)}) async-start(f32[1,2,4,128]{2,1,0,3:T(2,128)} %copy.21), calls=%async_computation | async-start | bytes 262144 | tf_op jit(solution)/shard_map/all_to_all | solution.py:35
  85.3 47.1 %all-to-all-start.1 = ((f32[1,2,4,128,512]{4,2,1,0,3:T(4,128)}), f32[1,2,4,128,512]{4,2,1,0,3:T(4,128)S(1)}, u32[]{:S(2)}, u32[]{:S(2)}) async-start(f32[1,2,4,128,512]{4,2,1,0,3:T(4,128)} %copy.24), calls=%async_computation.1 | async-start | bytes 4194304 | tf_op jit(solution)/shard_map/all_to_all | solution.py:34
  91.3 140.0 %reduce-scatter.4.cloned.1.call-start = ((), (), s32[]{:S(2)}) async-start(), calls=%async_computation.5 | async-start | bytes 3899392
  148.0 8.0 %copy-start.1 = (s32[2,4]{1,0:T(2,128)S(1)}, s32[2,4]{1,0:T(2,128)}, u32[]{:S(2)}) copy-start(s32[2,4]{1,0:T(2,128)} %param.9) | copy-start | bytes 100
Sparse Core Ops, SparseCore 0:
  9.7 41.5 all-gather.1
  156.1 75.1 reduce-scatter.3
where the time goes:
time: 241 us; the launch traced here: 240 us
  waiting for transfers between devices  166 us (69%)
  local copies, waits for them, and re-layouts  21.1 us (9%)
  matrix products  19.5 us (8%)
  between operations  13.5 us (6%)
  starting transfers between devices  13.4 us (6%)
  other arithmetic  6.25 us (3%)
    unnamed x3, waiting for transfers between devices  76 us
    all_gather x1, waiting for transfers between devices, on_device(): gathered = lax.all_gather(queries, 'ctx', axis=2, tiled=True)  43.1 us
    all_to_all x1, waiting for transfers between devices, on_device(): lax.all_to_all(numerator[None], 'ctx', split_axis=3, concat_axis=0, tiled...  40.2 us
    unnamed x8, local copies, waits for them, and re-layouts  16.2 us
    dot_general x1, matrix products, on_device(): jnp.dot(values, output_weight, preferred_element_type=jnp.float32)  7.27 us
    all_to_all x1, waiting for transfers between devices, on_device(): lax.all_to_all(denominator[None], 'ctx', split_axis=3, concat_axis=0, til...  7.13 us
    dot_general x1, matrix products, on_device(): jnp.einsum('rqw,rcw->rqc', stacked, latent_cache, preferred_element_type=...  6.1 us
    all_to_all x1, starting transfers between devices, on_device(): lax.all_to_all(numerator[None], 'ctx', split_axis=3, concat_axis=0, tiled...  5.98 us
  transfers between devices with their start and end apart: 5, of which 4 were waited for; matrix products, arithmetic and copies ran while one was open for 4% of the time, Pallas kernels for 0%

commit v1 on v0

v1 whole, which is shorter than its diff:
```python
import functools
import math

import jax
import jax.numpy as jnp
from jax import lax
from jax.experimental import pallas as pl
from jax.experimental.pallas import tpu as pltpu
from jax.sharding import PartitionSpec as P

SOFTMAX_SCALE = 192.0 ** (-0.5)
LOG2_SCALE = SOFTMAX_SCALE * math.log2(math.e)
SCORE_FLOOR = -1e30
STAT_LANES = 128
MIB = 1024 * 1024


def split_low(x):
    high = x.astype(jnp.bfloat16).astype(jnp.float32)
    return high, (x - high).astype(jnp.bfloat16).astype(jnp.float32)


def attend_kernel(
    chunks, spec, heads, latent, width, lengths_ref, *refs
):
    q_refs = refs[:chunks]
    own_ref, got_ref = refs[chunks : chunks + 2]
    out_refs = refs[chunks + 2 : 2 * chunks + 2]
    keys, scores, sems = refs[2 * chunks + 2 :]
    me = lax.axis_index("ctx")
    core = lax.rem(me, 2)
    block = own_ref.shape[2]
    per_block = block // width
    steps = 2 * per_block
    copies = []
    for step in range(steps):
        source = own_ref if step < per_block else got_ref
        start = (step % per_block) * width
        copy = pltpu.make_async_copy(
            source.at[core, :, pl.ds(start, width)], keys.at[step], sems.at[step]
        )
        copy.start()
        copies.append(copy)
    queries = jnp.concatenate([ref[...] for ref in q_refs], axis=0)
    rows = queries.shape[0]
    row = lax.broadcasted_iota(jnp.int32, (rows, 1), 0)
    draft = lax.rem(lax.div(row, heads), spec)
    horizon = lengths_ref[core] - spec + 1 + draft
    bases = (me * block, (me + 1 - 2 * core) * block)
    peak = jnp.full((rows, 1), SCORE_FLOOR, jnp.float32)
    for step in range(steps):
        copies[step].wait()
        tile = jnp.dot(queries, keys[step], preferred_element_type=jnp.float32)
        start = bases[step // per_block] + (step % per_block) * width
        position = start + lax.broadcasted_iota(jnp.int32, (1, width), 1)
        tile = jnp.where(position < horizon, tile * LOG2_SCALE, SCORE_FLOOR)
        scores[step] = tile
        peak = jnp.maximum(peak, jnp.max(tile, axis=1, keepdims=True))
    peak_high, peak_low = split_low(jnp.maximum(peak, 0.1 * SCORE_FLOOR))
    peak = peak_high + peak_low
    denominator = jnp.zeros((rows, 1), jnp.float32)
    numerator = jnp.zeros((rows, latent), jnp.float32)
    for step in range(steps):
        weights = jnp.exp2(scores[step] - peak)
        denominator += jnp.sum(weights, axis=1, keepdims=True)
        numerator += lax.dot_general(
            weights.astype(jnp.bfloat16),
            keys[step, :latent],
            (((1,), (1,)), ((), ())),
            preferred_element_type=jnp.float32,
        )
    denom_high, denom_low = split_low(denominator)
    lane = lax.broadcasted_iota(jnp.int32, (rows, STAT_LANES), 1)
    stats = jnp.where(lane == 0, peak_high, jnp.where(lane == 1, peak_low, 0.0))
    stats = jnp.where(lane == 2, denom_high, jnp.where(lane == 3, denom_low, stats))
    chunk = rows // chunks
    for i, out_ref in enumerate(out_refs):
        part = slice(i * chunk, (i + 1) * chunk)
        out_ref[:, :latent] = numerator[part].astype(jnp.bfloat16)
        out_ref[:, latent:] = stats[part].astype(jnp.bfloat16)


def attend(lengths, query_chunks, own_keys, got_keys, spec, heads, latent):
    chunks = len(query_chunks)
    chunk, feature = query_chunks[0].shape
    block = own_keys.shape[2]
    width = min(block, 1024)
    steps = 2 * (block // width)
    rows = chunks * chunk
    flops = 2 * rows * 2 * block * (feature + latent)
    return pl.pallas_call(
        functools.partial(attend_kernel, chunks, spec, heads, latent, width),
        out_shape=[jax.ShapeDtypeStruct((chunk, latent + STAT_LANES), jnp.bfloat16)] * chunks,
        in_specs=[pl.BlockSpec(memory_space=pltpu.SMEM)]
        + [pl.BlockSpec(memory_space=pltpu.VMEM)] * chunks
        + [pl.BlockSpec(memory_space=pl.ANY)] * 2,
        out_specs=[pl.BlockSpec(memory_space=pltpu.VMEM)] * chunks,
        scratch_shapes=[
            pltpu.VMEM((steps, feature, width), jnp.bfloat16),
            pltpu.VMEM((steps, rows, width), jnp.float32),
            pltpu.SemaphoreType.DMA((steps,)),
        ],
        compiler_params=pltpu.CompilerParams(vmem_limit_bytes=32 * MIB),
        cost_estimate=pl.CostEstimate(
            flops=flops, bytes_accessed=4 * block * feature, transcendentals=rows * 2 * block
        ),
        name="attend",
    )(lengths, *query_chunks, own_keys, got_keys)


def merge_kernel(parts, latent, *refs):
    in_refs, (own_ref, give_ref) = refs[:parts], refs[parts:]
    peaks, denominators = [], []
    for ref in in_refs:
        stats = ref[:, latent:].astype(jnp.float32)
        peaks.append(stats[:, 0:1] + stats[:, 1:2])
        denominators.append(stats[:, 2:3] + stats[:, 3:4])
    largest = functools.reduce(jnp.maximum, peaks)
    upper, lower = 0.0, 0.0
    for ref, peak, denominator in zip(in_refs, peaks, denominators):
        factor = jnp.exp2(peak - largest)
        upper += factor * ref[:, :latent].astype(jnp.float32)
        lower += factor * denominator
    attended = (upper / lower).astype(jnp.bfloat16)
    half = attended.shape[0] // 2
    own_ref[...] = attended[:half]
    give_ref[...] = attended[half:]


def merge(parts, latent):
    rows = parts[0].shape[0]
    return pl.pallas_call(
        functools.partial(merge_kernel, len(parts), latent),
        out_shape=[jax.ShapeDtypeStruct((rows // 2, latent), jnp.bfloat16)] * 2,
        compiler_params=pltpu.CompilerParams(vmem_limit_bytes=16 * MIB),
        name="merge",
    )(*parts)


def project_kernel(spec, heads, owners, own_ref, got_ref, up_ref, weight_ref, out_ref, values_ref):
    step = pl.program_id(0)

    @pl.when(step == 0)
    def _():
        core = lax.rem(lax.axis_index("ctx"), 2)
        own, got = own_ref[...], got_ref[...]
        first = jnp.where(core == 0, own, got)
        second = jnp.where(core == 0, got, own)
        attended = jnp.concatenate([first, second], axis=0)
        rows = attended.shape[0]
        row = lax.broadcasted_iota(jnp.int32, (rows, 1), 0)
        head = lax.rem(row, heads)
        for h in range(heads):
            tile = jnp.dot(attended, up_ref[h], preferred_element_type=jnp.float32)
            tile = jnp.where(head == h, tile, 0.0)
            tile = jnp.sum(tile.reshape(rows // heads, heads, tile.shape[1]), axis=1)
            wide = tile.shape[1]
            values_ref[:, h * wide : (h + 1) * wide] = tile.astype(jnp.bfloat16)

    tile = jnp.dot(values_ref[...], weight_ref[...], preferred_element_type=jnp.float32)
    columns = out_ref.shape[2]
    for i in range(out_ref.shape[0]):
        out_ref[i] = tile[:, i * columns : (i + 1) * columns].astype(out_ref.dtype)


def project(own, got, value_up, weight, spec, owners):
    heads, latent, wide = value_up.shape
    depth, model = weight.shape
    columns = model // owners
    rows = 2 * spec
    group = next(g for g in (2, 1, 4, 8, 16, owners) if (g * columns) % 128 == 0)
    steps = owners // group
    return pl.pallas_call(
        functools.partial(project_kernel, spec, heads, owners),
        grid=(steps,),
        out_shape=jax.ShapeDtypeStruct((owners, rows, columns), jnp.bfloat16),
        in_specs=[
            pl.BlockSpec(own.shape, lambda i: (0, 0)),
            pl.BlockSpec(got.shape, lambda i: (0, 0)),
            pl.BlockSpec(value_up.shape, lambda i: (0, 0, 0)),
            pl.BlockSpec((depth, group * columns), lambda i: (0, i)),
        ],
        out_specs=pl.BlockSpec((group, rows, columns), lambda i: (i, 0, 0)),
        scratch_shapes=[pltpu.VMEM((rows, depth), jnp.bfloat16)],
        compiler_params=pltpu.CompilerParams(vmem_limit_bytes=24 * MIB),
        name="project",
    )(own, got, value_up, weight)


def finish_kernel(in_ref, mask_ref, out_ref):
    total = jnp.sum(in_ref[...].astype(jnp.float32), axis=0)
    spec = out_ref.shape[1]
    for r in range(out_ref.shape[0]):
        for j in range(spec):
            row = total[r * spec + j : r * spec + j + 1, :]
            kept = row * mask_ref[r, j].astype(jnp.float32)
            out_ref[r, j : j + 1, :] = kept.astype(out_ref.dtype)


def finish(parts, draft_mask):
    owners, rows, columns = parts.shape
    requests, spec = draft_mask.shape
    return pl.pallas_call(
        finish_kernel,
        out_shape=jax.ShapeDtypeStruct((requests, spec, columns), jnp.bfloat16),
        in_specs=[
            pl.BlockSpec(memory_space=pltpu.VMEM),
            pl.BlockSpec(memory_space=pltpu.SMEM),
        ],
        out_specs=pl.BlockSpec(memory_space=pltpu.VMEM),
        compiler_params=pltpu.CompilerParams(vmem_limit_bytes=16 * MIB),
        name="finish",
    )(parts, draft_mask)


def on_device(n, queries, latent_cache, lengths, draft_mask, value_up, output_weight):
    requests, spec, heads, feature = queries.shape
    latent = value_up.shape[1]
    core = lax.rem(lax.axis_index("ctx"), 2)

    def swap(x, bits):
        return lax.ppermute(x, "ctx", [(i, i ^ bits) for i in range(n)])

    chunk = requests * spec * heads
    got = swap(queries, 1)
    both = jnp.stack([queries, got], axis=1)
    mine = lax.dynamic_index_in_dim(both, core, 0, keepdims=False).reshape(chunk, feature)
    own_keys = jnp.swapaxes(latent_cache, 1, 2)
    got_keys = swap(own_keys, 1)

    peers = [2 * k for k in range(1, n // 2)]
    near = peers[: n // 4 - 1]
    far = peers[n // 4 - 1 :]
    far_queries = [swap(mine, bits) for bits in far]
    near_queries = [mine] + [swap(mine, bits) for bits in near]
    shared = (spec, heads, latent)
    near_parts = attend(lengths, near_queries, own_keys, got_keys, *shared)
    far_parts = attend(lengths, far_queries, own_keys, got_keys, *shared)
    parts = [near_parts[0]]
    parts += [swap(part, bits) for part, bits in zip(near_parts[1:], near)]
    parts += [swap(part, bits) for part, bits in zip(far_parts, far)]
    own, give = merge(parts, latent)
    outs = project(own, swap(give, 1), value_up, output_weight, spec, n)
    received = lax.all_to_all(outs, "ctx", 0, 0, tiled=True)
    return finish(received, draft_mask)


def solution(mesh):
    return jax.shard_map(
        functools.partial(on_device, mesh.shape["ctx"]),
        mesh=mesh,
        in_specs=(
            P("grp", None, "ctx", None),
            P("grp", "ctx", None),
            P("grp"),
            P("grp", None),
            P("ctx", None, None),
            P("ctx", None),
        ),
        out_specs=P("grp", None, "ctx"),
        check_vma=False,
    )
```

time: 241 us -> 77.8 us (0.32)
  waiting for transfers between devices: 166 us -> 15.1 us
  matrix products: 19.5 us -> 0 us
  Pallas kernels: 0 us -> 17.5 us
  local copies, waits for them, and re-layouts: 21.1 us -> 4.23 us
  starting transfers between devices: 13.4 us -> 27.7 us
  between operations: 13.5 us -> 0.06 us
  blocking collectives: 0 us -> 12.1 us
  other arithmetic: 6.25 us -> 0.79 us
    unnamed x3 -> x0, waiting for transfers between devices: 76 us -> none
    all_to_all x3 -> x0, waiting for transfers between devices: 47.4 us -> none  [the longest x1 40.2 us: on_device(): lax.all_to_all(numerator[None], 'ctx', split_axis=3, concat_axis=0, tiled...]
    all_gather x1 -> x0, waiting for transfers between devices: 43.1 us -> none  [on_device(): gathered = lax.all_gather(queries, 'ctx', axis=2, tiled=True)]
    ppermute x0 -> x17, starting transfers between devices: none -> 27.7 us  [swap(): return lax.ppermute(x, 'ctx', [(i, i ^ bits) for i in range(n)])]
    dot_general x4 -> x0, matrix products: 19.5 us -> none  [the longest x1 7.27 us: on_device(): jnp.dot(values, output_weight, preferred_element_type=jnp.float32)]
    pallas_call x0 -> x5, Pallas kernels: none -> 17.5 us  [the longest x2 10.8 us: attend(): pl.pallas_call(functools.partial(attend_kernel, chunks, spec, heads, late...]
    ppermute x0 -> x17, waiting for transfers between devices: none -> 15.1 us  [swap(): return lax.ppermute(x, 'ctx', [(i, i ^ bits) for i in range(n)])]
    all_to_all x3 -> x0, starting transfers between devices: 13.2 us -> none  [the longest x1 5.98 us: on_device(): lax.all_to_all(numerator[None], 'ctx', split_axis=3, concat_axis=0, tiled...]
  transfers between devices with their start and end apart: 5 -> 17, of which waited for: 4 -> 9; matrix products, arithmetic and copies ran while one was open for 4% -> 1% of each run, Pallas kernels for 0% -> 14%
where the time goes in v1:
time: 77.8 us; the launch traced here: 77.5 us
  starting transfers between devices  27.7 us (36%)
  Pallas kernels  17.5 us (22%)
  waiting for transfers between devices  15.1 us (19%)
  blocking collectives  12.1 us (16%)
  local copies, waits for them, and re-layouts  4.23 us (5%)
  other arithmetic  0.79 us (1%)
    ppermute x17, starting transfers between devices, swap(): return lax.ppermute(x, 'ctx', [(i, i ^ bits) for i in range(n)])  27.7 us
    ppermute x17, waiting for transfers between devices, swap(): return lax.ppermute(x, 'ctx', [(i, i ^ bits) for i in range(n)])  15.1 us
    all_to_all x1, blocking collectives, on_device(): received = lax.all_to_all(outs, 'ctx', 0, 0, tiled=True)  12.1 us
    pallas_call x2, Pallas kernels, attend(): pl.pallas_call(functools.partial(attend_kernel, chunks, spec, heads, late...  10.8 us
    pallas_call x1, Pallas kernels, project(): pl.pallas_call(functools.partial(project_kernel, spec, heads, owners), gr...  5.08 us
    unnamed x12, local copies, waits for them, and re-layouts  4.23 us
  transfers between devices with their start and end apart: 17, of which 9 were waited for; matrix products, arithmetic and copies ran while one was open for 1% of the time, Pallas kernels for 14%

profile of v1, /device:TPU:0, one launch (start us, length us, event | category | flops | bytes accessed | tf_op | source)
XLA Modules:
  0.0 77.5 jit_solution(14839572669552316156)
XLA Ops:
  0.0 0.5 collective-permute-start.4
  0.5 5.6 %collective-permute-done = bf16[2,4,8,576]{3,2,1,0:T(8,128)(2,1)S(1)} collective-permute-done((bf16[2,4,8,576]{3,2,1,0:T(8,128)(2,1)}, bf16[2,4,8,576]{3,2,1,0:T(8,128)(2,1)S(1)}, u32[]{:S(2)}, u32[]{:S(2)}) %collective-permute-start) | collective-permute-done | bytes 73760 | tf_op jit(solution)/shard_map/ppermute | solution.py:222
  6.1 0.8 %fusion = bf16[1,2,4,8,576]{4,3,2,0,1:T(8,128)(2,1)S(1)} fusion(s32[]{:T(128)S(6)} %select_n.4, bf16[2,1,4,8,576]{4,3,2,0,1:T(8,128)(2,1)} %bitcast.15, bf16[2,1,4,8,576]{4,3,2,0,1:T(8,128)(2,1)S(1)} %bitcast.16), kind=kLoop, calls=%fused_computation.2 | loop fusion | flops 36864 | bytes 221188 | tf_op jit(solution)/shard_map/stack | solution.py:226
  6.9 5.3 %collective-permute-start.10 = (bf16[64,576]{1,0:T(8,128)(2,1)S(1)}, bf16[64,576]{1,0:T(8,128)(2,1)S(1)}, u32[]{:S(2)}, u32[]{:S(2)}) collective-permute-start(bf16[64,576]{1,0:T(8,128)(2,1)S(1)} %bitcast.7), channel_id=1, source_target_pairs={{0,12},{1,13},{2,14},{3,15},{4,8},{5,9},{6,10},{7,11},{8,4},{9,5},... | collective-permute-start | bytes 221192 | tf_op jit(solution)/shard_map/ppermute | solution.py:222
  12.2 1.2 %collective-permute-start.11 = (bf16[64,576]{1,0:T(8,128)(2,1)S(1)}, bf16[64,576]{1,0:T(8,128)(2,1)S(1)}, u32[]{:S(2)}, u32[]{:S(2)}) collective-permute-start(bf16[64,576]{1,0:T(8,128)(2,1)S(1)} %bitcast.8), channel_id=1, source_target_pairs={{0,14},{1,15},{2,12},{3,13},{4,10},{5,11},{6,8},{7,9},{8,6},{9,7},... | collective-permute-start | bytes 221192 | tf_op jit(solution)/shard_map/ppermute | solution.py:222
  13.4 0.8 %collective-permute-start.8 = (bf16[64,576]{1,0:T(8,128)(2,1)S(1)}, bf16[64,576]{1,0:T(8,128)(2,1)S(1)}, u32[]{:S(2)}, u32[]{:S(2)}) collective-permute-start(bf16[64,576]{1,0:T(8,128)(2,1)S(1)} %bitcast.9), channel_id=1, source_target_pairs={{0,8},{1,9},{2,10},{3,11},{4,12},{5,13},{6,14},{7,15},{8,0},{9,1},... | collective-permute-start | bytes 221192 | tf_op jit(solution)/shard_map/ppermute | solution.py:222
  14.2 1.9 %collective-permute-start.9 = (bf16[64,576]{1,0:T(8,128)(2,1)S(1)}, bf16[64,576]{1,0:T(8,128)(2,1)S(1)}, u32[]{:S(2)}, u32[]{:S(2)}) collective-permute-start(bf16[64,576]{1,0:T(8,128)(2,1)S(1)} %bitcast.10), channel_id=1, source_target_pairs={{0,10},{1,11},{2,8},{3,9},{4,14},{5,15},{6,12},{7,13},{8,2},{9,3},... | collective-permute-start | bytes 221192 | tf_op jit(solution)/shard_map/ppermute | solution.py:222
  16.1 1.7 %collective-permute-start.1 = (bf16[64,576]{1,0:T(8,128)(2,1)S(1)}, bf16[64,576]{1,0:T(8,128)(2,1)S(1)}, u32[]{:S(2)}, u32[]{:S(2)}) collective-permute-start(bf16[64,576]{1,0:T(8,128)(2,1)S(1)} %bitcast.11), channel_id=1, source_target_pairs={{0,2},{1,3},{2,0},{3,1},{4,6},{5,7},{6,4},{7,5},{8,10},{9,11},{10,... | collective-permute-start | bytes 221192 | tf_op jit(solution)/shard_map/ppermute | solution.py:222
  17.8 2.5 %collective-permute-done.11.refs_3_ = bf16[64,576]{1,0:T(8,128)(2,1)S(1)} collective-permute-done((bf16[64,576]{1,0:T(8,128)(2,1)S(1)}, bf16[64,576]{1,0:T(8,128)(2,1)S(1)}, u32[]{:S(2)}, u32[]{:S(2)}) %collective-permute-start.11) | collective-permute-done | bytes 73760 | tf_op jit(solution)/shard_map/ppermute | solution.py:222
  20.3 4.9 %collective-permute-start.2 = (bf16[64,576]{1,0:T(8,128)(2,1)S(1)}, bf16[64,576]{1,0:T(8,128)(2,1)S(1)}, u32[]{:S(2)}, u32[]{:S(2)}) collective-permute-start(bf16[64,576]{1,0:T(8,128)(2,1)S(1)} %bitcast.12), channel_id=1, source_target_pairs={{0,4},{1,5},{2,6},{3,7},{4,0},{5,1},{6,2},{7,3},{8,12},{9,13},{10,... | collective-permute-start | bytes 221192 | tf_op jit(solution)/shard_map/ppermute | solution.py:222
  25.3 0.2 collective-permute-done.8.refs_0_
  25.5 0.6 collective-permute-start.3
  26.1 1.7 %collective-permute-done.9.refs_1_ = bf16[64,576]{1,0:T(8,128)(2,1)S(1)} collective-permute-done((bf16[64,576]{1,0:T(8,128)(2,1)S(1)}, bf16[64,576]{1,0:T(8,128)(2,1)S(1)}, u32[]{:S(2)}, u32[]{:S(2)}) %collective-permute-start.9) | collective-permute-done | bytes 73760 | tf_op jit(solution)/shard_map/ppermute | solution.py:222
  27.8 2.3 %copy-done = bf16[2,2048,576]{1,2,0:T(8,128)(2,1)S(1)} copy-done((bf16[2,2048,576]{1,2,0:T(8,128)(2,1)S(1)}, bf16[2,2048,576]{1,2,0:T(8,128)(2,1)}, u32[]{:S(2)}) %copy-start) | copy-done | bytes 4718616
  30.1 0.7 copy-done.4
  30.8 5.6 %attend.3 = (bf16[64,640]{1,0:T(8,128)(2,1)S(1)}, bf16[64,640]{1,0:T(8,128)(2,1)S(1)}, bf16[64,640]{1,0:T(8,128)(2,1)S(1)}, bf16[64,640]{1,0:T(8,128)(2,1)S(1)}) custom-call(s32[2]{0:T(128)S(1)} %copy-done.4, bf16[64,576]{1,0:T(8,128)(2,1)S(1)} %collective-permute-done.8.refs_0_, bf16[64,576]{1,0:T(8,128)(2,1)S(1)} %collective-permute-done.9.refs_1_, ...), custom_call_target="tpu_custom_call" | custom-call | flops 2281701376 | bytes 4718592 | tf_op jit(solution)/shard_map/attend/pallas_call | solution.py:91
  36.3 1.9 %collective-permute-start.12 = (bf16[64,640]{1,0:T(8,128)(2,1)S(1)}, bf16[64,640]{1,0:T(8,128)(2,1)S(1)}, u32[]{:S(2)}, u32[]{:S(2)}) collective-permute-start(bf16[64,640]{1,0:T(8,128)(2,1)S(1)} %get-tuple-element.19), channel_id=1, source_target_pairs={{0,8},{1,9},{2,10},{3,11},{4,12},{5,13},{6,14},{7,15},{8,0},{9,1},... | collective-permute-start | bytes 245768 | tf_op jit(solution)/shard_map/ppermute | solution.py:222
  38.2 1.0 %collective-permute-start.13 = (bf16[64,640]{1,0:T(8,128)(2,1)S(1)}, bf16[64,640]{1,0:T(8,128)(2,1)S(1)}, u32[]{:S(2)}, u32[]{:S(2)}) collective-permute-start(bf16[64,640]{1,0:T(8,128)(2,1)S(1)} %get-tuple-element.20), channel_id=1, source_target_pairs={{0,10},{1,11},{2,8},{3,9},{4,14},{5,15},{6,12},{7,13},{8,2},{9,3},... | collective-permute-start | bytes 245768 | tf_op jit(solution)/shard_map/ppermute | solution.py:222
  39.2 2.5 %collective-permute-start.14 = (bf16[64,640]{1,0:T(8,128)(2,1)S(1)}, bf16[64,640]{1,0:T(8,128)(2,1)S(1)}, u32[]{:S(2)}, u32[]{:S(2)}) collective-permute-start(bf16[64,640]{1,0:T(8,128)(2,1)S(1)} %get-tuple-element.21), channel_id=1, source_target_pairs={{0,12},{1,13},{2,14},{3,15},{4,8},{5,9},{6,10},{7,11},{8,4},{9,5},... | collective-permute-start | bytes 245768 | tf_op jit(solution)/shard_map/ppermute | solution.py:222
  41.7 2.3 %collective-permute-start.15 = (bf16[64,640]{1,0:T(8,128)(2,1)S(1)}, bf16[64,640]{1,0:T(8,128)(2,1)S(1)}, u32[]{:S(2)}, u32[]{:S(2)}) collective-permute-start(bf16[64,640]{1,0:T(8,128)(2,1)S(1)} %get-tuple-element.22), channel_id=1, source_target_pairs={{0,14},{1,15},{2,12},{3,13},{4,10},{5,11},{6,8},{7,9},{8,6},{9,7},... | collective-permute-start | bytes 245768 | tf_op jit(solution)/shard_map/ppermute | solution.py:222
  44.0 5.3 %attend.2 = (bf16[64,640]{1,0:T(8,128)(2,1)S(1)}, bf16[64,640]{1,0:T(8,128)(2,1)S(1)}, bf16[64,640]{1,0:T(8,128)(2,1)S(1)}, bf16[64,640]{1,0:T(8,128)(2,1)S(1)}) custom-call(s32[2]{0:T(128)S(1)} %copy-done.4, bf16[64,576]{1,0:T(8,128)(2,1)S(1)} %bitcast.14, bf16[64,576]{1,0:T(8,128)(2,1)S(1)} %collective-permute-done.1.refs_1_, ...), custom_call_target="tpu_custom_call" | custom-call | flops 2281701376 | bytes 4718592 | tf_op jit(solution)/shard_map/attend/pallas_call | solution.py:91
  49.3 0.5 collective-permute-start.5
  49.9 0.5 collective-permute-done.13.refs_5_
  50.4 2.5 %collective-permute-start.7 = (bf16[64,640]{1,0:T(8,128)(2,1)S(1)}, bf16[64,640]{1,0:T(8,128)(2,1)S(1)}, u32[]{:S(2)}, u32[]{:S(2)}) collective-permute-start(bf16[64,640]{1,0:T(8,128)(2,1)S(1)} %get-tuple-element.18), channel_id=1, source_target_pairs={{0,6},{1,7},{2,4},{3,5},{4,2},{5,3},{6,0},{7,1},{8,14},{9,15},{10,... | collective-permute-start | bytes 245768 | tf_op jit(solution)/shard_map/ppermute | solution.py:222
  52.9 1.3 %collective-permute-done.5.refs_1_ = bf16[64,640]{1,0:T(8,128)(2,1)S(1)} collective-permute-done((bf16[64,640]{1,0:T(8,128)(2,1)S(1)}, bf16[64,640]{1,0:T(8,128)(2,1)S(1)}, u32[]{:S(2)}, u32[]{:S(2)}) %collective-permute-start.5) | collective-permute-done | bytes 81952 | tf_op jit(solution)/shard_map/ppermute | solution.py:222
  54.3 1.9 %collective-permute-done.7.refs_3_ = bf16[64,640]{1,0:T(8,128)(2,1)S(1)} collective-permute-done((bf16[64,640]{1,0:T(8,128)(2,1)S(1)}, bf16[64,640]{1,0:T(8,128)(2,1)S(1)}, u32[]{:S(2)}, u32[]{:S(2)}) %collective-permute-start.7) | collective-permute-done | bytes 81952 | tf_op jit(solution)/shard_map/ppermute | solution.py:222
  56.2 0.4 merge.1
  56.7 1.2 %collective-permute-done.16.got_ref = bf16[32,512]{1,0:T(8,128)(2,1)S(1)} collective-permute-done((bf16[32,512]{1,0:T(8,128)(2,1)S(1)}, bf16[32,512]{1,0:T(8,128)(2,1)S(1)}, u32[]{:S(2)}, u32[]{:S(2)}) %collective-permute-start.16) | collective-permute-done | bytes 32800 | tf_op jit(solution)/shard_map/ppermute | solution.py:222
  57.9 1.2 %copy-done.3 = bf16[8,512,128]{2,1,0:T(8,128)(2,1)S(1)} copy-done((bf16[8,512,128]{2,1,0:T(8,128)(2,1)S(1)}, bf16[8,512,128]{2,1,0:T(8,128)(2,1)}, u32[]{:S(2)}) %copy-start.3) | copy-done | bytes 1048600
  59.1 5.1 %project.1 = bf16[16,8,448]{2,1,0:T(8,128)(2,1)S(1)} custom-call(bf16[32,512]{1,0:T(8,128)(2,1)S(1)} %get-tuple-element.23.own_ref, bf16[32,512]{1,0:T(8,128)(2,1)S(1)} %collective-permute-done.16.got_ref, bf16[8,512,128]{2,1,0:T(8,128)(2,1)S(1)} %copy-done.3, bf16[1024,7168]{1,0:T(8,128)(2,1)S(1)} %copy-done.2), custom_call_target="tpu_custom_call" | custom-call | tf_op jit(solution)/shard_map/project/pallas_call | solution.py:173
  64.2 12.1 %all_to_all.5.in_ref = bf16[16,8,448]{2,1,0:T(8,128)(2,1)S(1)} all-to-all(bf16[16,8,448]{2,1,0:T(8,128)(2,1)S(1)} %project.1), channel_id=1, replica_groups=mesh['grp'=2,'ctx'=16] {'ctx'}, dimensions={0} | all-to-all | bytes 229376 | tf_op jit(solution)/shard_map/all_to_all | solution.py:244
  76.3 1.2 %finish.1 = bf16[2,4,448]{2,1,0:T(4,128)(2,1)} custom-call(bf16[16,8,448]{2,1,0:T(8,128)(2,1)S(1)} %all_to_all.5.in_ref, s32[2,4]{1,0:T(2,128)S(1)} %copy-done.5), custom_call_target="tpu_custom_call" | custom-call | tf_op jit(solution)/shard_map/finish/pallas_call | solution.py:203
  (21 shorter events, 0.3 us)
Async XLA Ops:
  0.0 27.8 %collective-permute-start.4 = (bf16[2,576,2048]{2,1,0:T(8,128)(2,1)}, bf16[2,576,2048]{2,1,0:T(8,128)(2,1)}, u32[]{:S(2)}, u32[]{:S(2)}) collective-permute-start(bf16[2,576,2048]{2,1,0:T(8,128)(2,1)} %bitcast.4), channel_id=1, source_target_pairs={{0,1},{1,0},{2,3},{3,2},{4,5},{5,4},{6,7},{7,6},{8,9},{9,8},{10,11... | collective-permute-start | bytes 14155784 | tf_op jit(solution)/shard_map/ppermute | solution.py:222
  0.5 5.7 %collective-permute-start = (bf16[2,4,8,576]{3,2,1,0:T(8,128)(2,1)}, bf16[2,4,8,576]{3,2,1,0:T(8,128)(2,1)S(1)}, u32[]{:S(2)}, u32[]{:S(2)}) collective-permute-start(bf16[2,4,8,576]{3,2,1,0:T(8,128)(2,1)} %param.6), channel_id=1, source_target_pairs={{0,1},{1,0},{2,3},{3,2},{4,5},{5,4},{6,7},{7,6},{8,9},{9,8},{10,11... | collective-permute-start | bytes 221192 | tf_op jit(solution)/shard_map/ppermute | solution.py:222
  6.9 9.2 %collective-permute-start.10 = (bf16[64,576]{1,0:T(8,128)(2,1)S(1)}, bf16[64,576]{1,0:T(8,128)(2,1)S(1)}, u32[]{:S(2)}, u32[]{:S(2)}) collective-permute-start(bf16[64,576]{1,0:T(8,128)(2,1)S(1)} %bitcast.7), channel_id=1, source_target_pairs={{0,12},{1,13},{2,14},{3,15},{4,8},{5,9},{6,10},{7,11},{8,4},{9,5},... | collective-permute-start | bytes 221192 | tf_op jit(solution)/shard_map/ppermute | solution.py:222
  12.2 8.1 %collective-permute-start.11 = (bf16[64,576]{1,0:T(8,128)(2,1)S(1)}, bf16[64,576]{1,0:T(8,128)(2,1)S(1)}, u32[]{:S(2)}, u32[]{:S(2)}) collective-permute-start(bf16[64,576]{1,0:T(8,128)(2,1)S(1)} %bitcast.8), channel_id=1, source_target_pairs={{0,14},{1,15},{2,12},{3,13},{4,10},{5,11},{6,8},{7,9},{8,6},{9,7},... | collective-permute-start | bytes 221192 | tf_op jit(solution)/shard_map/ppermute | solution.py:222
  13.4 12.1 %collective-permute-start.8 = (bf16[64,576]{1,0:T(8,128)(2,1)S(1)}, bf16[64,576]{1,0:T(8,128)(2,1)S(1)}, u32[]{:S(2)}, u32[]{:S(2)}) collective-permute-start(bf16[64,576]{1,0:T(8,128)(2,1)S(1)} %bitcast.9), channel_id=1, source_target_pairs={{0,8},{1,9},{2,10},{3,11},{4,12},{5,13},{6,14},{7,15},{8,0},{9,1},... | collective-permute-start | bytes 221192 | tf_op jit(solution)/shard_map/ppermute | solution.py:222
  14.2 13.5 %collective-permute-start.9 = (bf16[64,576]{1,0:T(8,128)(2,1)S(1)}, bf16[64,576]{1,0:T(8,128)(2,1)S(1)}, u32[]{:S(2)}, u32[]{:S(2)}) collective-permute-start(bf16[64,576]{1,0:T(8,128)(2,1)S(1)} %bitcast.10), channel_id=1, source_target_pairs={{0,10},{1,11},{2,8},{3,9},{4,14},{5,15},{6,12},{7,13},{8,2},{9,3},... | collective-permute-start | bytes 221192 | tf_op jit(solution)/shard_map/ppermute | solution.py:222
  16.1 23.1 %collective-permute-start.1 = (bf16[64,576]{1,0:T(8,128)(2,1)S(1)}, bf16[64,576]{1,0:T(8,128)(2,1)S(1)}, u32[]{:S(2)}, u32[]{:S(2)}) collective-permute-start(bf16[64,576]{1,0:T(8,128)(2,1)S(1)} %bitcast.11), channel_id=1, source_target_pairs={{0,2},{1,3},{2,0},{3,1},{4,6},{5,7},{6,4},{7,5},{8,10},{9,11},{10,... | collective-permute-start | bytes 221192 | tf_op jit(solution)/shard_map/ppermute | solution.py:222
  20.3 21.4 %collective-permute-start.2 = (bf16[64,576]{1,0:T(8,128)(2,1)S(1)}, bf16[64,576]{1,0:T(8,128)(2,1)S(1)}, u32[]{:S(2)}, u32[]{:S(2)}) collective-permute-start(bf16[64,576]{1,0:T(8,128)(2,1)S(1)} %bitcast.12), channel_id=1, source_target_pairs={{0,4},{1,5},{2,6},{3,7},{4,0},{5,1},{6,2},{7,3},{8,12},{9,13},{10,... | collective-permute-start | bytes 221192 | tf_op jit(solution)/shard_map/ppermute | solution.py:222
  25.5 18.6 %collective-permute-start.3 = (bf16[64,576]{1,0:T(8,128)(2,1)S(1)}, bf16[64,576]{1,0:T(8,128)(2,1)S(1)}, u32[]{:S(2)}, u32[]{:S(2)}) collective-permute-start(bf16[64,576]{1,0:T(8,128)(2,1)S(1)} %bitcast.13), channel_id=1, source_target_pairs={{0,6},{1,7},{2,4},{3,5},{4,2},{5,3},{6,0},{7,1},{8,14},{9,15},{10,... | collective-permute-start | bytes 221192 | tf_op jit(solution)/shard_map/ppermute | solution.py:222
  27.8 2.3 %copy-start = (bf16[2,2048,576]{1,2,0:T(8,128)(2,1)S(1)}, bf16[2,2048,576]{1,2,0:T(8,128)(2,1)}, u32[]{:S(2)}) copy-start(bf16[2,2048,576]{1,2,0:T(8,128)(2,1)} %param.7) | copy-start | bytes 14155780
  30.1 0.7 copy-start.4
  30.8 13.3 %copy-start.1 = (bf16[2,2048,576]{1,2,0:T(8,128)(2,1)S(1)}, bf16[2,2048,576]{1,2,0:T(8,128)(2,1)}, u32[]{:S(2)}) copy-start(bf16[2,2048,576]{1,2,0:T(8,128)(2,1)} %param.7) | copy-start | bytes 14155780
  30.8 27.1 %copy-start.2 = (bf16[1024,7168]{1,0:T(8,128)(2,1)S(1)}, bf16[1024,7168]{1,0:T(8,128)(2,1)}, u32[]{:S(2)}) copy-start(bf16[1024,7168]{1,0:T(8,128)(2,1)} %weight_ref.1) | copy-start | bytes 44040196
  36.3 13.5 %collective-permute-start.12 = (bf16[64,640]{1,0:T(8,128)(2,1)S(1)}, bf16[64,640]{1,0:T(8,128)(2,1)S(1)}, u32[]{:S(2)}, u32[]{:S(2)}) collective-permute-start(bf16[64,640]{1,0:T(8,128)(2,1)S(1)} %get-tuple-element.19), channel_id=1, source_target_pairs={{0,8},{1,9},{2,10},{3,11},{4,12},{5,13},{6,14},{7,15},{8,0},{9,1},... | collective-permute-start | bytes 245768 | tf_op jit(solution)/shard_map/ppermute | solution.py:222
  38.2 12.2 %collective-permute-start.13 = (bf16[64,640]{1,0:T(8,128)(2,1)S(1)}, bf16[64,640]{1,0:T(8,128)(2,1)S(1)}, u32[]{:S(2)}, u32[]{:S(2)}) collective-permute-start(bf16[64,640]{1,0:T(8,128)(2,1)S(1)} %get-tuple-element.20), channel_id=1, source_target_pairs={{0,10},{1,11},{2,8},{3,9},{4,14},{5,15},{6,12},{7,13},{8,2},{9,3},... | collective-permute-start | bytes 245768 | tf_op jit(solution)/shard_map/ppermute | solution.py:222
  39.2 13.7 %collective-permute-start.14 = (bf16[64,640]{1,0:T(8,128)(2,1)S(1)}, bf16[64,640]{1,0:T(8,128)(2,1)S(1)}, u32[]{:S(2)}, u32[]{:S(2)}) collective-permute-start(bf16[64,640]{1,0:T(8,128)(2,1)S(1)} %get-tuple-element.21), channel_id=1, source_target_pairs={{0,12},{1,13},{2,14},{3,15},{4,8},{5,9},{6,10},{7,11},{8,4},{9,5},... | collective-permute-start | bytes 245768 | tf_op jit(solution)/shard_map/ppermute | solution.py:222
  41.7 11.2 %collective-permute-start.15 = (bf16[64,640]{1,0:T(8,128)(2,1)S(1)}, bf16[64,640]{1,0:T(8,128)(2,1)S(1)}, u32[]{:S(2)}, u32[]{:S(2)}) collective-permute-start(bf16[64,640]{1,0:T(8,128)(2,1)S(1)} %get-tuple-element.22), channel_id=1, source_target_pairs={{0,14},{1,15},{2,12},{3,13},{4,10},{5,11},{6,8},{7,9},{8,6},{9,7},... | collective-permute-start | bytes 245768 | tf_op jit(solution)/shard_map/ppermute | solution.py:222
  49.3 4.9 %collective-permute-start.5 = (bf16[64,640]{1,0:T(8,128)(2,1)S(1)}, bf16[64,640]{1,0:T(8,128)(2,1)S(1)}, u32[]{:S(2)}, u32[]{:S(2)}) collective-permute-start(bf16[64,640]{1,0:T(8,128)(2,1)S(1)} %get-tuple-element.16), channel_id=1, source_target_pairs={{0,2},{1,3},{2,0},{3,1},{4,6},{5,7},{6,4},{7,5},{8,10},{9,11},{10,... | collective-permute-start | bytes 245768 | tf_op jit(solution)/shard_map/ppermute | solution.py:222
  49.9 4.4 %collective-permute-start.6 = (bf16[64,640]{1,0:T(8,128)(2,1)S(1)}, bf16[64,640]{1,0:T(8,128)(2,1)S(1)}, u32[]{:S(2)}, u32[]{:S(2)}) collective-permute-start(bf16[64,640]{1,0:T(8,128)(2,1)S(1)} %get-tuple-element.17), channel_id=1, source_target_pairs={{0,4},{1,5},{2,6},{3,7},{4,0},{5,1},{6,2},{7,3},{8,12},{9,13},{10,... | collective-permute-start | bytes 245768 | tf_op jit(solution)/shard_map/ppermute | solution.py:222
  50.4 5.8 %collective-permute-start.7 = (bf16[64,640]{1,0:T(8,128)(2,1)S(1)}, bf16[64,640]{1,0:T(8,128)(2,1)S(1)}, u32[]{:S(2)}, u32[]{:S(2)}) collective-permute-start(bf16[64,640]{1,0:T(8,128)(2,1)S(1)} %get-tuple-element.18), channel_id=1, source_target_pairs={{0,6},{1,7},{2,4},{3,5},{4,2},{5,3},{6,0},{7,1},{8,14},{9,15},{10,... | collective-permute-start | bytes 245768 | tf_op jit(solution)/shard_map/ppermute | solution.py:222
  56.6 1.3 %collective-permute-start.16 = (bf16[32,512]{1,0:T(8,128)(2,1)S(1)}, bf16[32,512]{1,0:T(8,128)(2,1)S(1)}, u32[]{:S(2)}, u32[]{:S(2)}) collective-permute-start(bf16[32,512]{1,0:T(8,128)(2,1)S(1)} %get-tuple-element.24), channel_id=1, source_target_pairs={{0,1},{1,0},{2,3},{3,2},{4,5},{5,4},{6,7},{7,6},{8,9},{9,8},{10,11... | collective-permute-start | bytes 98312 | tf_op jit(solution)/shard_map/ppermute | solution.py:222
  57.9 1.2 %copy-start.3 = (bf16[8,512,128]{2,1,0:T(8,128)(2,1)S(1)}, bf16[8,512,128]{2,1,0:T(8,128)(2,1)}, u32[]{:S(2)}) copy-start(bf16[8,512,128]{2,1,0:T(8,128)(2,1)} %up_ref.1) | copy-start | bytes 3145732
  59.1 17.2 %copy-start.5 = (s32[2,4]{1,0:T(2,128)S(1)}, s32[2,4]{1,0:T(2,128)}, u32[]{:S(2)}) copy-start(s32[2,4]{1,0:T(2,128)} %mask_ref.1) | copy-start | bytes 100

commit v2 on v0

v2 whole, which is shorter than its diff:
```python
import functools
import math

import jax
import jax.numpy as jnp
from jax import lax
from jax.experimental import pallas as pl
from jax.experimental.pallas import tpu as pltpu
from jax.sharding import PartitionSpec as P

SOFTMAX_SCALE = 192.0 ** (-0.5)
LOG2_SCALE = SOFTMAX_SCALE * math.log2(math.e)
SCORE_FLOOR = -1e30
STAT_LANES = 128
MIB = 1024 * 1024


def split_low(x):
    high = x.astype(jnp.bfloat16).astype(jnp.float32)
    return high, (x - high).astype(jnp.bfloat16).astype(jnp.float32)


def attend_kernel(chunks, spec, heads, latent, lengths_ref, *refs):
    q_refs, key_refs, out_refs = refs[:chunks], refs[chunks : chunks + 2], refs[chunks + 2 :]
    block = key_refs[0].shape[1]
    width = min(block, 512)
    per_block = block // width
    steps = 2 * per_block
    me = lax.axis_index("ctx")
    bases = (me * block, (me + 1 - 2 * lax.rem(me, 2)) * block)
    queries = jnp.concatenate([ref[...] for ref in q_refs], axis=0)
    rows = queries.shape[0]
    row = lax.broadcasted_iota(jnp.int32, (rows, 1), 0)
    draft = lax.rem(lax.div(row, heads), spec)
    horizon = lengths_ref[pl.ds(lax.rem(me, 2), 1), :1] - spec + 1 + draft

    def keys(step, features):
        start = (step % per_block) * width
        return key_refs[step // per_block][:features, start : start + width]

    def score(step):
        tile = jnp.dot(queries, keys(step, None), preferred_element_type=jnp.float32)
        start = bases[step // per_block] + (step % per_block) * width
        position = start + lax.broadcasted_iota(jnp.int32, (1, width), 1)
        return jnp.where(position < horizon, tile * LOG2_SCALE, SCORE_FLOOR)

    peak = jnp.full((rows, 1), 0.1 * SCORE_FLOOR, jnp.float32)
    denominator = jnp.zeros((rows, 1), jnp.float32)
    numerator = jnp.zeros((rows, latent), jnp.float32)
    tile = score(0)
    for step in range(steps):
        following = score(step + 1) if step + 1 < steps else None
        higher = jnp.maximum(peak, jnp.max(tile, axis=1, keepdims=True))
        if step == steps - 1:
            higher = sum(split_low(higher))
        weights = jnp.exp2(tile - higher)
        ratio = jnp.exp2(peak - higher)
        denominator = denominator * ratio + jnp.sum(weights, axis=1, keepdims=True)
        numerator = numerator * ratio + lax.dot_general(
            weights.astype(jnp.bfloat16),
            keys(step, latent),
            (((1,), (1,)), ((), ())),
            preferred_element_type=jnp.float32,
        )
        peak, tile = higher, following
    chunk = rows // chunks
    for i, out_ref in enumerate(out_refs):
        part = slice(i * chunk, (i + 1) * chunk)
        store_part(out_ref, latent, peak[part], denominator[part], numerator[part])


def attend(lengths, query_chunks, keys, spec, heads, latent):
    chunks = len(query_chunks)
    chunk, feature = query_chunks[0].shape
    rows, positions = chunks * chunk, 2 * keys[0].shape[1]
    return pl.pallas_call(
        functools.partial(attend_kernel, chunks, spec, heads, latent),
        out_shape=[jax.ShapeDtypeStruct((chunk, latent + STAT_LANES), jnp.bfloat16)] * chunks,
        compiler_params=pltpu.CompilerParams(vmem_limit_bytes=12 * MIB),
        cost_estimate=pl.CostEstimate(
            flops=2 * rows * positions * (feature + latent),
            bytes_accessed=2 * positions * feature,
            transcendentals=rows * positions,
        ),
        name="attend",
    )(lengths, *query_chunks, *keys)


def merged(in_refs, latent):
    peaks, denominators = [], []
    for ref in in_refs:
        stats = ref[:, latent:].astype(jnp.float32)
        peaks.append(stats[:, 0:1] + stats[:, 1:2])
        denominators.append(stats[:, 2:3] + stats[:, 3:4])
    largest = functools.reduce(jnp.maximum, peaks)
    upper, lower = 0.0, 0.0
    for ref, peak, denominator in zip(in_refs, peaks, denominators):
        factor = jnp.exp2(peak - largest)
        upper += factor * ref[:, :latent].astype(jnp.float32)
        lower += factor * denominator
    return largest, lower, upper


def store_part(ref, latent, peak, denominator, numerator):
    peak_high, peak_low = split_low(peak)
    denom_high, denom_low = split_low(denominator)
    lane = lax.broadcasted_iota(jnp.int32, (ref.shape[0], STAT_LANES), 1)
    stats = jnp.where(lane == 0, peak_high, jnp.where(lane == 1, peak_low, 0.0))
    stats = jnp.where(lane == 2, denom_high, jnp.where(lane == 3, denom_low, stats))
    ref[:, :latent] = numerator.astype(jnp.bfloat16)
    ref[:, latent:] = stats.astype(jnp.bfloat16)


def combine_kernel(parts, latent, *refs):
    store_part(refs[parts], latent, *merged(refs[:parts], latent))


def combine(parts, latent):
    return pl.pallas_call(
        functools.partial(combine_kernel, len(parts), latent),
        out_shape=jax.ShapeDtypeStruct(parts[0].shape, jnp.bfloat16),
        compiler_params=pltpu.CompilerParams(vmem_limit_bytes=8 * MIB),
        name="combine",
    )(*parts)


def merge_kernel(parts, latent, *refs):
    _, lower, upper = merged(refs[:parts], latent)
    own_ref, give_ref = refs[parts:]
    attended = (upper / lower).astype(jnp.bfloat16)
    half = attended.shape[0] // 2
    own_ref[...] = attended[:half]
    give_ref[...] = attended[half:]


def merge(parts, latent):
    rows = parts[0].shape[0]
    return pl.pallas_call(
        functools.partial(merge_kernel, len(parts), latent),
        out_shape=[jax.ShapeDtypeStruct((rows // 2, latent), jnp.bfloat16)] * 2,
        compiler_params=pltpu.CompilerParams(vmem_limit_bytes=8 * MIB),
        name="merge",
    )(*parts)


def project_kernel(heads, group, own_ref, got_ref, up_ref, weight_ref, out_ref):
    core = lax.rem(lax.axis_index("ctx"), 2)
    own, got = own_ref[...], got_ref[...]
    first = jnp.where(core == 0, own, got)
    second = jnp.where(core == 0, got, own)
    attended = jnp.concatenate([first, second], axis=0)
    rows = attended.shape[0]
    head = lax.rem(lax.broadcasted_iota(jnp.int32, (rows, 1), 0), heads)
    values = []
    for h in range(heads):
        tile = jnp.dot(attended, up_ref[h], preferred_element_type=jnp.float32)
        tile = jnp.where(head == h, tile, 0.0)
        tile = jnp.sum(tile.reshape(rows // heads, heads, tile.shape[1]), axis=1)
        values.append(tile.astype(jnp.bfloat16))
    values = jnp.concatenate(values, axis=1)
    owners, _, columns = out_ref.shape
    for i in range(0, owners, group):
        part = weight_ref[:, i * columns : (i + group) * columns]
        tile = jnp.dot(values, part, preferred_element_type=jnp.float32)
        for j in range(group):
            piece = tile[:, j * columns : (j + 1) * columns]
            out_ref[i + j] = piece.astype(out_ref.dtype)


def project(own, got, value_up, weight, spec, owners):
    heads = own.shape[0] // spec
    columns = weight.shape[1] // owners
    group = next(g for g in (2, 1, 4, 8, 16, owners) if (g * columns) % 128 == 0)
    return pl.pallas_call(
        functools.partial(project_kernel, heads, group),
        out_shape=jax.ShapeDtypeStruct((owners, 2 * spec, columns), jnp.bfloat16),
        in_specs=[pl.BlockSpec(memory_space=pltpu.VMEM)] * 4,
        out_specs=pl.BlockSpec(memory_space=pltpu.VMEM),
        compiler_params=pltpu.CompilerParams(vmem_limit_bytes=12 * MIB),
        name="project",
    )(own, got, value_up, weight)


def finish_kernel(in_ref, keep_ref, out_ref):
    total = jnp.sum(in_ref[...].astype(jnp.float32), axis=0) * keep_ref[:, :1]
    spec = out_ref.shape[1]
    for r in range(out_ref.shape[0]):
        out_ref[r] = total[r * spec : (r + 1) * spec].astype(out_ref.dtype)


def finish(parts, keep, requests):
    _, rows, columns = parts.shape
    return pl.pallas_call(
        finish_kernel,
        out_shape=jax.ShapeDtypeStruct((requests, rows // requests, columns), jnp.bfloat16),
        compiler_params=pltpu.CompilerParams(vmem_limit_bytes=8 * MIB),
        name="finish",
    )(parts, keep)


def on_device(n, queries, latent_cache, lengths, draft_mask, value_up, output_weight):
    requests, spec, heads, feature = queries.shape
    latent = value_up.shape[1]
    core = lax.rem(lax.axis_index("ctx"), 2)

    def swap(x, bits):
        return lax.ppermute(x, "ctx", [(i, i ^ bits) for i in range(n)])

    chunk = requests * spec * heads
    got = swap(queries, 1)
    both = jnp.stack([queries, got], axis=1)
    mine = lax.dynamic_index_in_dim(both, core, 0, keepdims=False).reshape(chunk, feature)
    own_keys = jnp.swapaxes(latent_cache, 1, 2)
    own_keys = lax.optimization_barrier((own_keys, got))[0]
    got_keys = swap(own_keys, 1)

    far_bit = n // 2
    near = [2 * k for k in range(1, n // 4)]
    far = swap(mine, far_bit)
    near_queries = [swap(mine, bits) for bits in near]

    own_keys, draft_mask = lax.optimization_barrier((own_keys, draft_mask, mine))[:2]
    keys = [lax.dynamic_index_in_dim(k, core, 0, keepdims=False) for k in (own_keys, got_keys)]
    far, keys, near_queries = lax.optimization_barrier((far, keys, near_queries))
    far_queries = [swap(far, bits) for bits in near]
    spread = jnp.broadcast_to(lengths[:, None], (requests, STAT_LANES))
    keep = draft_mask.astype(jnp.float32).reshape(requests * spec, 1)
    keep = jnp.broadcast_to(keep, (requests * spec, STAT_LANES))
    near_parts = attend(spread, [mine, *near_queries], keys, spec, heads, latent)
    near_parts, far_queries = lax.optimization_barrier((near_parts, far_queries))
    far_parts = attend(spread, [far, *far_queries], keys, spec, heads, latent)
    near_parts, far_parts = lax.optimization_barrier((near_parts, far_parts))
    far_part = combine(
        [far_parts[0]] + [swap(part, bits) for part, bits in zip(far_parts[1:], near)], latent
    )
    parts = [swap(far_part, far_bit), near_parts[0]]
    parts += [swap(part, bits) for part, bits in zip(near_parts[1:], near)]
    own, give = merge(parts, latent)
    outs = project(own, swap(give, 1), value_up, output_weight, spec, n)
    received = lax.all_to_all(outs, "ctx", 0, 0, tiled=True)
    return finish(received, keep, requests)


def solution(mesh):
    return jax.shard_map(
        functools.partial(on_device, mesh.shape["ctx"]),
        mesh=mesh,
        in_specs=(
            P("grp", None, "ctx", None),
            P("grp", "ctx", None),
            P("grp"),
            P("grp", None),
            P("ctx", None, None),
            P("ctx", None),
        ),
        out_specs=P("grp", None, "ctx"),
        check_vma=False,
    )
```

time: 241 us -> 58.6 us (0.24)
  waiting for transfers between devices: 166 us -> 15.8 us
  matrix products: 19.5 us -> 0 us
  local copies, waits for them, and re-layouts: 21.1 us -> 3.89 us
  between operations: 13.5 us -> 0.15 us
  starting transfers between devices: 13.4 us -> 26.7 us
  Pallas kernels: 0 us -> 10.9 us
  other arithmetic: 6.25 us -> 0.8 us
    unnamed x3 -> x0, waiting for transfers between devices: 76 us -> none
    all_gather x1 -> x0, waiting for transfers between devices: 43.1 us -> none  [on_device(): gathered = lax.all_gather(queries, 'ctx', axis=2, tiled=True)]
    all_to_all x3 -> x1, waiting for transfers between devices: 47.4 us -> 7.83 us  [on_device(): received = lax.all_to_all(outs, 'ctx', 0, 0, tiled=True)]
    ppermute x0 -> x17, starting transfers between devices: none -> 20.9 us  [swap(): return lax.ppermute(x, 'ctx', [(i, i ^ bits) for i in range(n)])]
    dot_general x4 -> x0, matrix products: 19.5 us -> none  [the longest x1 7.27 us: on_device(): jnp.dot(values, output_weight, preferred_element_type=jnp.float32)]
    unnamed x8, local copies, waits for them, and re-layouts: 16.2 us -> 0.02 us
    pallas_call x0 -> x6, Pallas kernels: none -> 10.9 us  [the longest x2 6.76 us: attend(): pl.pallas_call(functools.partial(attend_kernel, chunks, spec, heads, late...]
    ppermute x0 -> x17, waiting for transfers between devices: none -> 8.01 us  [swap(): return lax.ppermute(x, 'ctx', [(i, i ^ bits) for i in range(n)])]
  transfers between devices with their start and end apart: 5 -> 18, of which waited for: 4 -> 9; matrix products, arithmetic and copies ran while one was open for 4% -> 8% of each run, Pallas kernels for 0% -> 6%
where the time goes in v2:
time: 58.6 us; the launch traced here: 58.3 us
  starting transfers between devices  26.7 us (46%)
  waiting for transfers between devices  15.8 us (27%)
  Pallas kernels  10.9 us (19%)
  local copies, waits for them, and re-layouts  3.89 us (7%)
  other arithmetic  0.8 us (1%)
    ppermute x17, starting transfers between devices, swap(): return lax.ppermute(x, 'ctx', [(i, i ^ bits) for i in range(n)])  20.9 us
    ppermute x17, waiting for transfers between devices, swap(): return lax.ppermute(x, 'ctx', [(i, i ^ bits) for i in range(n)])  8.01 us
    all_to_all x1, waiting for transfers between devices, on_device(): received = lax.all_to_all(outs, 'ctx', 0, 0, tiled=True)  7.83 us
    pallas_call x2, Pallas kernels, attend(): pl.pallas_call(functools.partial(attend_kernel, chunks, spec, heads, late...  6.76 us
    all_to_all x1, starting transfers between devices, on_device(): received = lax.all_to_all(outs, 'ctx', 0, 0, tiled=True)  5.75 us
    squeeze x2, local copies, waits for them, and re-layouts, on_device(): lax.dynamic_index_in_dim(k, core, 0, keepdims=False)  3.65 us
    pallas_call x1, Pallas kernels, project(): pl.pallas_call(functools.partial(project_kernel, heads, group), out_shape...  2.92 us
  transfers between devices with their start and end apart: 18, of which 9 were waited for; matrix products, arithmetic and copies ran while one was open for 8% of the time, Pallas kernels for 6%

profile of v2, /device:TPU:0, one launch (start us, length us, event | category | flops | bytes accessed | tf_op | source)
XLA Modules:
  0.0 58.3 jit_solution(13052544700909722433)
XLA Ops:
  0.0 0.5 collective-permute-start
  0.5 1.1 %collective-permute-done = bf16[2,4,8,576]{3,2,1,0:T(8,128)(2,1)S(1)} collective-permute-done((bf16[2,4,8,576]{3,2,1,0:T(8,128)(2,1)}, bf16[2,4,8,576]{3,2,1,0:T(8,128)(2,1)S(1)}, u32[]{:S(2)}, u32[]{:S(2)}) %collective-permute-start) | collective-permute-done | bytes 73760 | tf_op jit(solution)/shard_map/ppermute | solution.py:207
  1.6 0.4 collective-permute-start.2
  1.9 0.8 %fusion = bf16[1,2,4,8,576]{4,3,2,0,1:T(8,128)(2,1)S(1)} fusion(s32[]{:T(128)S(6)} %select_n.7, bf16[2,1,4,8,576]{4,3,2,0,1:T(8,128)(2,1)} %bitcast.15, bf16[2,1,4,8,576]{4,3,2,0,1:T(8,128)(2,1)S(1)} %bitcast.16), kind=kLoop, calls=%fused_computation.4 | loop fusion | flops 36864 | bytes 221188 | tf_op jit(solution)/shard_map/stack | solution.py:211
  2.8 3.8 %collective-permute-start.1 = (bf16[64,576]{1,0:T(8,128)(2,1)S(1)}, bf16[64,576]{1,0:T(8,128)(2,1)S(1)}, u32[]{:S(2)}, u32[]{:S(2)}) collective-permute-start(bf16[64,576]{1,0:T(8,128)(2,1)S(1)} %bitcast.8), channel_id=1, source_target_pairs={{0,8},{1,9},{2,10},{3,11},{4,12},{5,13},{6,14},{7,15},{8,0},{9,1},... | collective-permute-start | bytes 221192 | tf_op jit(solution)/shard_map/ppermute | solution.py:207
  6.6 1.5 %collective-permute-start.3 = (bf16[64,576]{1,0:T(8,128)(2,1)S(1)}, bf16[64,576]{1,0:T(8,128)(2,1)S(1)}, u32[]{:S(2)}, u32[]{:S(2)}) collective-permute-start(bf16[64,576]{1,0:T(8,128)(2,1)S(1)} %bitcast.9), channel_id=1, source_target_pairs={{0,2},{1,3},{2,0},{3,1},{4,6},{5,7},{6,4},{7,5},{8,10},{9,11},{10,... | collective-permute-start | bytes 221192 | tf_op jit(solution)/shard_map/ppermute | solution.py:207
  8.1 1.6 %collective-permute-start.4 = (bf16[64,576]{1,0:T(8,128)(2,1)S(1)}, bf16[64,576]{1,0:T(8,128)(2,1)S(1)}, u32[]{:S(2)}, u32[]{:S(2)}) collective-permute-start(bf16[64,576]{1,0:T(8,128)(2,1)S(1)} %bitcast.10), channel_id=1, source_target_pairs={{0,4},{1,5},{2,6},{3,7},{4,0},{5,1},{6,2},{7,3},{8,12},{9,13},{10,... | collective-permute-start | bytes 221192 | tf_op jit(solution)/shard_map/ppermute | solution.py:207
  9.7 0.4 collective-permute-start.5
  10.0 1.8 %dynamic-slice_bitcast_fusion.1.refs_4_ = bf16[576,2048]{1,0:T(8,128)(2,1)S(1)} fusion(bf16[2,576,2048]{2,1,0:T(8,128)(2,1)} %bitcast.14, s32[]{:T(128)S(6)} %select_n.7), kind=kLoop, calls=%fused_computation.1 | loop fusion | bytes 4718596 | tf_op jit(solution)/shard_map/jit(dynamic_index_in_dim)/squeeze | solution.py:223
  11.9 1.8 %dynamic-slice_bitcast_fusion.refs_5_ = bf16[576,2048]{1,0:T(8,128)(2,1)S(1)} fusion(bf16[2,576,2048]{2,1,0:T(8,128)(2,1)} %collective-permute-done.2, s32[]{:T(128)S(6)} %select_n.7), kind=kLoop, calls=%fused_computation | loop fusion | bytes 4718596 | tf_op jit(solution)/shard_map/jit(dynamic_index_in_dim)/squeeze | solution.py:223
  13.7 1.2 %collective-permute-done.5.refs_3_ = bf16[64,576]{1,0:T(8,128)(2,1)S(1)} collective-permute-done((bf16[64,576]{1,0:T(8,128)(2,1)S(1)}, bf16[64,576]{1,0:T(8,128)(2,1)S(1)}, u32[]{:S(2)}, u32[]{:S(2)}) %collective-permute-start.5) | collective-permute-done | bytes 73760 | tf_op jit(solution)/shard_map/ppermute | solution.py:207
  15.0 1.0 %collective-permute-start.6 = (bf16[64,576]{1,0:T(8,128)(2,1)S(1)}, bf16[64,576]{1,0:T(8,128)(2,1)S(1)}, u32[]{:S(2)}, u32[]{:S(2)}) collective-permute-start(bf16[64,576]{1,0:T(8,128)(2,1)S(1)} %collective-permute-done.1.refs_0_), channel_id=1, source_target_pairs={{0,2},{1,3},{2,0},{3,1},{4,6},{5,7},{6,4},{7,5},{8,10},{9,11},{10,... | collective-permute-start | bytes 221192 | tf_op jit(solution)/shard_map/ppermute | solution.py:207
  16.0 1.0 %collective-permute-start.7 = (bf16[64,576]{1,0:T(8,128)(2,1)S(1)}, bf16[64,576]{1,0:T(8,128)(2,1)S(1)}, u32[]{:S(2)}, u32[]{:S(2)}) collective-permute-start(bf16[64,576]{1,0:T(8,128)(2,1)S(1)} %collective-permute-done.1.refs_0_), channel_id=1, source_target_pairs={{0,4},{1,5},{2,6},{3,7},{4,0},{5,1},{6,2},{7,3},{8,12},{9,13},{10,... | collective-permute-start | bytes 221192 | tf_op jit(solution)/shard_map/ppermute | solution.py:207
  17.0 1.5 %collective-permute-start.8 = (bf16[64,576]{1,0:T(8,128)(2,1)S(1)}, bf16[64,576]{1,0:T(8,128)(2,1)S(1)}, u32[]{:S(2)}, u32[]{:S(2)}) collective-permute-start(bf16[64,576]{1,0:T(8,128)(2,1)S(1)} %collective-permute-done.1.refs_0_), channel_id=1, source_target_pairs={{0,6},{1,7},{2,4},{3,5},{4,2},{5,3},{6,0},{7,1},{8,14},{9,15},{10,... | collective-permute-start | bytes 221192 | tf_op jit(solution)/shard_map/ppermute | solution.py:207
  18.6 3.4 %attend.2 = (bf16[64,640]{1,0:T(8,128)(2,1)S(1)}, bf16[64,640]{1,0:T(8,128)(2,1)S(1)}, bf16[64,640]{1,0:T(8,128)(2,1)S(1)}, bf16[64,640]{1,0:T(8,128)(2,1)S(1)}) custom-call(s32[2,128]{1,0:T(2,128)S(1)} %broadcast_in_dim.6.lengths_ref, bf16[64,576]{1,0:T(8,128)(2,1)S(1)} %bitcast.12, bf16[64,576]{1,0:T(8,128)(2,1)S(1)} %collective-permute-done.3.refs_1_, ...), custom_call_target="tpu_custom_call" | custom-call | flops 2281701376 | bytes 4718592 | tf_op jit(solution)/shard_map/attend/pallas_call | solution.py:76
  22.0 0.4 collective-permute-done.8.refs_3_
  22.4 3.4 %attend.3 = (bf16[64,640]{1,0:T(8,128)(2,1)S(1)}, bf16[64,640]{1,0:T(8,128)(2,1)S(1)}, bf16[64,640]{1,0:T(8,128)(2,1)S(1)}, bf16[64,640]{1,0:T(8,128)(2,1)S(1)}) custom-call(s32[2,128]{1,0:T(2,128)S(1)} %broadcast_in_dim.6.lengths_ref, bf16[64,576]{1,0:T(8,128)(2,1)S(1)} %collective-permute-done.1.refs_0_, ...), custom_call_target="tpu_custom_call" | custom-call | flops 2281701376 | bytes 4718592 | tf_op jit(solution)/shard_map/attend/pallas_call | solution.py:76
  25.7 0.8 %collective-permute-start.9 = (bf16[64,640]{1,0:T(8,128)(2,1)S(1)}, bf16[64,640]{1,0:T(8,128)(2,1)S(1)}, u32[]{:S(2)}, u32[]{:S(2)}) collective-permute-start(bf16[64,640]{1,0:T(8,128)(2,1)S(1)} %get-tuple-element.63), channel_id=1, source_target_pairs={{0,2},{1,3},{2,0},{3,1},{4,6},{5,7},{6,4},{7,5},{8,10},{9,11},{10,... | collective-permute-start | bytes 245768 | tf_op jit(solution)/shard_map/ppermute | solution.py:207
  26.6 1.3 %collective-permute-start.10 = (bf16[64,640]{1,0:T(8,128)(2,1)S(1)}, bf16[64,640]{1,0:T(8,128)(2,1)S(1)}, u32[]{:S(2)}, u32[]{:S(2)}) collective-permute-start(bf16[64,640]{1,0:T(8,128)(2,1)S(1)} %get-tuple-element.64), channel_id=1, source_target_pairs={{0,4},{1,5},{2,6},{3,7},{4,0},{5,1},{6,2},{7,3},{8,12},{9,13},{10,... | collective-permute-start | bytes 245768 | tf_op jit(solution)/shard_map/ppermute | solution.py:207
  27.8 1.5 %collective-permute-start.11 = (bf16[64,640]{1,0:T(8,128)(2,1)S(1)}, bf16[64,640]{1,0:T(8,128)(2,1)S(1)}, u32[]{:S(2)}, u32[]{:S(2)}) collective-permute-start(bf16[64,640]{1,0:T(8,128)(2,1)S(1)} %get-tuple-element.65), channel_id=1, source_target_pairs={{0,6},{1,7},{2,4},{3,5},{4,2},{5,3},{6,0},{7,1},{8,14},{9,15},{10,... | collective-permute-start | bytes 245768 | tf_op jit(solution)/shard_map/ppermute | solution.py:207
  29.3 0.8 %collective-permute-start.13 = (bf16[64,640]{1,0:T(8,128)(2,1)S(1)}, bf16[64,640]{1,0:T(8,128)(2,1)S(1)}, u32[]{:S(2)}, u32[]{:S(2)}) collective-permute-start(bf16[64,640]{1,0:T(8,128)(2,1)S(1)} %get-tuple-element.67), channel_id=1, source_target_pairs={{0,2},{1,3},{2,0},{3,1},{4,6},{5,7},{6,4},{7,5},{8,10},{9,11},{10,... | collective-permute-start | bytes 245768 | tf_op jit(solution)/shard_map/ppermute | solution.py:207
  30.1 1.3 %collective-permute-start.14 = (bf16[64,640]{1,0:T(8,128)(2,1)S(1)}, bf16[64,640]{1,0:T(8,128)(2,1)S(1)}, u32[]{:S(2)}, u32[]{:S(2)}) collective-permute-start(bf16[64,640]{1,0:T(8,128)(2,1)S(1)} %get-tuple-element.68), channel_id=1, source_target_pairs={{0,4},{1,5},{2,6},{3,7},{4,0},{5,1},{6,2},{7,3},{8,12},{9,13},{10,... | collective-permute-start | bytes 245768 | tf_op jit(solution)/shard_map/ppermute | solution.py:207
  31.5 1.2 %collective-permute-start.15 = (bf16[64,640]{1,0:T(8,128)(2,1)S(1)}, bf16[64,640]{1,0:T(8,128)(2,1)S(1)}, u32[]{:S(2)}, u32[]{:S(2)}) collective-permute-start(bf16[64,640]{1,0:T(8,128)(2,1)S(1)} %get-tuple-element.69), channel_id=1, source_target_pairs={{0,6},{1,7},{2,4},{3,5},{4,2},{5,3},{6,0},{7,1},{8,14},{9,15},{10,... | collective-permute-start | bytes 245768 | tf_op jit(solution)/shard_map/ppermute | solution.py:207
  32.8 0.9 %collective-permute-done.11.refs_3_ = bf16[64,640]{1,0:T(8,128)(2,1)S(1)} collective-permute-done((bf16[64,640]{1,0:T(8,128)(2,1)S(1)}, bf16[64,640]{1,0:T(8,128)(2,1)S(1)}, u32[]{:S(2)}, u32[]{:S(2)}) %collective-permute-start.11) | collective-permute-done | bytes 81952 | tf_op jit(solution)/shard_map/ppermute | solution.py:207
  34.0 2.4 %collective-permute-start.12 = (bf16[64,640]{1,0:T(8,128)(2,1)S(1)}, bf16[64,640]{1,0:T(8,128)(2,1)S(1)}, u32[]{:S(2)}, u32[]{:S(2)}) collective-permute-start(bf16[64,640]{1,0:T(8,128)(2,1)S(1)} %combine.1), channel_id=1, source_target_pairs={{0,8},{1,9},{2,10},{3,11},{4,12},{5,13},{6,14},{7,15},{8,0},{9,1},... | collective-permute-start | bytes 245768 | tf_op jit(solution)/shard_map/ppermute | solution.py:207
  36.4 0.5 collective-permute-done.15.refs_4_
  36.9 2.5 %collective-permute-done.12.refs_0_ = bf16[64,640]{1,0:T(8,128)(2,1)S(1)} collective-permute-done((bf16[64,640]{1,0:T(8,128)(2,1)S(1)}, bf16[64,640]{1,0:T(8,128)(2,1)S(1)}, u32[]{:S(2)}, u32[]{:S(2)}) %collective-permute-start.12) | collective-permute-done | bytes 81952 | tf_op jit(solution)/shard_map/ppermute | solution.py:207
  39.7 1.2 %collective-permute-done.16.got_ref = bf16[32,512]{1,0:T(8,128)(2,1)S(1)} collective-permute-done((bf16[32,512]{1,0:T(8,128)(2,1)S(1)}, bf16[32,512]{1,0:T(8,128)(2,1)S(1)}, u32[]{:S(2)}, u32[]{:S(2)}) %collective-permute-start.16) | collective-permute-done | bytes 32800 | tf_op jit(solution)/shard_map/ppermute | solution.py:207
  40.9 2.9 %project.1 = bf16[16,8,448]{2,1,0:T(8,128)(2,1)} custom-call(bf16[32,512]{1,0:T(8,128)(2,1)S(1)} %get-tuple-element.70.own_ref, bf16[32,512]{1,0:T(8,128)(2,1)S(1)} %collective-permute-done.16.got_ref, bf16[8,512,128]{2,1,0:T(8,128)(2,1)S(1)} %copy-done.1, bf16[1024,7168]{1,0:T(8,128)(2,1)S(1)} %copy-done), custom_call_target="tpu_custom_call" | custom-call | tf_op jit(solution)/shard_map/project/pallas_call | solution.py:174
  43.8 5.7 %all-to-all-start = ((bf16[16,8,448]{2,1,0:T(8,128)(2,1)}), bf16[16,8,448]{2,1,0:T(8,128)(2,1)S(1)}, u32[]{:S(2)}, u32[]{:S(2)}) async-start(bf16[16,8,448]{2,1,0:T(8,128)(2,1)} %project.1), calls=%async_computation | async-start | bytes 262144 | tf_op jit(solution)/shard_map/all_to_all | solution.py:240
  49.7 7.8 %all-to-all-done.in_ref = bf16[16,8,448]{2,1,0:T(8,128)(2,1)S(1)} async-done(((bf16[16,8,448]{2,1,0:T(8,128)(2,1)}), bf16[16,8,448]{2,1,0:T(8,128)(2,1)S(1)}, u32[]{:S(2)}, u32[]{:S(2)}) %all-to-all-start) | async-done | bytes 114720 | tf_op jit(solution)/shard_map/all_to_all | solution.py:240
  57.6 0.7 %finish.1 = bf16[2,4,448]{2,1,0:T(4,128)(2,1)} custom-call(bf16[16,8,448]{2,1,0:T(8,128)(2,1)S(1)} %all-to-all-done.in_ref, f32[8,128]{1,0:T(8,128)S(1)} %broadcast_in_dim.15.keep_ref), custom_call_target="tpu_custom_call" | custom-call | tf_op jit(solution)/shard_map/finish/pallas_call | solution.py:193
  (25 shorter events, 1.1 us)
Async XLA Ops:
  0.0 1.6 %collective-permute-start = (bf16[2,4,8,576]{3,2,1,0:T(8,128)(2,1)}, bf16[2,4,8,576]{3,2,1,0:T(8,128)(2,1)S(1)}, u32[]{:S(2)}, u32[]{:S(2)}) collective-permute-start(bf16[2,4,8,576]{3,2,1,0:T(8,128)(2,1)} %param.6), channel_id=1, source_target_pairs={{0,1},{1,0},{2,3},{3,2},{4,5},{5,4},{6,7},{7,6},{8,9},{9,8},{10,11... | collective-permute-start | bytes 221192 | tf_op jit(solution)/shard_map/ppermute | solution.py:207
  1.6 10.3 %collective-permute-start.2 = (bf16[2,576,2048]{2,1,0:T(8,128)(2,1)}, bf16[2,576,2048]{2,1,0:T(8,128)(2,1)}, u32[]{:S(2)}, u32[]{:S(2)}) collective-permute-start(bf16[2,576,2048]{2,1,0:T(8,128)(2,1)} %bitcast.13), channel_id=1, source_target_pairs={{0,1},{1,0},{2,3},{3,2},{4,5},{5,4},{6,7},{7,6},{8,9},{9,8},{10,11... | collective-permute-start | bytes 14155784 | tf_op jit(solution)/shard_map/ppermute | solution.py:207
  2.7 15.7 %copy-start.3 = (s32[2]{0:T(128)S(1)}, s32[2]{0:T(128)}, u32[]{:S(2)}) copy-start(s32[2]{0:T(128)} %param.8) | copy-start | bytes 28
  2.8 11.0 %collective-permute-start.1 = (bf16[64,576]{1,0:T(8,128)(2,1)S(1)}, bf16[64,576]{1,0:T(8,128)(2,1)S(1)}, u32[]{:S(2)}, u32[]{:S(2)}) collective-permute-start(bf16[64,576]{1,0:T(8,128)(2,1)S(1)} %bitcast.8), channel_id=1, source_target_pairs={{0,8},{1,9},{2,10},{3,11},{4,12},{5,13},{6,14},{7,15},{8,0},{9,1},... | collective-permute-start | bytes 221192 | tf_op jit(solution)/shard_map/ppermute | solution.py:207
  6.6 7.2 %collective-permute-start.3 = (bf16[64,576]{1,0:T(8,128)(2,1)S(1)}, bf16[64,576]{1,0:T(8,128)(2,1)S(1)}, u32[]{:S(2)}, u32[]{:S(2)}) collective-permute-start(bf16[64,576]{1,0:T(8,128)(2,1)S(1)} %bitcast.9), channel_id=1, source_target_pairs={{0,2},{1,3},{2,0},{3,1},{4,6},{5,7},{6,4},{7,5},{8,10},{9,11},{10,... | collective-permute-start | bytes 221192 | tf_op jit(solution)/shard_map/ppermute | solution.py:207
  8.1 5.7 %collective-permute-start.4 = (bf16[64,576]{1,0:T(8,128)(2,1)S(1)}, bf16[64,576]{1,0:T(8,128)(2,1)S(1)}, u32[]{:S(2)}, u32[]{:S(2)}) collective-permute-start(bf16[64,576]{1,0:T(8,128)(2,1)S(1)} %bitcast.10), channel_id=1, source_target_pairs={{0,4},{1,5},{2,6},{3,7},{4,0},{5,1},{6,2},{7,3},{8,12},{9,13},{10,... | collective-permute-start | bytes 221192 | tf_op jit(solution)/shard_map/ppermute | solution.py:207
  9.7 5.3 %collective-permute-start.5 = (bf16[64,576]{1,0:T(8,128)(2,1)S(1)}, bf16[64,576]{1,0:T(8,128)(2,1)S(1)}, u32[]{:S(2)}, u32[]{:S(2)}) collective-permute-start(bf16[64,576]{1,0:T(8,128)(2,1)S(1)} %bitcast.11), channel_id=1, source_target_pairs={{0,6},{1,7},{2,4},{3,5},{4,2},{5,3},{6,0},{7,1},{8,14},{9,15},{10,... | collective-permute-start | bytes 221192 | tf_op jit(solution)/shard_map/ppermute | solution.py:207
  15.0 7.0 %collective-permute-start.6 = (bf16[64,576]{1,0:T(8,128)(2,1)S(1)}, bf16[64,576]{1,0:T(8,128)(2,1)S(1)}, u32[]{:S(2)}, u32[]{:S(2)}) collective-permute-start(bf16[64,576]{1,0:T(8,128)(2,1)S(1)} %collective-permute-done.1.refs_0_), channel_id=1, source_target_pairs={{0,2},{1,3},{2,0},{3,1},{4,6},{5,7},{6,4},{7,5},{8,10},{9,11},{10,... | collective-permute-start | bytes 221192 | tf_op jit(solution)/shard_map/ppermute | solution.py:207
  16.0 6.0 %collective-permute-start.7 = (bf16[64,576]{1,0:T(8,128)(2,1)S(1)}, bf16[64,576]{1,0:T(8,128)(2,1)S(1)}, u32[]{:S(2)}, u32[]{:S(2)}) collective-permute-start(bf16[64,576]{1,0:T(8,128)(2,1)S(1)} %collective-permute-done.1.refs_0_), channel_id=1, source_target_pairs={{0,4},{1,5},{2,6},{3,7},{4,0},{5,1},{6,2},{7,3},{8,12},{9,13},{10,... | collective-permute-start | bytes 221192 | tf_op jit(solution)/shard_map/ppermute | solution.py:207
  17.0 5.3 %collective-permute-start.8 = (bf16[64,576]{1,0:T(8,128)(2,1)S(1)}, bf16[64,576]{1,0:T(8,128)(2,1)S(1)}, u32[]{:S(2)}, u32[]{:S(2)}) collective-permute-start(bf16[64,576]{1,0:T(8,128)(2,1)S(1)} %collective-permute-done.1.refs_0_), channel_id=1, source_target_pairs={{0,6},{1,7},{2,4},{3,5},{4,2},{5,3},{6,0},{7,1},{8,14},{9,15},{10,... | collective-permute-start | bytes 221192 | tf_op jit(solution)/shard_map/ppermute | solution.py:207
  18.6 22.4 %copy-start = (bf16[1024,7168]{1,0:T(8,128)(2,1)S(1)}, bf16[1024,7168]{1,0:T(8,128)(2,1)}, u32[]{:S(2)}) copy-start(bf16[1024,7168]{1,0:T(8,128)(2,1)} %weight_ref.1) | copy-start | bytes 44040196
  21.9 19.0 %copy-start.1 = (bf16[8,512,128]{2,1,0:T(8,128)(2,1)S(1)}, bf16[8,512,128]{2,1,0:T(8,128)(2,1)}, u32[]{:S(2)}) copy-start(bf16[8,512,128]{2,1,0:T(8,128)(2,1)} %up_ref.1) | copy-start | bytes 3145732
  25.7 5.8 %collective-permute-start.9 = (bf16[64,640]{1,0:T(8,128)(2,1)S(1)}, bf16[64,640]{1,0:T(8,128)(2,1)S(1)}, u32[]{:S(2)}, u32[]{:S(2)}) collective-permute-start(bf16[64,640]{1,0:T(8,128)(2,1)S(1)} %get-tuple-element.63), channel_id=1, source_target_pairs={{0,2},{1,3},{2,0},{3,1},{4,6},{5,7},{6,4},{7,5},{8,10},{9,11},{10,... | collective-permute-start | bytes 245768 | tf_op jit(solution)/shard_map/ppermute | solution.py:207
  26.6 6.2 %collective-permute-start.10 = (bf16[64,640]{1,0:T(8,128)(2,1)S(1)}, bf16[64,640]{1,0:T(8,128)(2,1)S(1)}, u32[]{:S(2)}, u32[]{:S(2)}) collective-permute-start(bf16[64,640]{1,0:T(8,128)(2,1)S(1)} %get-tuple-element.64), channel_id=1, source_target_pairs={{0,4},{1,5},{2,6},{3,7},{4,0},{5,1},{6,2},{7,3},{8,12},{9,13},{10,... | collective-permute-start | bytes 245768 | tf_op jit(solution)/shard_map/ppermute | solution.py:207
  27.8 5.8 %collective-permute-start.11 = (bf16[64,640]{1,0:T(8,128)(2,1)S(1)}, bf16[64,640]{1,0:T(8,128)(2,1)S(1)}, u32[]{:S(2)}, u32[]{:S(2)}) collective-permute-start(bf16[64,640]{1,0:T(8,128)(2,1)S(1)} %get-tuple-element.65), channel_id=1, source_target_pairs={{0,6},{1,7},{2,4},{3,5},{4,2},{5,3},{6,0},{7,1},{8,14},{9,15},{10,... | collective-permute-start | bytes 245768 | tf_op jit(solution)/shard_map/ppermute | solution.py:207
  29.3 7.1 %collective-permute-start.13 = (bf16[64,640]{1,0:T(8,128)(2,1)S(1)}, bf16[64,640]{1,0:T(8,128)(2,1)S(1)}, u32[]{:S(2)}, u32[]{:S(2)}) collective-permute-start(bf16[64,640]{1,0:T(8,128)(2,1)S(1)} %get-tuple-element.67), channel_id=1, source_target_pairs={{0,2},{1,3},{2,0},{3,1},{4,6},{5,7},{6,4},{7,5},{8,10},{9,11},{10,... | collective-permute-start | bytes 245768 | tf_op jit(solution)/shard_map/ppermute | solution.py:207
  30.1 6.4 %collective-permute-start.14 = (bf16[64,640]{1,0:T(8,128)(2,1)S(1)}, bf16[64,640]{1,0:T(8,128)(2,1)S(1)}, u32[]{:S(2)}, u32[]{:S(2)}) collective-permute-start(bf16[64,640]{1,0:T(8,128)(2,1)S(1)} %get-tuple-element.68), channel_id=1, source_target_pairs={{0,4},{1,5},{2,6},{3,7},{4,0},{5,1},{6,2},{7,3},{8,12},{9,13},{10,... | collective-permute-start | bytes 245768 | tf_op jit(solution)/shard_map/ppermute | solution.py:207
  31.5 5.3 %collective-permute-start.15 = (bf16[64,640]{1,0:T(8,128)(2,1)S(1)}, bf16[64,640]{1,0:T(8,128)(2,1)S(1)}, u32[]{:S(2)}, u32[]{:S(2)}) collective-permute-start(bf16[64,640]{1,0:T(8,128)(2,1)S(1)} %get-tuple-element.69), channel_id=1, source_target_pairs={{0,6},{1,7},{2,4},{3,5},{4,2},{5,3},{6,0},{7,1},{8,14},{9,15},{10,... | collective-permute-start | bytes 245768 | tf_op jit(solution)/shard_map/ppermute | solution.py:207
  34.0 5.4 %collective-permute-start.12 = (bf16[64,640]{1,0:T(8,128)(2,1)S(1)}, bf16[64,640]{1,0:T(8,128)(2,1)S(1)}, u32[]{:S(2)}, u32[]{:S(2)}) collective-permute-start(bf16[64,640]{1,0:T(8,128)(2,1)S(1)} %combine.1), channel_id=1, source_target_pairs={{0,8},{1,9},{2,10},{3,11},{4,12},{5,13},{6,14},{7,15},{8,0},{9,1},... | collective-permute-start | bytes 245768 | tf_op jit(solution)/shard_map/ppermute | solution.py:207
  39.6 1.3 %collective-permute-start.16 = (bf16[32,512]{1,0:T(8,128)(2,1)S(1)}, bf16[32,512]{1,0:T(8,128)(2,1)S(1)}, u32[]{:S(2)}, u32[]{:S(2)}) collective-permute-start(bf16[32,512]{1,0:T(8,128)(2,1)S(1)} %get-tuple-element.71), channel_id=1, source_target_pairs={{0,1},{1,0},{2,3},{3,2},{4,5},{5,4},{6,7},{7,6},{8,9},{9,8},{10,11... | collective-permute-start | bytes 98312 | tf_op jit(solution)/shard_map/ppermute | solution.py:207
  40.9 8.7 %copy-start.2 = (s32[2,4]{1,0:T(2,128)S(1)}, s32[2,4]{1,0:T(2,128)}, u32[]{:S(2)}) copy-start(s32[2,4]{1,0:T(2,128)} %param.9) | copy-start | bytes 100
  43.8 13.7 %all-to-all-start = ((bf16[16,8,448]{2,1,0:T(8,128)(2,1)}), bf16[16,8,448]{2,1,0:T(8,128)(2,1)S(1)}, u32[]{:S(2)}, u32[]{:S(2)}) async-start(bf16[16,8,448]{2,1,0:T(8,128)(2,1)} %project.1), calls=%async_computation | async-start | bytes 262144 | tf_op jit(solution)/shard_map/all_to_all | solution.py:240

commit v3 on v2

--- a/solution.py
+++ b/solution.py
@@ -13,6 +13,7 @@
 SCORE_FLOOR = -1e30
 STAT_LANES = 128
 MIB = 1024 * 1024
+HINT = 20 * MIB
 
 
 def split_low(x):
@@ -20,9 +21,27 @@
     return high, (x - high).astype(jnp.bfloat16).astype(jnp.float32)
 
 
+def select_kernel(own_ref, got_ref, out_ref):
+    core = lax.rem(lax.axis_index("ctx"), 2)
+    rows = out_ref.shape[0] // 2
+    out_ref[:rows] = own_ref[core].reshape(rows, -1)
+    out_ref[rows:] = got_ref[core].reshape(rows, -1)
+
+
+def select(own, got):
+    requests, spec, heads, feature = own.shape
+    return pl.pallas_call(
+        select_kernel,
+        out_shape=jax.ShapeDtypeStruct((2 * spec * heads, feature), own.dtype),
+        compiler_params=pltpu.CompilerParams(vmem_limit_bytes=8 * MIB),
+        cost_estimate=pl.CostEstimate(flops=0, bytes_accessed=HINT, transcendentals=0),
+        name="select",
+    )(own, got)
+
+
 def attend_kernel(chunks, spec, heads, latent, lengths_ref, *refs):
     q_refs, key_refs, out_refs = refs[:chunks], refs[chunks : chunks + 2], refs[chunks + 2 :]
-    block = key_refs[0].shape[1]
+    block = key_refs[1].shape[1]
     width = min(block, 512)
     per_block = block // width
     steps = 2 * per_block
@@ -36,7 +55,9 @@
 
     def keys(step, features):
         start = (step % per_block) * width
-        return key_refs[step // per_block][:features, start : start + width]
+        if step < per_block:
+            return key_refs[0][lax.rem(me, 2), :features, start : start + width]
+        return key_refs[1][:features, start : start + width]
 
     def score(step):
         tile = jnp.dot(queries, keys(step, None), preferred_element_type=jnp.float32)
@@ -72,7 +93,7 @@
 def attend(lengths, query_chunks, keys, spec, heads, latent):
     chunks = len(query_chunks)
     chunk, feature = query_chunks[0].shape
-    rows, positions = chunks * chunk, 2 * keys[0].shape[1]
+    rows, positions = chunks * chunk, 2 * keys[1].shape[1]
     return pl.pallas_call(
         functools.partial(attend_kernel, chunks, spec, heads, latent),
         out_shape=[jax.ShapeDtypeStruct((chunk, latent + STAT_LANES), jnp.bfloat16)] * chunks,
@@ -208,20 +229,18 @@
 
     chunk = requests * spec * heads
     got = swap(queries, 1)
-    both = jnp.stack([queries, got], axis=1)
-    mine = lax.dynamic_index_in_dim(both, core, 0, keepdims=False).reshape(chunk, feature)
+    mine = select(queries, got)
     own_keys = jnp.swapaxes(latent_cache, 1, 2)
-    own_keys = lax.optimization_barrier((own_keys, got))[0]
-    got_keys = swap(own_keys, 1)
+    got_keys = swap(lax.optimization_barrier((own_keys, got))[0], 1)
 
     far_bit = n // 2
-    near = [2 * k for k in range(1, n // 4)]
+    near = [2 * k for k in range(1, n // 4)][::-1]
     far = swap(mine, far_bit)
     near_queries = [swap(mine, bits) for bits in near]
 
-    own_keys, draft_mask = lax.optimization_barrier((own_keys, draft_mask, mine))[:2]
-    keys = [lax.dynamic_index_in_dim(k, core, 0, keepdims=False) for k in (own_keys, got_keys)]
-    far, keys, near_queries = lax.optimization_barrier((far, keys, near_queries))
+    draft_mask = lax.optimization_barrier((draft_mask, mine))[0]
+    keys = [own_keys, lax.dynamic_index_in_dim(got_keys, core, 0, keepdims=False)]
+    far, near_queries[2] = lax.optimization_barrier((far, near_queries[2]))
     far_queries = [swap(far, bits) for bits in near]
     spread = jnp.broadcast_to(lengths[:, None], (requests, STAT_LANES))
     keep = draft_mask.astype(jnp.float32).reshape(requests * spec, 1)

time: 58.6 us -> 56.8 us (0.969)
  starting transfers between devices: 26.7 us -> 25.7 us
  local copies, waits for them, and re-layouts: 3.89 us -> 2.95 us
  other arithmetic: 0.8 us -> 0.01 us
  waiting for transfers between devices: 15.8 us -> 16.5 us
    all_to_all x1, starting transfers between devices: 5.75 us -> 3.58 us  [on_device(): received = lax.all_to_all(outs, 'ctx', 0, 0, tiled=True)]
    squeeze x2 -> x1, local copies, waits for them, and re-layouts: 3.65 us -> 1.82 us  [on_device(): lax.dynamic_index_in_dim(got_keys, core, 0, keepdims=False)]
    ppermute x17, starting transfers between devices: 20.9 us -> 22.1 us  [swap(): return lax.ppermute(x, 'ctx', [(i, i ^ bits) for i in range(n)])]
    unnamed x8 -> x12, local copies, waits for them, and re-layouts: 0.02 us -> 0.91 us
    another operation x1 -> x0, other arithmetic: 0.79 us -> none  [on_device(): both = jnp.stack([queries, got], axis=1)]
    ppermute x17, waiting for transfers between devices: 8.01 us -> 8.65 us  [swap(): return lax.ppermute(x, 'ctx', [(i, i ^ bits) for i in range(n)])]
  transfers between devices with their start and end apart: 18 -> 18, of which waited for: 9 -> 6; matrix products, arithmetic and copies ran while one was open for 8% -> 3% of each run, Pallas kernels for 6% -> 7%
where the time goes in v3:
time: 56.8 us; the launch traced here: 56.6 us
  starting transfers between devices  25.7 us (45%)
  waiting for transfers between devices  16.5 us (29%)
  Pallas kernels  11.3 us (20%)
  local copies, waits for them, and re-layouts  2.95 us (5%)
    ppermute x17, starting transfers between devices, swap(): return lax.ppermute(x, 'ctx', [(i, i ^ bits) for i in range(n)])  22.1 us
    ppermute x17, waiting for transfers between devices, swap(): return lax.ppermute(x, 'ctx', [(i, i ^ bits) for i in range(n)])  8.65 us
    all_to_all x1, waiting for transfers between devices, on_device(): received = lax.all_to_all(outs, 'ctx', 0, 0, tiled=True)  7.83 us
    pallas_call x2, Pallas kernels, attend(): pl.pallas_call(functools.partial(attend_kernel, chunks, spec, heads, late...  7.08 us
    all_to_all x1, starting transfers between devices, on_device(): received = lax.all_to_all(outs, 'ctx', 0, 0, tiled=True)  3.58 us
    pallas_call x1, Pallas kernels, project(): pl.pallas_call(functools.partial(project_kernel, heads, group), out_shape...  2.93 us
    squeeze x1, local copies, waits for them, and re-layouts, on_device(): lax.dynamic_index_in_dim(got_keys, core, 0, keepdims=False)  1.82 us
  transfers between devices with their start and end apart: 18, of which 6 were waited for; matrix products, arithmetic and copies ran while one was open for 3% of the time, Pallas kernels for 7%

profile of v3, /device:TPU:0, one launch (start us, length us, event | category | flops | bytes accessed | tf_op | source)
XLA Modules:
  0.0 56.6 jit_solution(7337232481766191500)
XLA Ops:
  0.0 0.5 collective-permute-start
  0.5 1.1 %collective-permute-done.got_ref = bf16[2,4,8,576]{3,2,1,0:T(8,128)(2,1)S(1)} collective-permute-done((bf16[2,4,8,576]{3,2,1,0:T(8,128)(2,1)}, bf16[2,4,8,576]{3,2,1,0:T(8,128)(2,1)S(1)}, u32[]{:S(2)}, u32[]{:S(2)}) %collective-permute-start) | collective-permute-done | bytes 73760 | tf_op jit(solution)/shard_map/ppermute | solution.py:228
  1.6 0.4 collective-permute-start.5
  1.9 0.9 %copy-done.2 = bf16[2,4,8,576]{3,2,1,0:T(8,128)(2,1)S(1)} copy-done((bf16[2,4,8,576]{3,2,1,0:T(8,128)(2,1)S(1)}, bf16[2,4,8,576]{3,2,1,0:T(8,128)(2,1)}, u32[]{:S(2)}) %copy-start.2) | copy-done | bytes 73752
  2.8 3.8 %collective-permute-start.3 = (bf16[64,576]{1,0:T(8,128)(2,1)S(1)}, bf16[64,576]{1,0:T(8,128)(2,1)S(1)}, u32[]{:S(2)}, u32[]{:S(2)}) collective-permute-start(bf16[64,576]{1,0:T(8,128)(2,1)S(1)} %select.3.refs_0_), channel_id=1, source_target_pairs={{0,8},{1,9},{2,10},{3,11},{4,12},{5,13},{6,14},{7,15},{8,0},{9,1},... | collective-permute-start | bytes 221192 | tf_op jit(solution)/shard_map/ppermute | solution.py:228
  6.6 1.5 %collective-permute-start.4 = (bf16[64,576]{1,0:T(8,128)(2,1)S(1)}, bf16[64,576]{1,0:T(8,128)(2,1)S(1)}, u32[]{:S(2)}, u32[]{:S(2)}) collective-permute-start(bf16[64,576]{1,0:T(8,128)(2,1)S(1)} %select.3.refs_0_), channel_id=1, source_target_pairs={{0,2},{1,3},{2,0},{3,1},{4,6},{5,7},{6,4},{7,5},{8,10},{9,11},{10,... | collective-permute-start | bytes 221192 | tf_op jit(solution)/shard_map/ppermute | solution.py:228
  8.2 1.5 %collective-permute-start.1 = (bf16[64,576]{1,0:T(8,128)(2,1)S(1)}, bf16[64,576]{1,0:T(8,128)(2,1)S(1)}, u32[]{:S(2)}, u32[]{:S(2)}) collective-permute-start(bf16[64,576]{1,0:T(8,128)(2,1)S(1)} %select.3.refs_0_), channel_id=1, source_target_pairs={{0,6},{1,7},{2,4},{3,5},{4,2},{5,3},{6,0},{7,1},{8,14},{9,15},{10,... | collective-permute-start | bytes 221192 | tf_op jit(solution)/shard_map/ppermute | solution.py:228
  9.7 0.4 collective-permute-start.2
  10.1 1.3 %collective-permute-done.3.refs_0_ = bf16[64,576]{1,0:T(8,128)(2,1)S(1)} collective-permute-done((bf16[64,576]{1,0:T(8,128)(2,1)S(1)}, bf16[64,576]{1,0:T(8,128)(2,1)S(1)}, u32[]{:S(2)}, u32[]{:S(2)}) %collective-permute-start.3) | collective-permute-done | bytes 73760 | tf_op jit(solution)/shard_map/ppermute | solution.py:228
  11.5 3.3 %collective-permute-start.6 = (bf16[64,576]{1,0:T(8,128)(2,1)S(1)}, bf16[64,576]{1,0:T(8,128)(2,1)S(1)}, u32[]{:S(2)}, u32[]{:S(2)}) collective-permute-start(bf16[64,576]{1,0:T(8,128)(2,1)S(1)} %collective-permute-done.3.refs_0_), channel_id=1, source_target_pairs={{0,6},{1,7},{2,4},{3,5},{4,2},{5,3},{6,0},{7,1},{8,14},{9,15},{10,... | collective-permute-start | bytes 221192 | tf_op jit(solution)/shard_map/ppermute | solution.py:228
  14.8 0.4 collective-permute-start.7
  15.3 0.1 collective-permute-start.8
  15.4 1.8 %dynamic-slice_bitcast_fusion.refs_5_ = bf16[576,2048]{1,0:T(8,128)(2,1)S(1)} fusion(bf16[2,576,2048]{2,1,0:T(8,128)(2,1)} %collective-permute-done.5, s32[]{:T(128)S(6)} %select_n.4), kind=kLoop, calls=%fused_computation | loop fusion | bytes 4718596 | tf_op jit(solution)/shard_map/jit(dynamic_index_in_dim)/squeeze | solution.py:242
  17.3 3.5 %attend.2 = (bf16[64,640]{1,0:T(8,128)(2,1)S(1)}, bf16[64,640]{1,0:T(8,128)(2,1)S(1)}, bf16[64,640]{1,0:T(8,128)(2,1)S(1)}, bf16[64,640]{1,0:T(8,128)(2,1)S(1)}) custom-call(s32[2,128]{1,0:T(2,128)S(1)} %broadcast_in_dim.6.lengths_ref, bf16[64,576]{1,0:T(8,128)(2,1)S(1)} %select.3.refs_0_, bf16[64,576]{1,0:T(8,128)(2,1)S(1)} %collective-permute-done.1.refs_1_, ...), custom_call_target="tpu_custom_call" | custom-call | flops 2281701376 | bytes 4718592 | tf_op jit(solution)/shard_map/attend/pallas_call | solution.py:97
  20.9 3.6 %attend.3 = (bf16[64,640]{1,0:T(8,128)(2,1)S(1)}, bf16[64,640]{1,0:T(8,128)(2,1)S(1)}, bf16[64,640]{1,0:T(8,128)(2,1)S(1)}, bf16[64,640]{1,0:T(8,128)(2,1)S(1)}) custom-call(s32[2,128]{1,0:T(2,128)S(1)} %broadcast_in_dim.6.lengths_ref, bf16[64,576]{1,0:T(8,128)(2,1)S(1)} %collective-permute-done.3.refs_0_, ...), custom_call_target="tpu_custom_call" | custom-call | flops 2281701376 | bytes 4718592 | tf_op jit(solution)/shard_map/attend/pallas_call | solution.py:97
  24.5 1.5 %collective-permute-start.10 = (bf16[64,640]{1,0:T(8,128)(2,1)S(1)}, bf16[64,640]{1,0:T(8,128)(2,1)S(1)}, u32[]{:S(2)}, u32[]{:S(2)}) collective-permute-start(bf16[64,640]{1,0:T(8,128)(2,1)S(1)} %get-tuple-element.54), channel_id=1, source_target_pairs={{0,4},{1,5},{2,6},{3,7},{4,0},{5,1},{6,2},{7,3},{8,12},{9,13},{10,... | collective-permute-start | bytes 245768 | tf_op jit(solution)/shard_map/ppermute | solution.py:228
  26.0 2.0 %collective-permute-start.11 = (bf16[64,640]{1,0:T(8,128)(2,1)S(1)}, bf16[64,640]{1,0:T(8,128)(2,1)S(1)}, u32[]{:S(2)}, u32[]{:S(2)}) collective-permute-start(bf16[64,640]{1,0:T(8,128)(2,1)S(1)} %get-tuple-element.55), channel_id=1, source_target_pairs={{0,2},{1,3},{2,0},{3,1},{4,6},{5,7},{6,4},{7,5},{8,10},{9,11},{10,... | collective-permute-start | bytes 245768 | tf_op jit(solution)/shard_map/ppermute | solution.py:228
  28.0 2.9 %collective-permute-start.13 = (bf16[64,640]{1,0:T(8,128)(2,1)S(1)}, bf16[64,640]{1,0:T(8,128)(2,1)S(1)}, u32[]{:S(2)}, u32[]{:S(2)}) collective-permute-start(bf16[64,640]{1,0:T(8,128)(2,1)S(1)} %get-tuple-element.57), channel_id=1, source_target_pairs={{0,6},{1,7},{2,4},{3,5},{4,2},{5,3},{6,0},{7,1},{8,14},{9,15},{10,... | collective-permute-start | bytes 245768 | tf_op jit(solution)/shard_map/ppermute | solution.py:228
  30.9 0.4 collective-permute-start.14
  31.4 0.4 collective-permute-start.15
  31.8 1.6 %collective-permute-done.9.refs_1_ = bf16[64,640]{1,0:T(8,128)(2,1)S(1)} collective-permute-done((bf16[64,640]{1,0:T(8,128)(2,1)S(1)}, bf16[64,640]{1,0:T(8,128)(2,1)S(1)}, u32[]{:S(2)}, u32[]{:S(2)}) %collective-permute-start.9) | collective-permute-done | bytes 81952 | tf_op jit(solution)/shard_map/ppermute | solution.py:228
  33.4 0.3 combine.1
  33.6 2.8 %collective-permute-start.12 = (bf16[64,640]{1,0:T(8,128)(2,1)S(1)}, bf16[64,640]{1,0:T(8,128)(2,1)S(1)}, u32[]{:S(2)}, u32[]{:S(2)}) collective-permute-start(bf16[64,640]{1,0:T(8,128)(2,1)S(1)} %combine.1), channel_id=1, source_target_pairs={{0,8},{1,9},{2,10},{3,11},{4,12},{5,13},{6,14},{7,15},{8,0},{9,1},... | collective-permute-start | bytes 245768 | tf_op jit(solution)/shard_map/ppermute | solution.py:228
  36.4 3.4 %collective-permute-done.12.refs_0_ = bf16[64,640]{1,0:T(8,128)(2,1)S(1)} collective-permute-done((bf16[64,640]{1,0:T(8,128)(2,1)S(1)}, bf16[64,640]{1,0:T(8,128)(2,1)S(1)}, u32[]{:S(2)}, u32[]{:S(2)}) %collective-permute-start.12) | collective-permute-done | bytes 81952 | tf_op jit(solution)/shard_map/ppermute | solution.py:228
  39.8 0.3 merge.1
  40.1 0.1 collective-permute-start.16
  40.2 1.2 %collective-permute-done.16.got_ref = bf16[32,512]{1,0:T(8,128)(2,1)S(1)} collective-permute-done((bf16[32,512]{1,0:T(8,128)(2,1)S(1)}, bf16[32,512]{1,0:T(8,128)(2,1)S(1)}, u32[]{:S(2)}, u32[]{:S(2)}) %collective-permute-start.16) | collective-permute-done | bytes 32800 | tf_op jit(solution)/shard_map/ppermute | solution.py:228
  41.4 2.9 %project.1 = bf16[16,8,448]{2,1,0:T(8,128)(2,1)} custom-call(bf16[32,512]{1,0:T(8,128)(2,1)S(1)} %get-tuple-element.60.own_ref, bf16[32,512]{1,0:T(8,128)(2,1)S(1)} %collective-permute-done.16.got_ref, bf16[8,512,128]{2,1,0:T(8,128)(2,1)S(1)} %copy-done.1, bf16[1024,7168]{1,0:T(8,128)(2,1)S(1)} %copy-done), custom_call_target="tpu_custom_call" | custom-call | tf_op jit(solution)/shard_map/project/pallas_call | solution.py:195
  44.3 3.6 %all-to-all-start = ((bf16[16,8,448]{2,1,0:T(8,128)(2,1)}), bf16[16,8,448]{2,1,0:T(8,128)(2,1)S(1)}, u32[]{:S(2)}, u32[]{:S(2)}) async-start(bf16[16,8,448]{2,1,0:T(8,128)(2,1)} %project.1), calls=%async_computation | async-start | bytes 262144 | tf_op jit(solution)/shard_map/all_to_all | solution.py:259
  47.9 0.1 broadcast_in_dim.14
  48.0 7.8 %all-to-all-done.in_ref = bf16[16,8,448]{2,1,0:T(8,128)(2,1)S(1)} async-done(((bf16[16,8,448]{2,1,0:T(8,128)(2,1)}), bf16[16,8,448]{2,1,0:T(8,128)(2,1)S(1)}, u32[]{:S(2)}, u32[]{:S(2)}) %all-to-all-start) | async-done | bytes 114720 | tf_op jit(solution)/shard_map/all_to_all | solution.py:259
  55.9 0.7 %finish.1 = bf16[2,4,448]{2,1,0:T(4,128)(2,1)} custom-call(bf16[16,8,448]{2,1,0:T(8,128)(2,1)S(1)} %all-to-all-done.in_ref, f32[8,128]{1,0:T(8,128)S(1)} %broadcast_in_dim.15.keep_ref), custom_call_target="tpu_custom_call" | custom-call | tf_op jit(solution)/shard_map/finish/pallas_call | solution.py:214
  (28 shorter events, 0.2 us)
Async XLA Ops:
  0.0 17.2 %copy-start.5 = (s32[2]{0:T(128)S(1)}, s32[2]{0:T(128)}, u32[]{:S(2)}) copy-start(s32[2]{0:T(128)} %param.8) | copy-start | bytes 28
  0.0 1.6 %collective-permute-start = (bf16[2,4,8,576]{3,2,1,0:T(8,128)(2,1)}, bf16[2,4,8,576]{3,2,1,0:T(8,128)(2,1)S(1)}, u32[]{:S(2)}, u32[]{:S(2)}) collective-permute-start(bf16[2,4,8,576]{3,2,1,0:T(8,128)(2,1)} %own_ref.1), channel_id=1, source_target_pairs={{0,1},{1,0},{2,3},{3,2},{4,5},{5,4},{6,7},{7,6},{8,9},{9,8},{10,11... | collective-permute-start | bytes 221192 | tf_op jit(solution)/shard_map/ppermute | solution.py:228
  1.6 13.7 %collective-permute-start.5 = (bf16[2,576,2048]{2,1,0:T(8,128)(2,1)}, bf16[2,576,2048]{2,1,0:T(8,128)(2,1)}, u32[]{:S(2)}, u32[]{:S(2)}) collective-permute-start(bf16[2,576,2048]{2,1,0:T(8,128)(2,1)} %bitcast.3), channel_id=1, source_target_pairs={{0,1},{1,0},{2,3},{3,2},{4,5},{5,4},{6,7},{7,6},{8,9},{9,8},{10,11... | collective-permute-start | bytes 14155784 | tf_op jit(solution)/shard_map/ppermute | solution.py:228
  1.9 0.9 %copy-start.2 = (bf16[2,4,8,576]{3,2,1,0:T(8,128)(2,1)S(1)}, bf16[2,4,8,576]{3,2,1,0:T(8,128)(2,1)}, u32[]{:S(2)}) copy-start(bf16[2,4,8,576]{3,2,1,0:T(8,128)(2,1)} %own_ref.1) | copy-start | bytes 221188
  2.8 8.6 %collective-permute-start.3 = (bf16[64,576]{1,0:T(8,128)(2,1)S(1)}, bf16[64,576]{1,0:T(8,128)(2,1)S(1)}, u32[]{:S(2)}, u32[]{:S(2)}) collective-permute-start(bf16[64,576]{1,0:T(8,128)(2,1)S(1)} %select.3.refs_0_), channel_id=1, source_target_pairs={{0,8},{1,9},{2,10},{3,11},{4,12},{5,13},{6,14},{7,15},{8,0},{9,1},... | collective-permute-start | bytes 221192 | tf_op jit(solution)/shard_map/ppermute | solution.py:228
  6.6 4.8 %collective-permute-start.4 = (bf16[64,576]{1,0:T(8,128)(2,1)S(1)}, bf16[64,576]{1,0:T(8,128)(2,1)S(1)}, u32[]{:S(2)}, u32[]{:S(2)}) collective-permute-start(bf16[64,576]{1,0:T(8,128)(2,1)S(1)} %select.3.refs_0_), channel_id=1, source_target_pairs={{0,2},{1,3},{2,0},{3,1},{4,6},{5,7},{6,4},{7,5},{8,10},{9,11},{10,... | collective-permute-start | bytes 221192 | tf_op jit(solution)/shard_map/ppermute | solution.py:228
  8.2 9.2 %copy-start.3 = (bf16[2,2048,576]{1,2,0:T(8,128)(2,1)S(1)}, bf16[2,2048,576]{1,2,0:T(8,128)(2,1)}, u32[]{:S(2)}) copy-start(bf16[2,2048,576]{1,2,0:T(8,128)(2,1)} %param.7) | copy-start | bytes 14155780
  8.2 9.0 %collective-permute-start.1 = (bf16[64,576]{1,0:T(8,128)(2,1)S(1)}, bf16[64,576]{1,0:T(8,128)(2,1)S(1)}, u32[]{:S(2)}, u32[]{:S(2)}) collective-permute-start(bf16[64,576]{1,0:T(8,128)(2,1)S(1)} %select.3.refs_0_), channel_id=1, source_target_pairs={{0,6},{1,7},{2,4},{3,5},{4,2},{5,3},{6,0},{7,1},{8,14},{9,15},{10,... | collective-permute-start | bytes 221192 | tf_op jit(solution)/shard_map/ppermute | solution.py:228
  9.7 7.5 %collective-permute-start.2 = (bf16[64,576]{1,0:T(8,128)(2,1)S(1)}, bf16[64,576]{1,0:T(8,128)(2,1)S(1)}, u32[]{:S(2)}, u32[]{:S(2)}) collective-permute-start(bf16[64,576]{1,0:T(8,128)(2,1)S(1)} %select.3.refs_0_), channel_id=1, source_target_pairs={{0,4},{1,5},{2,6},{3,7},{4,0},{5,1},{6,2},{7,3},{8,12},{9,13},{10,... | collective-permute-start | bytes 221192 | tf_op jit(solution)/shard_map/ppermute | solution.py:228
  11.5 9.4 %collective-permute-start.6 = (bf16[64,576]{1,0:T(8,128)(2,1)S(1)}, bf16[64,576]{1,0:T(8,128)(2,1)S(1)}, u32[]{:S(2)}, u32[]{:S(2)}) collective-permute-start(bf16[64,576]{1,0:T(8,128)(2,1)S(1)} %collective-permute-done.3.refs_0_), channel_id=1, source_target_pairs={{0,6},{1,7},{2,4},{3,5},{4,2},{5,3},{6,0},{7,1},{8,14},{9,15},{10,... | collective-permute-start | bytes 221192 | tf_op jit(solution)/shard_map/ppermute | solution.py:228
  14.8 6.1 %collective-permute-start.7 = (bf16[64,576]{1,0:T(8,128)(2,1)S(1)}, bf16[64,576]{1,0:T(8,128)(2,1)S(1)}, u32[]{:S(2)}, u32[]{:S(2)}) collective-permute-start(bf16[64,576]{1,0:T(8,128)(2,1)S(1)} %collective-permute-done.3.refs_0_), channel_id=1, source_target_pairs={{0,4},{1,5},{2,6},{3,7},{4,0},{5,1},{6,2},{7,3},{8,12},{9,13},{10,... | collective-permute-start | bytes 221192 | tf_op jit(solution)/shard_map/ppermute | solution.py:228
  15.3 5.6 %collective-permute-start.8 = (bf16[64,576]{1,0:T(8,128)(2,1)S(1)}, bf16[64,576]{1,0:T(8,128)(2,1)S(1)}, u32[]{:S(2)}, u32[]{:S(2)}) collective-permute-start(bf16[64,576]{1,0:T(8,128)(2,1)S(1)} %collective-permute-done.3.refs_0_), channel_id=1, source_target_pairs={{0,2},{1,3},{2,0},{3,1},{4,6},{5,7},{6,4},{7,5},{8,10},{9,11},{10,... | collective-permute-start | bytes 221192 | tf_op jit(solution)/shard_map/ppermute | solution.py:228
  17.3 24.0 %copy-start = (bf16[1024,7168]{1,0:T(8,128)(2,1)S(1)}, bf16[1024,7168]{1,0:T(8,128)(2,1)}, u32[]{:S(2)}) copy-start(bf16[1024,7168]{1,0:T(8,128)(2,1)} %weight_ref.1) | copy-start | bytes 44040196
  20.9 20.5 %copy-start.1 = (bf16[8,512,128]{2,1,0:T(8,128)(2,1)S(1)}, bf16[8,512,128]{2,1,0:T(8,128)(2,1)}, u32[]{:S(2)}) copy-start(bf16[8,512,128]{2,1,0:T(8,128)(2,1)} %up_ref.1) | copy-start | bytes 3145732
  24.5 6.9 %collective-permute-start.10 = (bf16[64,640]{1,0:T(8,128)(2,1)S(1)}, bf16[64,640]{1,0:T(8,128)(2,1)S(1)}, u32[]{:S(2)}, u32[]{:S(2)}) collective-permute-start(bf16[64,640]{1,0:T(8,128)(2,1)S(1)} %get-tuple-element.54), channel_id=1, source_target_pairs={{0,4},{1,5},{2,6},{3,7},{4,0},{5,1},{6,2},{7,3},{8,12},{9,13},{10,... | collective-permute-start | bytes 245768 | tf_op jit(solution)/shard_map/ppermute | solution.py:228
  26.0 5.8 %collective-permute-start.11 = (bf16[64,640]{1,0:T(8,128)(2,1)S(1)}, bf16[64,640]{1,0:T(8,128)(2,1)S(1)}, u32[]{:S(2)}, u32[]{:S(2)}) collective-permute-start(bf16[64,640]{1,0:T(8,128)(2,1)S(1)} %get-tuple-element.55), channel_id=1, source_target_pairs={{0,2},{1,3},{2,0},{3,1},{4,6},{5,7},{6,4},{7,5},{8,10},{9,11},{10,... | collective-permute-start | bytes 245768 | tf_op jit(solution)/shard_map/ppermute | solution.py:228
  28.0 5.3 %collective-permute-start.9 = (bf16[64,640]{1,0:T(8,128)(2,1)S(1)}, bf16[64,640]{1,0:T(8,128)(2,1)S(1)}, u32[]{:S(2)}, u32[]{:S(2)}) collective-permute-start(bf16[64,640]{1,0:T(8,128)(2,1)S(1)} %get-tuple-element.53), channel_id=1, source_target_pairs={{0,6},{1,7},{2,4},{3,5},{4,2},{5,3},{6,0},{7,1},{8,14},{9,15},{10,... | collective-permute-start | bytes 245768 | tf_op jit(solution)/shard_map/ppermute | solution.py:228
  28.0 8.4 %collective-permute-start.13 = (bf16[64,640]{1,0:T(8,128)(2,1)S(1)}, bf16[64,640]{1,0:T(8,128)(2,1)S(1)}, u32[]{:S(2)}, u32[]{:S(2)}) collective-permute-start(bf16[64,640]{1,0:T(8,128)(2,1)S(1)} %get-tuple-element.57), channel_id=1, source_target_pairs={{0,6},{1,7},{2,4},{3,5},{4,2},{5,3},{6,0},{7,1},{8,14},{9,15},{10,... | collective-permute-start | bytes 245768 | tf_op jit(solution)/shard_map/ppermute | solution.py:228
  30.9 5.5 %collective-permute-start.14 = (bf16[64,640]{1,0:T(8,128)(2,1)S(1)}, bf16[64,640]{1,0:T(8,128)(2,1)S(1)}, u32[]{:S(2)}, u32[]{:S(2)}) collective-permute-start(bf16[64,640]{1,0:T(8,128)(2,1)S(1)} %get-tuple-element.58), channel_id=1, source_target_pairs={{0,4},{1,5},{2,6},{3,7},{4,0},{5,1},{6,2},{7,3},{8,12},{9,13},{10,... | collective-permute-start | bytes 245768 | tf_op jit(solution)/shard_map/ppermute | solution.py:228
  31.4 5.0 %collective-permute-start.15 = (bf16[64,640]{1,0:T(8,128)(2,1)S(1)}, bf16[64,640]{1,0:T(8,128)(2,1)S(1)}, u32[]{:S(2)}, u32[]{:S(2)}) collective-permute-start(bf16[64,640]{1,0:T(8,128)(2,1)S(1)} %get-tuple-element.59), channel_id=1, source_target_pairs={{0,2},{1,3},{2,0},{3,1},{4,6},{5,7},{6,4},{7,5},{8,10},{9,11},{10,... | collective-permute-start | bytes 245768 | tf_op jit(solution)/shard_map/ppermute | solution.py:228
  33.6 6.1 %collective-permute-start.12 = (bf16[64,640]{1,0:T(8,128)(2,1)S(1)}, bf16[64,640]{1,0:T(8,128)(2,1)S(1)}, u32[]{:S(2)}, u32[]{:S(2)}) collective-permute-start(bf16[64,640]{1,0:T(8,128)(2,1)S(1)} %combine.1), channel_id=1, source_target_pairs={{0,8},{1,9},{2,10},{3,11},{4,12},{5,13},{6,14},{7,15},{8,0},{9,1},... | collective-permute-start | bytes 245768 | tf_op jit(solution)/shard_map/ppermute | solution.py:228
  40.1 1.3 %collective-permute-start.16 = (bf16[32,512]{1,0:T(8,128)(2,1)S(1)}, bf16[32,512]{1,0:T(8,128)(2,1)S(1)}, u32[]{:S(2)}, u32[]{:S(2)}) collective-permute-start(bf16[32,512]{1,0:T(8,128)(2,1)S(1)} %get-tuple-element.61), channel_id=1, source_target_pairs={{0,1},{1,0},{2,3},{3,2},{4,5},{5,4},{6,7},{7,6},{8,9},{9,8},{10,11... | collective-permute-start | bytes 98312 | tf_op jit(solution)/shard_map/ppermute | solution.py:228
  41.4 6.5 %copy-start.4 = (s32[2,4]{1,0:T(2,128)S(1)}, s32[2,4]{1,0:T(2,128)}, u32[]{:S(2)}) copy-start(s32[2,4]{1,0:T(2,128)} %param.9) | copy-start | bytes 100
  44.3 11.5 %all-to-all-start = ((bf16[16,8,448]{2,1,0:T(8,128)(2,1)}), bf16[16,8,448]{2,1,0:T(8,128)(2,1)S(1)}, u32[]{:S(2)}, u32[]{:S(2)}) async-start(bf16[16,8,448]{2,1,0:T(8,128)(2,1)} %project.1), calls=%async_computation | async-start | bytes 262144 | tf_op jit(solution)/shard_map/all_to_all | solution.py:259

commit v4 on v3

--- a/solution.py
+++ b/solution.py
@@ -24,12 +24,12 @@
 def select_kernel(own_ref, got_ref, out_ref):
     core = lax.rem(lax.axis_index("ctx"), 2)
     rows = out_ref.shape[0] // 2
-    out_ref[:rows] = own_ref[core].reshape(rows, -1)
+    out_ref[:rows] = own_ref[...].reshape(rows, -1)
     out_ref[rows:] = got_ref[core].reshape(rows, -1)
 
 
 def select(own, got):
-    requests, spec, heads, feature = own.shape
+    spec, heads, feature = own.shape
     return pl.pallas_call(
         select_kernel,
         out_shape=jax.ShapeDtypeStruct((2 * spec * heads, feature), own.dtype),
@@ -164,7 +164,7 @@
     )(*parts)
 
 
-def project_kernel(heads, group, own_ref, got_ref, up_ref, weight_ref, out_ref):
+def project_kernel(heads, group, own_ref, got_ref, up_ref, weight_ref, out_ref, sums_ref):
     core = lax.rem(lax.axis_index("ctx"), 2)
     own, got = own_ref[...], got_ref[...]
     first = jnp.where(core == 0, own, got)
@@ -184,8 +184,8 @@
         part = weight_ref[:, i * columns : (i + group) * columns]
         tile = jnp.dot(values, part, preferred_element_type=jnp.float32)
         for j in range(group):
-            piece = tile[:, j * columns : (j + 1) * columns]
-            out_ref[i + j] = piece.astype(out_ref.dtype)
+            sums_ref[i + j] = tile[:, j * columns : (j + 1) * columns]
+    out_ref[...] = sums_ref[...].astype(out_ref.dtype)
 
 
 def project(own, got, value_up, weight, spec, owners):
@@ -197,6 +197,7 @@
         out_shape=jax.ShapeDtypeStruct((owners, 2 * spec, columns), jnp.bfloat16),
         in_specs=[pl.BlockSpec(memory_space=pltpu.VMEM)] * 4,
         out_specs=pl.BlockSpec(memory_space=pltpu.VMEM),
+        scratch_shapes=[pltpu.VMEM((owners, 2 * spec, columns), jnp.float32)],
         compiler_params=pltpu.CompilerParams(vmem_limit_bytes=12 * MIB),
         name="project",
     )(own, got, value_up, weight)
@@ -229,7 +230,9 @@
 
     chunk = requests * spec * heads
     got = swap(queries, 1)
-    mine = select(queries, got)
+    own_queries = lax.dynamic_index_in_dim(queries, core, 0, keepdims=False)
+    own_queries, got = lax.optimization_barrier((own_queries, got))
+    mine = select(own_queries, got)
     own_keys = jnp.swapaxes(latent_cache, 1, 2)
     got_keys = swap(lax.optimization_barrier((own_keys, got))[0], 1)
 

time: 56.8 us -> 54.2 us (0.954)
  local copies, waits for them, and re-layouts: 2.95 us -> 1.33 us
  waiting for transfers between devices: 16.5 us -> 15.7 us
    squeeze x1, local copies, waits for them, and re-layouts: 1.82 us -> 0.16 us  [on_device(): lax.dynamic_index_in_dim(got_keys, core, 0, keepdims=False)]
    squeeze x0 -> x1, local copies, waits for them, and re-layouts: none -> 0.93 us  [on_device(): own_queries = lax.dynamic_index_in_dim(queries, core, 0, keepdims=False)]
    unnamed x12 -> x10, local copies, waits for them, and re-layouts: 0.91 us -> 0.02 us
    ppermute x17, waiting for transfers between devices: 8.65 us -> 7.9 us  [swap(): return lax.ppermute(x, 'ctx', [(i, i ^ bits) for i in range(n)])]
  transfers between devices with their start and end apart: 18 -> 18, of which waited for: 6 -> 8; matrix products, arithmetic and copies ran while one was open for 3% -> 2% of each run, Pallas kernels for 7% -> 7%
where the time goes in v4:
time: 54.2 us; the launch traced here: 54 us
  starting transfers between devices  25.7 us (47%)
  waiting for transfers between devices  15.7 us (29%)
  Pallas kernels  11.1 us (20%)
  local copies, waits for them, and re-layouts  1.33 us (2%)
    ppermute x17, starting transfers between devices, swap(): return lax.ppermute(x, 'ctx', [(i, i ^ bits) for i in range(n)])  22.1 us
    ppermute x17, waiting for transfers between devices, swap(): return lax.ppermute(x, 'ctx', [(i, i ^ bits) for i in range(n)])  7.9 us
    all_to_all x1, waiting for transfers between devices, on_device(): received = lax.all_to_all(outs, 'ctx', 0, 0, tiled=True)  7.83 us
    pallas_call x2, Pallas kernels, attend(): pl.pallas_call(functools.partial(attend_kernel, chunks, spec, heads, late...  6.88 us
    all_to_all x1, starting transfers between devices, on_device(): received = lax.all_to_all(outs, 'ctx', 0, 0, tiled=True)  3.55 us
    pallas_call x1, Pallas kernels, project(): pl.pallas_call(functools.partial(project_kernel, heads, group), out_shape...  2.94 us
  transfers between devices with their start and end apart: 18, of which 8 were waited for; matrix products, arithmetic and copies ran while one was open for 2% of the time, Pallas kernels for 7%

profile of v4, /device:TPU:0, one launch (start us, length us, event | category | flops | bytes accessed | tf_op | source)
XLA Modules:
  0.0 54.0 jit_solution(10239551552927733343)
XLA Ops:
  0.0 0.5 collective-permute-start
  0.5 0.9 %dynamic-slice_bitcast_fusion.1.own_ref = bf16[4,8,576]{2,1,0:T(8,128)(2,1)S(1)} fusion(bf16[2,4,8,576]{3,2,1,0:T(8,128)(2,1)} %param.6, s32[]{:T(128)S(6)} %select_n.6), kind=kLoop, calls=%fused_computation.1 | loop fusion | bytes 73732 | tf_op jit(solution)/shard_map/jit(dynamic_index_in_dim)/squeeze | solution.py:233
  1.4 0.2 collective-permute-done.got_ref
  1.6 0.4 collective-permute-start.5
  2.0 3.8 %collective-permute-start.3 = (bf16[64,576]{1,0:T(8,128)(2,1)S(1)}, bf16[64,576]{1,0:T(8,128)(2,1)S(1)}, u32[]{:S(2)}, u32[]{:S(2)}) collective-permute-start(bf16[64,576]{1,0:T(8,128)(2,1)S(1)} %select.3.refs_0_), channel_id=1, source_target_pairs={{0,8},{1,9},{2,10},{3,11},{4,12},{5,13},{6,14},{7,15},{8,0},{9,1},... | collective-permute-start | bytes 221192 | tf_op jit(solution)/shard_map/ppermute | solution.py:229
  5.8 1.5 %collective-permute-start.4 = (bf16[64,576]{1,0:T(8,128)(2,1)S(1)}, bf16[64,576]{1,0:T(8,128)(2,1)S(1)}, u32[]{:S(2)}, u32[]{:S(2)}) collective-permute-start(bf16[64,576]{1,0:T(8,128)(2,1)S(1)} %select.3.refs_0_), channel_id=1, source_target_pairs={{0,2},{1,3},{2,0},{3,1},{4,6},{5,7},{6,4},{7,5},{8,10},{9,11},{10,... | collective-permute-start | bytes 221192 | tf_op jit(solution)/shard_map/ppermute | solution.py:229
  7.3 1.5 %collective-permute-start.1 = (bf16[64,576]{1,0:T(8,128)(2,1)S(1)}, bf16[64,576]{1,0:T(8,128)(2,1)S(1)}, u32[]{:S(2)}, u32[]{:S(2)}) collective-permute-start(bf16[64,576]{1,0:T(8,128)(2,1)S(1)} %select.3.refs_0_), channel_id=1, source_target_pairs={{0,6},{1,7},{2,4},{3,5},{4,2},{5,3},{6,0},{7,1},{8,14},{9,15},{10,... | collective-permute-start | bytes 221192 | tf_op jit(solution)/shard_map/ppermute | solution.py:229
  8.8 0.4 collective-permute-start.2
  9.3 1.3 %collective-permute-done.3.refs_0_ = bf16[64,576]{1,0:T(8,128)(2,1)S(1)} collective-permute-done((bf16[64,576]{1,0:T(8,128)(2,1)S(1)}, bf16[64,576]{1,0:T(8,128)(2,1)S(1)}, u32[]{:S(2)}, u32[]{:S(2)}) %collective-permute-start.3) | collective-permute-done | bytes 73760 | tf_op jit(solution)/shard_map/ppermute | solution.py:229
  10.6 3.4 %collective-permute-start.6 = (bf16[64,576]{1,0:T(8,128)(2,1)S(1)}, bf16[64,576]{1,0:T(8,128)(2,1)S(1)}, u32[]{:S(2)}, u32[]{:S(2)}) collective-permute-start(bf16[64,576]{1,0:T(8,128)(2,1)S(1)} %collective-permute-done.3.refs_0_), channel_id=1, source_target_pairs={{0,6},{1,7},{2,4},{3,5},{4,2},{5,3},{6,0},{7,1},{8,14},{9,15},{10,... | collective-permute-start | bytes 221192 | tf_op jit(solution)/shard_map/ppermute | solution.py:229
  13.9 0.4 collective-permute-start.7
  14.5 0.2 dynamic-slice_bitcast_fusion.refs_5_
  14.8 3.4 %attend.2 = (bf16[64,640]{1,0:T(8,128)(2,1)S(1)}, bf16[64,640]{1,0:T(8,128)(2,1)S(1)}, bf16[64,640]{1,0:T(8,128)(2,1)S(1)}, bf16[64,640]{1,0:T(8,128)(2,1)S(1)}) custom-call(s32[2,128]{1,0:T(2,128)S(1)} %broadcast_in_dim.6.lengths_ref, bf16[64,576]{1,0:T(8,128)(2,1)S(1)} %select.3.refs_0_, bf16[64,576]{1,0:T(8,128)(2,1)S(1)} %collective-permute-done.1.refs_1_, ...), custom_call_target="tpu_custom_call" | custom-call | flops 2281701376 | bytes 4718592 | tf_op jit(solution)/shard_map/attend/pallas_call | solution.py:97
  18.2 0.1 collective-permute-done.7.refs_2_
  18.4 0.5 collective-permute-done.8.refs_3_
  18.8 3.4 %attend.3 = (bf16[64,640]{1,0:T(8,128)(2,1)S(1)}, bf16[64,640]{1,0:T(8,128)(2,1)S(1)}, bf16[64,640]{1,0:T(8,128)(2,1)S(1)}, bf16[64,640]{1,0:T(8,128)(2,1)S(1)}) custom-call(s32[2,128]{1,0:T(2,128)S(1)} %broadcast_in_dim.6.lengths_ref, bf16[64,576]{1,0:T(8,128)(2,1)S(1)} %collective-permute-done.3.refs_0_, ...), custom_call_target="tpu_custom_call" | custom-call | flops 2281701376 | bytes 4718592 | tf_op jit(solution)/shard_map/attend/pallas_call | solution.py:97
  22.3 1.6 %collective-permute-start.10 = (bf16[64,640]{1,0:T(8,128)(2,1)S(1)}, bf16[64,640]{1,0:T(8,128)(2,1)S(1)}, u32[]{:S(2)}, u32[]{:S(2)}) collective-permute-start(bf16[64,640]{1,0:T(8,128)(2,1)S(1)} %get-tuple-element.58), channel_id=1, source_target_pairs={{0,4},{1,5},{2,6},{3,7},{4,0},{5,1},{6,2},{7,3},{8,12},{9,13},{10,... | collective-permute-start | bytes 245768 | tf_op jit(solution)/shard_map/ppermute | solution.py:229
  23.9 1.4 %collective-permute-start.11 = (bf16[64,640]{1,0:T(8,128)(2,1)S(1)}, bf16[64,640]{1,0:T(8,128)(2,1)S(1)}, u32[]{:S(2)}, u32[]{:S(2)}) collective-permute-start(bf16[64,640]{1,0:T(8,128)(2,1)S(1)} %get-tuple-element.59), channel_id=1, source_target_pairs={{0,2},{1,3},{2,0},{3,1},{4,6},{5,7},{6,4},{7,5},{8,10},{9,11},{10,... | collective-permute-start | bytes 245768 | tf_op jit(solution)/shard_map/ppermute | solution.py:229
  25.3 0.6 %collective-permute-start.9 = (bf16[64,640]{1,0:T(8,128)(2,1)S(1)}, bf16[64,640]{1,0:T(8,128)(2,1)S(1)}, u32[]{:S(2)}, u32[]{:S(2)}) collective-permute-start(bf16[64,640]{1,0:T(8,128)(2,1)S(1)} %get-tuple-element.57), channel_id=1, source_target_pairs={{0,6},{1,7},{2,4},{3,5},{4,2},{5,3},{6,0},{7,1},{8,14},{9,15},{10,... | collective-permute-start | bytes 245768 | tf_op jit(solution)/shard_map/ppermute | solution.py:229
  25.8 2.4 %collective-permute-start.13 = (bf16[64,640]{1,0:T(8,128)(2,1)S(1)}, bf16[64,640]{1,0:T(8,128)(2,1)S(1)}, u32[]{:S(2)}, u32[]{:S(2)}) collective-permute-start(bf16[64,640]{1,0:T(8,128)(2,1)S(1)} %get-tuple-element.61), channel_id=1, source_target_pairs={{0,6},{1,7},{2,4},{3,5},{4,2},{5,3},{6,0},{7,1},{8,14},{9,15},{10,... | collective-permute-start | bytes 245768 | tf_op jit(solution)/shard_map/ppermute | solution.py:229
  28.2 0.4 collective-permute-start.14
  28.7 0.7 %collective-permute-start.15 = (bf16[64,640]{1,0:T(8,128)(2,1)S(1)}, bf16[64,640]{1,0:T(8,128)(2,1)S(1)}, u32[]{:S(2)}, u32[]{:S(2)}) collective-permute-start(bf16[64,640]{1,0:T(8,128)(2,1)S(1)} %get-tuple-element.63), channel_id=1, source_target_pairs={{0,2},{1,3},{2,0},{3,1},{4,6},{5,7},{6,4},{7,5},{8,10},{9,11},{10,... | collective-permute-start | bytes 245768 | tf_op jit(solution)/shard_map/ppermute | solution.py:229
  29.4 1.2 %collective-permute-done.9.refs_1_ = bf16[64,640]{1,0:T(8,128)(2,1)S(1)} collective-permute-done((bf16[64,640]{1,0:T(8,128)(2,1)S(1)}, bf16[64,640]{1,0:T(8,128)(2,1)S(1)}, u32[]{:S(2)}, u32[]{:S(2)}) %collective-permute-start.9) | collective-permute-done | bytes 81952 | tf_op jit(solution)/shard_map/ppermute | solution.py:229
  30.6 0.3 combine.1
  30.9 3.0 %collective-permute-start.12 = (bf16[64,640]{1,0:T(8,128)(2,1)S(1)}, bf16[64,640]{1,0:T(8,128)(2,1)S(1)}, u32[]{:S(2)}, u32[]{:S(2)}) collective-permute-start(bf16[64,640]{1,0:T(8,128)(2,1)S(1)} %combine.1), channel_id=1, source_target_pairs={{0,8},{1,9},{2,10},{3,11},{4,12},{5,13},{6,14},{7,15},{8,0},{9,1},... | collective-permute-start | bytes 245768 | tf_op jit(solution)/shard_map/ppermute | solution.py:229
  33.9 3.3 %collective-permute-done.12.refs_0_ = bf16[64,640]{1,0:T(8,128)(2,1)S(1)} collective-permute-done((bf16[64,640]{1,0:T(8,128)(2,1)S(1)}, bf16[64,640]{1,0:T(8,128)(2,1)S(1)}, u32[]{:S(2)}, u32[]{:S(2)}) %collective-permute-start.12) | collective-permute-done | bytes 81952 | tf_op jit(solution)/shard_map/ppermute | solution.py:229
  37.2 0.3 merge.1
  37.6 1.2 %collective-permute-done.16.got_ref = bf16[32,512]{1,0:T(8,128)(2,1)S(1)} collective-permute-done((bf16[32,512]{1,0:T(8,128)(2,1)S(1)}, bf16[32,512]{1,0:T(8,128)(2,1)S(1)}, u32[]{:S(2)}, u32[]{:S(2)}) %collective-permute-start.16) | collective-permute-done | bytes 32800 | tf_op jit(solution)/shard_map/ppermute | solution.py:229
  38.8 2.9 %project.1 = bf16[16,8,448]{2,1,0:T(8,128)(2,1)} custom-call(bf16[32,512]{1,0:T(8,128)(2,1)S(1)} %get-tuple-element.64.own_ref, bf16[32,512]{1,0:T(8,128)(2,1)S(1)} %collective-permute-done.16.got_ref, bf16[8,512,128]{2,1,0:T(8,128)(2,1)S(1)} %copy-done.1, bf16[1024,7168]{1,0:T(8,128)(2,1)S(1)} %copy-done), custom_call_target="tpu_custom_call" | custom-call | tf_op jit(solution)/shard_map/project/pallas_call | solution.py:195
  41.7 3.6 %all-to-all-start = ((bf16[16,8,448]{2,1,0:T(8,128)(2,1)}), bf16[16,8,448]{2,1,0:T(8,128)(2,1)S(1)}, u32[]{:S(2)}, u32[]{:S(2)}) async-start(bf16[16,8,448]{2,1,0:T(8,128)(2,1)} %project.1), calls=%async_computation | async-start | bytes 262144 | tf_op jit(solution)/shard_map/all_to_all | solution.py:262
  45.4 7.8 %all-to-all-done.in_ref = bf16[16,8,448]{2,1,0:T(8,128)(2,1)S(1)} async-done(((bf16[16,8,448]{2,1,0:T(8,128)(2,1)}), bf16[16,8,448]{2,1,0:T(8,128)(2,1)S(1)}, u32[]{:S(2)}, u32[]{:S(2)}) %all-to-all-start) | async-done | bytes 114720 | tf_op jit(solution)/shard_map/all_to_all | solution.py:262
  53.3 0.7 %finish.1 = bf16[2,4,448]{2,1,0:T(4,128)(2,1)} custom-call(bf16[16,8,448]{2,1,0:T(8,128)(2,1)S(1)} %all-to-all-done.in_ref, f32[8,128]{1,0:T(8,128)S(1)} %broadcast_in_dim.15.keep_ref), custom_call_target="tpu_custom_call" | custom-call | tf_op jit(solution)/shard_map/finish/pallas_call | solution.py:215
  (27 shorter events, 0.5 us)
Async XLA Ops:
  0.0 14.7 %copy-start.4 = (s32[2]{0:T(128)S(1)}, s32[2]{0:T(128)}, u32[]{:S(2)}) copy-start(s32[2]{0:T(128)} %param.8) | copy-start | bytes 28
  0.0 1.6 %collective-permute-start = (bf16[2,4,8,576]{3,2,1,0:T(8,128)(2,1)}, bf16[2,4,8,576]{3,2,1,0:T(8,128)(2,1)S(1)}, u32[]{:S(2)}, u32[]{:S(2)}) collective-permute-start(bf16[2,4,8,576]{3,2,1,0:T(8,128)(2,1)} %param.6), channel_id=1, source_target_pairs={{0,1},{1,0},{2,3},{3,2},{4,5},{5,4},{6,7},{7,6},{8,9},{9,8},{10,11... | collective-permute-start | bytes 221192 | tf_op jit(solution)/shard_map/ppermute | solution.py:229
  0.5 14.3 %copy-start.2 = (bf16[2,2048,576]{1,2,0:T(8,128)(2,1)S(1)}, bf16[2,2048,576]{1,2,0:T(8,128)(2,1)}, u32[]{:S(2)}) copy-start(bf16[2,2048,576]{1,2,0:T(8,128)(2,1)} %param.7) | copy-start | bytes 14155780
  1.6 12.8 %collective-permute-start.5 = (bf16[2,576,2048]{2,1,0:T(8,128)(2,1)}, bf16[2,576,2048]{2,1,0:T(8,128)(2,1)S(1)}, u32[]{:S(2)}, u32[]{:S(2)}) collective-permute-start(bf16[2,576,2048]{2,1,0:T(8,128)(2,1)} %bitcast.5), channel_id=1, source_target_pairs={{0,1},{1,0},{2,3},{3,2},{4,5},{5,4},{6,7},{7,6},{8,9},{9,8},{10,11... | collective-permute-start | bytes 14155784 | tf_op jit(solution)/shard_map/ppermute | solution.py:229
  2.0 8.6 %collective-permute-start.3 = (bf16[64,576]{1,0:T(8,128)(2,1)S(1)}, bf16[64,576]{1,0:T(8,128)(2,1)S(1)}, u32[]{:S(2)}, u32[]{:S(2)}) collective-permute-start(bf16[64,576]{1,0:T(8,128)(2,1)S(1)} %select.3.refs_0_), channel_id=1, source_target_pairs={{0,8},{1,9},{2,10},{3,11},{4,12},{5,13},{6,14},{7,15},{8,0},{9,1},... | collective-permute-start | bytes 221192 | tf_op jit(solution)/shard_map/ppermute | solution.py:229
  5.8 4.8 %collective-permute-start.4 = (bf16[64,576]{1,0:T(8,128)(2,1)S(1)}, bf16[64,576]{1,0:T(8,128)(2,1)S(1)}, u32[]{:S(2)}, u32[]{:S(2)}) collective-permute-start(bf16[64,576]{1,0:T(8,128)(2,1)S(1)} %select.3.refs_0_), channel_id=1, source_target_pairs={{0,2},{1,3},{2,0},{3,1},{4,6},{5,7},{6,4},{7,5},{8,10},{9,11},{10,... | collective-permute-start | bytes 221192 | tf_op jit(solution)/shard_map/ppermute | solution.py:229
  7.3 7.4 %collective-permute-start.1 = (bf16[64,576]{1,0:T(8,128)(2,1)S(1)}, bf16[64,576]{1,0:T(8,128)(2,1)S(1)}, u32[]{:S(2)}, u32[]{:S(2)}) collective-permute-start(bf16[64,576]{1,0:T(8,128)(2,1)S(1)} %select.3.refs_0_), channel_id=1, source_target_pairs={{0,6},{1,7},{2,4},{3,5},{4,2},{5,3},{6,0},{7,1},{8,14},{9,15},{10,... | collective-permute-start | bytes 221192 | tf_op jit(solution)/shard_map/ppermute | solution.py:229
  8.8 5.9 %collective-permute-start.2 = (bf16[64,576]{1,0:T(8,128)(2,1)S(1)}, bf16[64,576]{1,0:T(8,128)(2,1)S(1)}, u32[]{:S(2)}, u32[]{:S(2)}) collective-permute-start(bf16[64,576]{1,0:T(8,128)(2,1)S(1)} %select.3.refs_0_), channel_id=1, source_target_pairs={{0,4},{1,5},{2,6},{3,7},{4,0},{5,1},{6,2},{7,3},{8,12},{9,13},{10,... | collective-permute-start | bytes 221192 | tf_op jit(solution)/shard_map/ppermute | solution.py:229
  10.6 7.6 %collective-permute-start.6 = (bf16[64,576]{1,0:T(8,128)(2,1)S(1)}, bf16[64,576]{1,0:T(8,128)(2,1)S(1)}, u32[]{:S(2)}, u32[]{:S(2)}) collective-permute-start(bf16[64,576]{1,0:T(8,128)(2,1)S(1)} %collective-permute-done.3.refs_0_), channel_id=1, source_target_pairs={{0,6},{1,7},{2,4},{3,5},{4,2},{5,3},{6,0},{7,1},{8,14},{9,15},{10,... | collective-permute-start | bytes 221192 | tf_op jit(solution)/shard_map/ppermute | solution.py:229
  13.9 4.4 %collective-permute-start.7 = (bf16[64,576]{1,0:T(8,128)(2,1)S(1)}, bf16[64,576]{1,0:T(8,128)(2,1)S(1)}, u32[]{:S(2)}, u32[]{:S(2)}) collective-permute-start(bf16[64,576]{1,0:T(8,128)(2,1)S(1)} %collective-permute-done.3.refs_0_), channel_id=1, source_target_pairs={{0,4},{1,5},{2,6},{3,7},{4,0},{5,1},{6,2},{7,3},{8,12},{9,13},{10,... | collective-permute-start | bytes 221192 | tf_op jit(solution)/shard_map/ppermute | solution.py:229
  14.4 4.4 %collective-permute-start.8 = (bf16[64,576]{1,0:T(8,128)(2,1)S(1)}, bf16[64,576]{1,0:T(8,128)(2,1)S(1)}, u32[]{:S(2)}, u32[]{:S(2)}) collective-permute-start(bf16[64,576]{1,0:T(8,128)(2,1)S(1)} %collective-permute-done.3.refs_0_), channel_id=1, source_target_pairs={{0,2},{1,3},{2,0},{3,1},{4,6},{5,7},{6,4},{7,5},{8,10},{9,11},{10,... | collective-permute-start | bytes 221192 | tf_op jit(solution)/shard_map/ppermute | solution.py:229
  14.8 24.0 %copy-start = (bf16[1024,7168]{1,0:T(8,128)(2,1)S(1)}, bf16[1024,7168]{1,0:T(8,128)(2,1)}, u32[]{:S(2)}) copy-start(bf16[1024,7168]{1,0:T(8,128)(2,1)} %weight_ref.1) | copy-start | bytes 44040196
  18.2 20.6 %copy-start.1 = (bf16[8,512,128]{2,1,0:T(8,128)(2,1)S(1)}, bf16[8,512,128]{2,1,0:T(8,128)(2,1)}, u32[]{:S(2)}) copy-start(bf16[8,512,128]{2,1,0:T(8,128)(2,1)} %up_ref.1) | copy-start | bytes 3145732
  22.3 6.4 %collective-permute-start.10 = (bf16[64,640]{1,0:T(8,128)(2,1)S(1)}, bf16[64,640]{1,0:T(8,128)(2,1)S(1)}, u32[]{:S(2)}, u32[]{:S(2)}) collective-permute-start(bf16[64,640]{1,0:T(8,128)(2,1)S(1)} %get-tuple-element.58), channel_id=1, source_target_pairs={{0,4},{1,5},{2,6},{3,7},{4,0},{5,1},{6,2},{7,3},{8,12},{9,13},{10,... | collective-permute-start | bytes 245768 | tf_op jit(solution)/shard_map/ppermute | solution.py:229
  23.9 5.5 %collective-permute-start.11 = (bf16[64,640]{1,0:T(8,128)(2,1)S(1)}, bf16[64,640]{1,0:T(8,128)(2,1)S(1)}, u32[]{:S(2)}, u32[]{:S(2)}) collective-permute-start(bf16[64,640]{1,0:T(8,128)(2,1)S(1)} %get-tuple-element.59), channel_id=1, source_target_pairs={{0,2},{1,3},{2,0},{3,1},{4,6},{5,7},{6,4},{7,5},{8,10},{9,11},{10,... | collective-permute-start | bytes 245768 | tf_op jit(solution)/shard_map/ppermute | solution.py:229
  25.3 5.3 %collective-permute-start.9 = (bf16[64,640]{1,0:T(8,128)(2,1)S(1)}, bf16[64,640]{1,0:T(8,128)(2,1)S(1)}, u32[]{:S(2)}, u32[]{:S(2)}) collective-permute-start(bf16[64,640]{1,0:T(8,128)(2,1)S(1)} %get-tuple-element.57), channel_id=1, source_target_pairs={{0,6},{1,7},{2,4},{3,5},{4,2},{5,3},{6,0},{7,1},{8,14},{9,15},{10,... | collective-permute-start | bytes 245768 | tf_op jit(solution)/shard_map/ppermute | solution.py:229
  25.8 8.1 %collective-permute-start.13 = (bf16[64,640]{1,0:T(8,128)(2,1)S(1)}, bf16[64,640]{1,0:T(8,128)(2,1)S(1)}, u32[]{:S(2)}, u32[]{:S(2)}) collective-permute-start(bf16[64,640]{1,0:T(8,128)(2,1)S(1)} %get-tuple-element.61), channel_id=1, source_target_pairs={{0,6},{1,7},{2,4},{3,5},{4,2},{5,3},{6,0},{7,1},{8,14},{9,15},{10,... | collective-permute-start | bytes 245768 | tf_op jit(solution)/shard_map/ppermute | solution.py:229
  28.2 5.7 %collective-permute-start.14 = (bf16[64,640]{1,0:T(8,128)(2,1)S(1)}, bf16[64,640]{1,0:T(8,128)(2,1)S(1)}, u32[]{:S(2)}, u32[]{:S(2)}) collective-permute-start(bf16[64,640]{1,0:T(8,128)(2,1)S(1)} %get-tuple-element.62), channel_id=1, source_target_pairs={{0,4},{1,5},{2,6},{3,7},{4,0},{5,1},{6,2},{7,3},{8,12},{9,13},{10,... | collective-permute-start | bytes 245768 | tf_op jit(solution)/shard_map/ppermute | solution.py:229
  28.7 5.3 %collective-permute-start.15 = (bf16[64,640]{1,0:T(8,128)(2,1)S(1)}, bf16[64,640]{1,0:T(8,128)(2,1)S(1)}, u32[]{:S(2)}, u32[]{:S(2)}) collective-permute-start(bf16[64,640]{1,0:T(8,128)(2,1)S(1)} %get-tuple-element.63), channel_id=1, source_target_pairs={{0,2},{1,3},{2,0},{3,1},{4,6},{5,7},{6,4},{7,5},{8,10},{9,11},{10,... | collective-permute-start | bytes 245768 | tf_op jit(solution)/shard_map/ppermute | solution.py:229
  30.9 6.3 %collective-permute-start.12 = (bf16[64,640]{1,0:T(8,128)(2,1)S(1)}, bf16[64,640]{1,0:T(8,128)(2,1)S(1)}, u32[]{:S(2)}, u32[]{:S(2)}) collective-permute-start(bf16[64,640]{1,0:T(8,128)(2,1)S(1)} %combine.1), channel_id=1, source_target_pairs={{0,8},{1,9},{2,10},{3,11},{4,12},{5,13},{6,14},{7,15},{8,0},{9,1},... | collective-permute-start | bytes 245768 | tf_op jit(solution)/shard_map/ppermute | solution.py:229
  37.5 1.3 %collective-permute-start.16 = (bf16[32,512]{1,0:T(8,128)(2,1)S(1)}, bf16[32,512]{1,0:T(8,128)(2,1)S(1)}, u32[]{:S(2)}, u32[]{:S(2)}) collective-permute-start(bf16[32,512]{1,0:T(8,128)(2,1)S(1)} %get-tuple-element.65), channel_id=1, source_target_pairs={{0,1},{1,0},{2,3},{3,2},{4,5},{5,4},{6,7},{7,6},{8,9},{9,8},{10,11... | collective-permute-start | bytes 98312 | tf_op jit(solution)/shard_map/ppermute | solution.py:229
  38.8 6.5 %copy-start.3 = (s32[2,4]{1,0:T(2,128)S(1)}, s32[2,4]{1,0:T(2,128)}, u32[]{:S(2)}) copy-start(s32[2,4]{1,0:T(2,128)} %param.9) | copy-start | bytes 100
  41.7 11.5 %all-to-all-start = ((bf16[16,8,448]{2,1,0:T(8,128)(2,1)}), bf16[16,8,448]{2,1,0:T(8,128)(2,1)S(1)}, u32[]{:S(2)}, u32[]{:S(2)}) async-start(bf16[16,8,448]{2,1,0:T(8,128)(2,1)} %project.1), calls=%async_computation | async-start | bytes 262144 | tf_op jit(solution)/shard_map/all_to_all | solution.py:262

commit v5 on v4

--- a/solution.py
+++ b/solution.py
@@ -39,7 +39,7 @@
     )(own, got)
 
 
-def attend_kernel(chunks, spec, heads, latent, lengths_ref, *refs):
+def attend_kernel(chunks, spec, heads, latent, lengths_ref, mask_ref, *refs):
     q_refs, key_refs, out_refs = refs[:chunks], refs[chunks : chunks + 2], refs[chunks + 2 :]
     block = key_refs[1].shape[1]
     width = min(block, 512)
@@ -84,13 +84,15 @@
             preferred_element_type=jnp.float32,
         )
         peak, tile = higher, following
+    mask = mask_ref[pl.ds(lax.rem(me, 2), 1), :].astype(jnp.float32)
+    numerator *= sum(jnp.where(draft == j, mask[:, j : j + 1], 0.0) for j in range(spec))
     chunk = rows // chunks
     for i, out_ref in enumerate(out_refs):
         part = slice(i * chunk, (i + 1) * chunk)
         store_part(out_ref, latent, peak[part], denominator[part], numerator[part])
 
 
-def attend(lengths, query_chunks, keys, spec, heads, latent):
+def attend(lengths, mask, query_chunks, keys, spec, heads, latent):
     chunks = len(query_chunks)
     chunk, feature = query_chunks[0].shape
     rows, positions = chunks * chunk, 2 * keys[1].shape[1]
@@ -104,7 +106,7 @@
             transcendentals=rows * positions,
         ),
         name="attend",
-    )(lengths, *query_chunks, *keys)
+    )(lengths, mask, *query_chunks, *keys)
 
 
 def merged(in_refs, latent):
@@ -164,7 +166,7 @@
     )(*parts)
 
 
-def project_kernel(heads, group, own_ref, got_ref, up_ref, weight_ref, out_ref, sums_ref):
+def project_kernel(heads, group, own_ref, got_ref, up_ref, weight_ref, out_ref):
     core = lax.rem(lax.axis_index("ctx"), 2)
     own, got = own_ref[...], got_ref[...]
     first = jnp.where(core == 0, own, got)
@@ -184,8 +186,8 @@
         part = weight_ref[:, i * columns : (i + group) * columns]
         tile = jnp.dot(values, part, preferred_element_type=jnp.float32)
         for j in range(group):
-            sums_ref[i + j] = tile[:, j * columns : (j + 1) * columns]
-    out_ref[...] = sums_ref[...].astype(out_ref.dtype)
+            piece = tile[:, j * columns : (j + 1) * columns]
+            out_ref[i + j] = piece.astype(out_ref.dtype)
 
 
 def project(own, got, value_up, weight, spec, owners):
@@ -197,27 +199,26 @@
         out_shape=jax.ShapeDtypeStruct((owners, 2 * spec, columns), jnp.bfloat16),
         in_specs=[pl.BlockSpec(memory_space=pltpu.VMEM)] * 4,
         out_specs=pl.BlockSpec(memory_space=pltpu.VMEM),
-        scratch_shapes=[pltpu.VMEM((owners, 2 * spec, columns), jnp.float32)],
         compiler_params=pltpu.CompilerParams(vmem_limit_bytes=12 * MIB),
         name="project",
     )(own, got, value_up, weight)
 
 
-def finish_kernel(in_ref, keep_ref, out_ref):
-    total = jnp.sum(in_ref[...].astype(jnp.float32), axis=0) * keep_ref[:, :1]
+def finish_kernel(in_ref, out_ref):
+    total = jnp.sum(in_ref[...].astype(jnp.float32), axis=0)
     spec = out_ref.shape[1]
     for r in range(out_ref.shape[0]):
         out_ref[r] = total[r * spec : (r + 1) * spec].astype(out_ref.dtype)
 
 
-def finish(parts, keep, requests):
+def finish(parts, requests):
     _, rows, columns = parts.shape
     return pl.pallas_call(
         finish_kernel,
         out_shape=jax.ShapeDtypeStruct((requests, rows // requests, columns), jnp.bfloat16),
         compiler_params=pltpu.CompilerParams(vmem_limit_bytes=8 * MIB),
         name="finish",
-    )(parts, keep)
+    )(parts)
 
 
 def on_device(n, queries, latent_cache, lengths, draft_mask, value_up, output_weight):
@@ -241,16 +242,13 @@
     far = swap(mine, far_bit)
     near_queries = [swap(mine, bits) for bits in near]
 
-    draft_mask = lax.optimization_barrier((draft_mask, mine))[0]
     keys = [own_keys, lax.dynamic_index_in_dim(got_keys, core, 0, keepdims=False)]
     far, near_queries[2] = lax.optimization_barrier((far, near_queries[2]))
     far_queries = [swap(far, bits) for bits in near]
     spread = jnp.broadcast_to(lengths[:, None], (requests, STAT_LANES))
-    keep = draft_mask.astype(jnp.float32).reshape(requests * spec, 1)
-    keep = jnp.broadcast_to(keep, (requests * spec, STAT_LANES))
-    near_parts = attend(spread, [mine, *near_queries], keys, spec, heads, latent)
+    near_parts = attend(spread, draft_mask, [mine, *near_queries], keys, spec, heads, latent)
     near_parts, far_queries = lax.optimization_barrier((near_parts, far_queries))
-    far_parts = attend(spread, [far, *far_queries], keys, spec, heads, latent)
+    far_parts = attend(spread, draft_mask, [far, *far_queries], keys, spec, heads, latent)
     near_parts, far_parts = lax.optimization_barrier((near_parts, far_parts))
     far_part = combine(
         [far_parts[0]] + [swap(part, bits) for part, bits in zip(far_parts[1:], near)], latent
@@ -260,7 +258,7 @@
     own, give = merge(parts, latent)
     outs = project(own, swap(give, 1), value_up, output_weight, spec, n)
     received = lax.all_to_all(outs, "ctx", 0, 0, tiled=True)
-    return finish(received, keep, requests)
+    return finish(received, requests)
 
 
 def solution(mesh):

time: 54.2 us -> 53.1 us (0.980)
  blocking collectives: 0 us -> 11.3 us
  waiting for transfers between devices: 15.7 us -> 7.91 us
  starting transfers between devices: 25.7 us -> 22.2 us
  Pallas kernels: 11.1 us -> 10.2 us
    all_to_all x0 -> x1, blocking collectives: none -> 11.3 us  [on_device(): received = lax.all_to_all(outs, 'ctx', 0, 0, tiled=True)]
    all_to_all x1 -> x0, waiting for transfers between devices: 7.83 us -> none  [on_device(): received = lax.all_to_all(outs, 'ctx', 0, 0, tiled=True)]
    all_to_all x1 -> x0, starting transfers between devices: 3.55 us -> none  [on_device(): received = lax.all_to_all(outs, 'ctx', 0, 0, tiled=True)]
    pallas_call x1, Pallas kernels: 2.94 us -> 2.26 us  [project(): pl.pallas_call(functools.partial(project_kernel, heads, group), out_shape...]
  transfers between devices with their start and end apart: 18 -> 17, of which waited for: 8 -> 8; matrix products, arithmetic and copies ran while one was open for 2% -> 2% of each run, Pallas kernels for 7% -> 7%
where the time goes in v5:
time: 53.1 us; the launch traced here: 52.9 us
  starting transfers between devices  22.2 us (42%)
  blocking collectives  11.3 us (21%)
  Pallas kernels  10.2 us (19%)
  waiting for transfers between devices  7.91 us (15%)
  local copies, waits for them, and re-layouts  1.18 us (2%)
    ppermute x17, starting transfers between devices, swap(): return lax.ppermute(x, 'ctx', [(i, i ^ bits) for i in range(n)])  22.2 us
    all_to_all x1, blocking collectives, on_device(): received = lax.all_to_all(outs, 'ctx', 0, 0, tiled=True)  11.3 us
    ppermute x17, waiting for transfers between devices, swap(): return lax.ppermute(x, 'ctx', [(i, i ^ bits) for i in range(n)])  7.91 us
    pallas_call x2, Pallas kernels, attend(): pl.pallas_call(functools.partial(attend_kernel, chunks, spec, heads, late...  6.74 us
    pallas_call x1, Pallas kernels, project(): pl.pallas_call(functools.partial(project_kernel, heads, group), out_shape...  2.26 us
  transfers between devices with their start and end apart: 17, of which 8 were waited for; matrix products, arithmetic and copies ran while one was open for 2% of the time, Pallas kernels for 7%

profile of v5, /device:TPU:0, one launch (start us, length us, event | category | flops | bytes accessed | tf_op | source)
XLA Modules:
  0.0 52.9 jit_solution(14229813593987073498)
XLA Ops:
  0.0 0.5 collective-permute-start
  0.5 0.9 %dynamic-slice_bitcast_fusion.1.own_ref = bf16[4,8,576]{2,1,0:T(8,128)(2,1)S(1)} fusion(bf16[2,4,8,576]{3,2,1,0:T(8,128)(2,1)} %param.6, s32[]{:T(128)S(6)} %select_n.6), kind=kLoop, calls=%fused_computation.1 | loop fusion | bytes 73732 | tf_op jit(solution)/shard_map/jit(dynamic_index_in_dim)/squeeze | solution.py:234
  1.4 0.2 collective-permute-done.got_ref
  1.6 0.4 collective-permute-start.5
  2.0 3.8 %collective-permute-start.3 = (bf16[64,576]{1,0:T(8,128)(2,1)S(1)}, bf16[64,576]{1,0:T(8,128)(2,1)S(1)}, u32[]{:S(2)}, u32[]{:S(2)}) collective-permute-start(bf16[64,576]{1,0:T(8,128)(2,1)S(1)} %select.3.refs_0_), channel_id=1, source_target_pairs={{0,8},{1,9},{2,10},{3,11},{4,12},{5,13},{6,14},{7,15},{8,0},{9,1},... | collective-permute-start | bytes 221192 | tf_op jit(solution)/shard_map/ppermute | solution.py:230
  5.8 1.5 %collective-permute-start.4 = (bf16[64,576]{1,0:T(8,128)(2,1)S(1)}, bf16[64,576]{1,0:T(8,128)(2,1)S(1)}, u32[]{:S(2)}, u32[]{:S(2)}) collective-permute-start(bf16[64,576]{1,0:T(8,128)(2,1)S(1)} %select.3.refs_0_), channel_id=1, source_target_pairs={{0,2},{1,3},{2,0},{3,1},{4,6},{5,7},{6,4},{7,5},{8,10},{9,11},{10,... | collective-permute-start | bytes 221192 | tf_op jit(solution)/shard_map/ppermute | solution.py:230
  7.3 1.5 %collective-permute-start.1 = (bf16[64,576]{1,0:T(8,128)(2,1)S(1)}, bf16[64,576]{1,0:T(8,128)(2,1)S(1)}, u32[]{:S(2)}, u32[]{:S(2)}) collective-permute-start(bf16[64,576]{1,0:T(8,128)(2,1)S(1)} %select.3.refs_0_), channel_id=1, source_target_pairs={{0,6},{1,7},{2,4},{3,5},{4,2},{5,3},{6,0},{7,1},{8,14},{9,15},{10,... | collective-permute-start | bytes 221192 | tf_op jit(solution)/shard_map/ppermute | solution.py:230
  8.8 0.4 collective-permute-start.2
  9.3 1.3 %collective-permute-done.3.refs_0_ = bf16[64,576]{1,0:T(8,128)(2,1)S(1)} collective-permute-done((bf16[64,576]{1,0:T(8,128)(2,1)S(1)}, bf16[64,576]{1,0:T(8,128)(2,1)S(1)}, u32[]{:S(2)}, u32[]{:S(2)}) %collective-permute-start.3) | collective-permute-done | bytes 73760 | tf_op jit(solution)/shard_map/ppermute | solution.py:230
  10.6 3.4 %collective-permute-start.6 = (bf16[64,576]{1,0:T(8,128)(2,1)S(1)}, bf16[64,576]{1,0:T(8,128)(2,1)S(1)}, u32[]{:S(2)}, u32[]{:S(2)}) collective-permute-start(bf16[64,576]{1,0:T(8,128)(2,1)S(1)} %collective-permute-done.3.refs_0_), channel_id=1, source_target_pairs={{0,6},{1,7},{2,4},{3,5},{4,2},{5,3},{6,0},{7,1},{8,14},{9,15},{10,... | collective-permute-start | bytes 221192 | tf_op jit(solution)/shard_map/ppermute | solution.py:230
  13.9 0.4 collective-permute-start.7
  14.5 0.2 dynamic-slice_bitcast_fusion.refs_5_
  14.8 3.4 %attend.2 = (bf16[64,640]{1,0:T(8,128)(2,1)S(1)}, bf16[64,640]{1,0:T(8,128)(2,1)S(1)}, bf16[64,640]{1,0:T(8,128)(2,1)S(1)}, bf16[64,640]{1,0:T(8,128)(2,1)S(1)}) custom-call(s32[2,128]{1,0:T(2,128)S(1)} %broadcast_in_dim.2.lengths_ref, s32[2,4]{1,0:T(2,128)S(1)} %copy-done.3, bf16[64,576]{1,0:T(8,128)(2,1)S(1)} %select.3.refs_0_, ...), custom_call_target="tpu_custom_call" | custom-call | flops 2281701376 | bytes 4718592 | tf_op jit(solution)/shard_map/attend/pallas_call | solution.py:99
  18.2 0.2 collective-permute-done.7.refs_2_
  18.4 0.5 collective-permute-done.8.refs_3_
  18.8 3.4 %attend.3 = (bf16[64,640]{1,0:T(8,128)(2,1)S(1)}, bf16[64,640]{1,0:T(8,128)(2,1)S(1)}, bf16[64,640]{1,0:T(8,128)(2,1)S(1)}, bf16[64,640]{1,0:T(8,128)(2,1)S(1)}) custom-call(s32[2,128]{1,0:T(2,128)S(1)} %broadcast_in_dim.2.lengths_ref, s32[2,4]{1,0:T(2,128)S(1)} %copy-done.3, bf16[64,576]{1,0:T(8,128)(2,1)S(1)} %collective-permute-done.3.refs_0_, ...), custom_call_target="tpu_custom_call" | custom-call | flops 2281701376 | bytes 4718592 | tf_op jit(solution)/shard_map/attend/pallas_call | solution.py:99
  22.2 1.6 %collective-permute-start.10 = (bf16[64,640]{1,0:T(8,128)(2,1)S(1)}, bf16[64,640]{1,0:T(8,128)(2,1)S(1)}, u32[]{:S(2)}, u32[]{:S(2)}) collective-permute-start(bf16[64,640]{1,0:T(8,128)(2,1)S(1)} %get-tuple-element.57), channel_id=1, source_target_pairs={{0,4},{1,5},{2,6},{3,7},{4,0},{5,1},{6,2},{7,3},{8,12},{9,13},{10,... | collective-permute-start | bytes 245768 | tf_op jit(solution)/shard_map/ppermute | solution.py:230
  23.8 1.3 %collective-permute-start.11 = (bf16[64,640]{1,0:T(8,128)(2,1)S(1)}, bf16[64,640]{1,0:T(8,128)(2,1)S(1)}, u32[]{:S(2)}, u32[]{:S(2)}) collective-permute-start(bf16[64,640]{1,0:T(8,128)(2,1)S(1)} %get-tuple-element.58), channel_id=1, source_target_pairs={{0,2},{1,3},{2,0},{3,1},{4,6},{5,7},{6,4},{7,5},{8,10},{9,11},{10,... | collective-permute-start | bytes 245768 | tf_op jit(solution)/shard_map/ppermute | solution.py:230
  25.1 0.6 %collective-permute-start.9 = (bf16[64,640]{1,0:T(8,128)(2,1)S(1)}, bf16[64,640]{1,0:T(8,128)(2,1)S(1)}, u32[]{:S(2)}, u32[]{:S(2)}) collective-permute-start(bf16[64,640]{1,0:T(8,128)(2,1)S(1)} %get-tuple-element.56), channel_id=1, source_target_pairs={{0,6},{1,7},{2,4},{3,5},{4,2},{5,3},{6,0},{7,1},{8,14},{9,15},{10,... | collective-permute-start | bytes 245768 | tf_op jit(solution)/shard_map/ppermute | solution.py:230
  25.8 2.3 %collective-permute-start.13 = (bf16[64,640]{1,0:T(8,128)(2,1)S(1)}, bf16[64,640]{1,0:T(8,128)(2,1)S(1)}, u32[]{:S(2)}, u32[]{:S(2)}) collective-permute-start(bf16[64,640]{1,0:T(8,128)(2,1)S(1)} %get-tuple-element.60), channel_id=1, source_target_pairs={{0,6},{1,7},{2,4},{3,5},{4,2},{5,3},{6,0},{7,1},{8,14},{9,15},{10,... | collective-permute-start | bytes 245768 | tf_op jit(solution)/shard_map/ppermute | solution.py:230
  28.1 0.5 collective-permute-start.14
  28.5 0.7 %collective-permute-start.15 = (bf16[64,640]{1,0:T(8,128)(2,1)S(1)}, bf16[64,640]{1,0:T(8,128)(2,1)S(1)}, u32[]{:S(2)}, u32[]{:S(2)}) collective-permute-start(bf16[64,640]{1,0:T(8,128)(2,1)S(1)} %get-tuple-element.62), channel_id=1, source_target_pairs={{0,2},{1,3},{2,0},{3,1},{4,6},{5,7},{6,4},{7,5},{8,10},{9,11},{10,... | collective-permute-start | bytes 245768 | tf_op jit(solution)/shard_map/ppermute | solution.py:230
  29.3 0.4 collective-permute-done.11.refs_3_
  29.6 0.8 %collective-permute-done.9.refs_1_ = bf16[64,640]{1,0:T(8,128)(2,1)S(1)} collective-permute-done((bf16[64,640]{1,0:T(8,128)(2,1)S(1)}, bf16[64,640]{1,0:T(8,128)(2,1)S(1)}, u32[]{:S(2)}, u32[]{:S(2)}) %collective-permute-start.9) | collective-permute-done | bytes 81952 | tf_op jit(solution)/shard_map/ppermute | solution.py:230
  30.5 0.3 combine.1
  30.8 3.1 %collective-permute-start.12 = (bf16[64,640]{1,0:T(8,128)(2,1)S(1)}, bf16[64,640]{1,0:T(8,128)(2,1)S(1)}, u32[]{:S(2)}, u32[]{:S(2)}) collective-permute-start(bf16[64,640]{1,0:T(8,128)(2,1)S(1)} %combine.1), channel_id=1, source_target_pairs={{0,8},{1,9},{2,10},{3,11},{4,12},{5,13},{6,14},{7,15},{8,0},{9,1},... | collective-permute-start | bytes 245768 | tf_op jit(solution)/shard_map/ppermute | solution.py:230
  33.9 3.3 %collective-permute-done.12.refs_0_ = bf16[64,640]{1,0:T(8,128)(2,1)S(1)} collective-permute-done((bf16[64,640]{1,0:T(8,128)(2,1)S(1)}, bf16[64,640]{1,0:T(8,128)(2,1)S(1)}, u32[]{:S(2)}, u32[]{:S(2)}) %collective-permute-start.12) | collective-permute-done | bytes 81952 | tf_op jit(solution)/shard_map/ppermute | solution.py:230
  37.1 0.3 merge.1
  37.5 1.2 %collective-permute-done.16.got_ref = bf16[32,512]{1,0:T(8,128)(2,1)S(1)} collective-permute-done((bf16[32,512]{1,0:T(8,128)(2,1)S(1)}, bf16[32,512]{1,0:T(8,128)(2,1)S(1)}, u32[]{:S(2)}, u32[]{:S(2)}) %collective-permute-start.16) | collective-permute-done | bytes 32800 | tf_op jit(solution)/shard_map/ppermute | solution.py:230
  38.7 2.3 %project.1 = bf16[16,8,448]{2,1,0:T(8,128)(2,1)S(1)} custom-call(bf16[32,512]{1,0:T(8,128)(2,1)S(1)} %get-tuple-element.63.own_ref, bf16[32,512]{1,0:T(8,128)(2,1)S(1)} %collective-permute-done.16.got_ref, bf16[8,512,128]{2,1,0:T(8,128)(2,1)S(1)} %copy-done.1, bf16[1024,7168]{1,0:T(8,128)(2,1)S(1)} %copy-done), custom_call_target="tpu_custom_call" | custom-call | tf_op jit(solution)/shard_map/project/pallas_call | solution.py:197
  41.0 11.3 %all_to_all.5.in_ref = bf16[16,8,448]{2,1,0:T(8,128)(2,1)S(1)} all-to-all(bf16[16,8,448]{2,1,0:T(8,128)(2,1)S(1)} %project.1), channel_id=1, replica_groups=mesh['grp'=2,'ctx'=16] {'ctx'}, dimensions={0} | all-to-all | bytes 229376 | tf_op jit(solution)/shard_map/all_to_all | solution.py:260
  52.3 0.6 %finish.1 = bf16[2,4,448]{2,1,0:T(4,128)(2,1)} custom-call(bf16[16,8,448]{2,1,0:T(8,128)(2,1)S(1)} %all_to_all.5.in_ref), custom_call_target="tpu_custom_call" | custom-call | tf_op jit(solution)/shard_map/finish/pallas_call | solution.py:216
  (23 shorter events, 0.3 us)
Async XLA Ops:
  0.0 14.7 %copy-start.4 = (s32[2]{0:T(128)S(1)}, s32[2]{0:T(128)}, u32[]{:S(2)}) copy-start(s32[2]{0:T(128)} %param.8) | copy-start | bytes 28
  0.0 14.8 %copy-start.3 = (s32[2,4]{1,0:T(2,128)S(1)}, s32[2,4]{1,0:T(2,128)}, u32[]{:S(2)}) copy-start(s32[2,4]{1,0:T(2,128)} %mask_ref.3) | copy-start | bytes 100
  0.0 1.6 %collective-permute-start = (bf16[2,4,8,576]{3,2,1,0:T(8,128)(2,1)}, bf16[2,4,8,576]{3,2,1,0:T(8,128)(2,1)S(1)}, u32[]{:S(2)}, u32[]{:S(2)}) collective-permute-start(bf16[2,4,8,576]{3,2,1,0:T(8,128)(2,1)} %param.6), channel_id=1, source_target_pairs={{0,1},{1,0},{2,3},{3,2},{4,5},{5,4},{6,7},{7,6},{8,9},{9,8},{10,11... | collective-permute-start | bytes 221192 | tf_op jit(solution)/shard_map/ppermute | solution.py:230
  0.5 14.3 %copy-start.2 = (bf16[2,2048,576]{1,2,0:T(8,128)(2,1)S(1)}, bf16[2,2048,576]{1,2,0:T(8,128)(2,1)}, u32[]{:S(2)}) copy-start(bf16[2,2048,576]{1,2,0:T(8,128)(2,1)} %param.7) | copy-start | bytes 14155780
  1.6 12.8 %collective-permute-start.5 = (bf16[2,576,2048]{2,1,0:T(8,128)(2,1)}, bf16[2,576,2048]{2,1,0:T(8,128)(2,1)S(1)}, u32[]{:S(2)}, u32[]{:S(2)}) collective-permute-start(bf16[2,576,2048]{2,1,0:T(8,128)(2,1)} %bitcast.5), channel_id=1, source_target_pairs={{0,1},{1,0},{2,3},{3,2},{4,5},{5,4},{6,7},{7,6},{8,9},{9,8},{10,11... | collective-permute-start | bytes 14155784 | tf_op jit(solution)/shard_map/ppermute | solution.py:230
  2.0 8.6 %collective-permute-start.3 = (bf16[64,576]{1,0:T(8,128)(2,1)S(1)}, bf16[64,576]{1,0:T(8,128)(2,1)S(1)}, u32[]{:S(2)}, u32[]{:S(2)}) collective-permute-start(bf16[64,576]{1,0:T(8,128)(2,1)S(1)} %select.3.refs_0_), channel_id=1, source_target_pairs={{0,8},{1,9},{2,10},{3,11},{4,12},{5,13},{6,14},{7,15},{8,0},{9,1},... | collective-permute-start | bytes 221192 | tf_op jit(solution)/shard_map/ppermute | solution.py:230
  5.8 4.8 %collective-permute-start.4 = (bf16[64,576]{1,0:T(8,128)(2,1)S(1)}, bf16[64,576]{1,0:T(8,128)(2,1)S(1)}, u32[]{:S(2)}, u32[]{:S(2)}) collective-permute-start(bf16[64,576]{1,0:T(8,128)(2,1)S(1)} %select.3.refs_0_), channel_id=1, source_target_pairs={{0,2},{1,3},{2,0},{3,1},{4,6},{5,7},{6,4},{7,5},{8,10},{9,11},{10,... | collective-permute-start | bytes 221192 | tf_op jit(solution)/shard_map/ppermute | solution.py:230
  7.3 7.4 %collective-permute-start.1 = (bf16[64,576]{1,0:T(8,128)(2,1)S(1)}, bf16[64,576]{1,0:T(8,128)(2,1)S(1)}, u32[]{:S(2)}, u32[]{:S(2)}) collective-permute-start(bf16[64,576]{1,0:T(8,128)(2,1)S(1)} %select.3.refs_0_), channel_id=1, source_target_pairs={{0,6},{1,7},{2,4},{3,5},{4,2},{5,3},{6,0},{7,1},{8,14},{9,15},{10,... | collective-permute-start | bytes 221192 | tf_op jit(solution)/shard_map/ppermute | solution.py:230
  8.8 5.9 %collective-permute-start.2 = (bf16[64,576]{1,0:T(8,128)(2,1)S(1)}, bf16[64,576]{1,0:T(8,128)(2,1)S(1)}, u32[]{:S(2)}, u32[]{:S(2)}) collective-permute-start(bf16[64,576]{1,0:T(8,128)(2,1)S(1)} %select.3.refs_0_), channel_id=1, source_target_pairs={{0,4},{1,5},{2,6},{3,7},{4,0},{5,1},{6,2},{7,3},{8,12},{9,13},{10,... | collective-permute-start | bytes 221192 | tf_op jit(solution)/shard_map/ppermute | solution.py:230
  10.6 7.6 %collective-permute-start.6 = (bf16[64,576]{1,0:T(8,128)(2,1)S(1)}, bf16[64,576]{1,0:T(8,128)(2,1)S(1)}, u32[]{:S(2)}, u32[]{:S(2)}) collective-permute-start(bf16[64,576]{1,0:T(8,128)(2,1)S(1)} %collective-permute-done.3.refs_0_), channel_id=1, source_target_pairs={{0,6},{1,7},{2,4},{3,5},{4,2},{5,3},{6,0},{7,1},{8,14},{9,15},{10,... | collective-permute-start | bytes 221192 | tf_op jit(solution)/shard_map/ppermute | solution.py:230
  13.9 4.4 %collective-permute-start.7 = (bf16[64,576]{1,0:T(8,128)(2,1)S(1)}, bf16[64,576]{1,0:T(8,128)(2,1)S(1)}, u32[]{:S(2)}, u32[]{:S(2)}) collective-permute-start(bf16[64,576]{1,0:T(8,128)(2,1)S(1)} %collective-permute-done.3.refs_0_), channel_id=1, source_target_pairs={{0,4},{1,5},{2,6},{3,7},{4,0},{5,1},{6,2},{7,3},{8,12},{9,13},{10,... | collective-permute-start | bytes 221192 | tf_op jit(solution)/shard_map/ppermute | solution.py:230
  14.4 4.4 %collective-permute-start.8 = (bf16[64,576]{1,0:T(8,128)(2,1)S(1)}, bf16[64,576]{1,0:T(8,128)(2,1)S(1)}, u32[]{:S(2)}, u32[]{:S(2)}) collective-permute-start(bf16[64,576]{1,0:T(8,128)(2,1)S(1)} %collective-permute-done.3.refs_0_), channel_id=1, source_target_pairs={{0,2},{1,3},{2,0},{3,1},{4,6},{5,7},{6,4},{7,5},{8,10},{9,11},{10,... | collective-permute-start | bytes 221192 | tf_op jit(solution)/shard_map/ppermute | solution.py:230
  14.8 23.9 %copy-start = (bf16[1024,7168]{1,0:T(8,128)(2,1)S(1)}, bf16[1024,7168]{1,0:T(8,128)(2,1)}, u32[]{:S(2)}) copy-start(bf16[1024,7168]{1,0:T(8,128)(2,1)} %weight_ref.1) | copy-start | bytes 44040196
  18.2 20.6 %copy-start.1 = (bf16[8,512,128]{2,1,0:T(8,128)(2,1)S(1)}, bf16[8,512,128]{2,1,0:T(8,128)(2,1)}, u32[]{:S(2)}) copy-start(bf16[8,512,128]{2,1,0:T(8,128)(2,1)} %up_ref.1) | copy-start | bytes 3145732
  22.2 6.3 %collective-permute-start.10 = (bf16[64,640]{1,0:T(8,128)(2,1)S(1)}, bf16[64,640]{1,0:T(8,128)(2,1)S(1)}, u32[]{:S(2)}, u32[]{:S(2)}) collective-permute-start(bf16[64,640]{1,0:T(8,128)(2,1)S(1)} %get-tuple-element.57), channel_id=1, source_target_pairs={{0,4},{1,5},{2,6},{3,7},{4,0},{5,1},{6,2},{7,3},{8,12},{9,13},{10,... | collective-permute-start | bytes 245768 | tf_op jit(solution)/shard_map/ppermute | solution.py:230
  23.8 5.8 %collective-permute-start.11 = (bf16[64,640]{1,0:T(8,128)(2,1)S(1)}, bf16[64,640]{1,0:T(8,128)(2,1)S(1)}, u32[]{:S(2)}, u32[]{:S(2)}) collective-permute-start(bf16[64,640]{1,0:T(8,128)(2,1)S(1)} %get-tuple-element.58), channel_id=1, source_target_pairs={{0,2},{1,3},{2,0},{3,1},{4,6},{5,7},{6,4},{7,5},{8,10},{9,11},{10,... | collective-permute-start | bytes 245768 | tf_op jit(solution)/shard_map/ppermute | solution.py:230
  25.1 5.3 %collective-permute-start.9 = (bf16[64,640]{1,0:T(8,128)(2,1)S(1)}, bf16[64,640]{1,0:T(8,128)(2,1)S(1)}, u32[]{:S(2)}, u32[]{:S(2)}) collective-permute-start(bf16[64,640]{1,0:T(8,128)(2,1)S(1)} %get-tuple-element.56), channel_id=1, source_target_pairs={{0,6},{1,7},{2,4},{3,5},{4,2},{5,3},{6,0},{7,1},{8,14},{9,15},{10,... | collective-permute-start | bytes 245768 | tf_op jit(solution)/shard_map/ppermute | solution.py:230
  25.8 8.1 %collective-permute-start.13 = (bf16[64,640]{1,0:T(8,128)(2,1)S(1)}, bf16[64,640]{1,0:T(8,128)(2,1)S(1)}, u32[]{:S(2)}, u32[]{:S(2)}) collective-permute-start(bf16[64,640]{1,0:T(8,128)(2,1)S(1)} %get-tuple-element.60), channel_id=1, source_target_pairs={{0,6},{1,7},{2,4},{3,5},{4,2},{5,3},{6,0},{7,1},{8,14},{9,15},{10,... | collective-permute-start | bytes 245768 | tf_op jit(solution)/shard_map/ppermute | solution.py:230
  28.1 5.8 %collective-permute-start.14 = (bf16[64,640]{1,0:T(8,128)(2,1)S(1)}, bf16[64,640]{1,0:T(8,128)(2,1)S(1)}, u32[]{:S(2)}, u32[]{:S(2)}) collective-permute-start(bf16[64,640]{1,0:T(8,128)(2,1)S(1)} %get-tuple-element.61), channel_id=1, source_target_pairs={{0,4},{1,5},{2,6},{3,7},{4,0},{5,1},{6,2},{7,3},{8,12},{9,13},{10,... | collective-permute-start | bytes 245768 | tf_op jit(solution)/shard_map/ppermute | solution.py:230
  28.5 5.3 %collective-permute-start.15 = (bf16[64,640]{1,0:T(8,128)(2,1)S(1)}, bf16[64,640]{1,0:T(8,128)(2,1)S(1)}, u32[]{:S(2)}, u32[]{:S(2)}) collective-permute-start(bf16[64,640]{1,0:T(8,128)(2,1)S(1)} %get-tuple-element.62), channel_id=1, source_target_pairs={{0,2},{1,3},{2,0},{3,1},{4,6},{5,7},{6,4},{7,5},{8,10},{9,11},{10,... | collective-permute-start | bytes 245768 | tf_op jit(solution)/shard_map/ppermute | solution.py:230
  30.8 6.4 %collective-permute-start.12 = (bf16[64,640]{1,0:T(8,128)(2,1)S(1)}, bf16[64,640]{1,0:T(8,128)(2,1)S(1)}, u32[]{:S(2)}, u32[]{:S(2)}) collective-permute-start(bf16[64,640]{1,0:T(8,128)(2,1)S(1)} %combine.1), channel_id=1, source_target_pairs={{0,8},{1,9},{2,10},{3,11},{4,12},{5,13},{6,14},{7,15},{8,0},{9,1},... | collective-permute-start | bytes 245768 | tf_op jit(solution)/shard_map/ppermute | solution.py:230
  37.4 1.3 %collective-permute-start.16 = (bf16[32,512]{1,0:T(8,128)(2,1)S(1)}, bf16[32,512]{1,0:T(8,128)(2,1)S(1)}, u32[]{:S(2)}, u32[]{:S(2)}) collective-permute-start(bf16[32,512]{1,0:T(8,128)(2,1)S(1)} %get-tuple-element.64), channel_id=1, source_target_pairs={{0,1},{1,0},{2,3},{3,2},{4,5},{5,4},{6,7},{7,6},{8,9},{9,8},{10,11... | collective-permute-start | bytes 98312 | tf_op jit(solution)/shard_map/ppermute | solution.py:230

commit v6 on v5

--- a/solution.py
+++ b/solution.py
@@ -251,7 +251,9 @@
     far_parts = attend(spread, draft_mask, [far, *far_queries], keys, spec, heads, latent)
     near_parts, far_parts = lax.optimization_barrier((near_parts, far_parts))
     far_part = combine(
-        [far_parts[0]] + [swap(part, bits) for part, bits in zip(far_parts[1:], near)], latent
+        [far_parts[0]]
+        + [swap(far_parts[i + 1], near[i]) for i in (1, 0, *range(2, len(near)))],
+        latent,
     )
     parts = [swap(far_part, far_bit), near_parts[0]]
     parts += [swap(part, bits) for part, bits in zip(near_parts[1:], near)]

time: 53.1 us -> 52.5 us (0.989)
  waiting for transfers between devices: 7.91 us -> 6.56 us
  blocking collectives: 11.3 us -> 12.2 us
    ppermute x17, waiting for transfers between devices: 7.91 us -> 6.56 us  [swap(): return lax.ppermute(x, 'ctx', [(i, i ^ bits) for i in range(n)])]
    all_to_all x1, blocking collectives: 11.3 us -> 12.2 us  [on_device(): received = lax.all_to_all(outs, 'ctx', 0, 0, tiled=True)]
where the time goes in v6:
time: 52.5 us; the launch traced here: 52.3 us
  starting transfers between devices  22.1 us (42%)
  blocking collectives  12.2 us (23%)
  Pallas kernels  10.2 us (19%)
  waiting for transfers between devices  6.56 us (12%)
  local copies, waits for them, and re-layouts  1.18 us (2%)
    ppermute x17, starting transfers between devices, swap(): return lax.ppermute(x, 'ctx', [(i, i ^ bits) for i in range(n)])  22.1 us
    all_to_all x1, blocking collectives, on_device(): received = lax.all_to_all(outs, 'ctx', 0, 0, tiled=True)  12.2 us
    pallas_call x2, Pallas kernels, attend(): pl.pallas_call(functools.partial(attend_kernel, chunks, spec, heads, late...  6.74 us
    ppermute x17, waiting for transfers between devices, swap(): return lax.ppermute(x, 'ctx', [(i, i ^ bits) for i in range(n)])  6.56 us
    pallas_call x1, Pallas kernels, project(): pl.pallas_call(functools.partial(project_kernel, heads, group), out_shape...  2.27 us
  transfers between devices with their start and end apart: 17, of which 8 were waited for; matrix products, arithmetic and copies ran while one was open for 2% of the time, Pallas kernels for 7%

profile of v6, /device:TPU:0, one launch (start us, length us, event | category | flops | bytes accessed | tf_op | source)
XLA Modules:
  0.0 52.3 jit_solution(3740923041986639134)
XLA Ops:
  0.0 0.5 collective-permute-start
  0.5 0.9 %dynamic-slice_bitcast_fusion.1.own_ref = bf16[4,8,576]{2,1,0:T(8,128)(2,1)S(1)} fusion(bf16[2,4,8,576]{3,2,1,0:T(8,128)(2,1)} %param.6, s32[]{:T(128)S(6)} %select_n.6), kind=kLoop, calls=%fused_computation.1 | loop fusion | bytes 73732 | tf_op jit(solution)/shard_map/jit(dynamic_index_in_dim)/squeeze | solution.py:234
  1.4 0.2 collective-permute-done.got_ref
  1.6 0.4 collective-permute-start.5
  2.0 3.8 %collective-permute-start.3 = (bf16[64,576]{1,0:T(8,128)(2,1)S(1)}, bf16[64,576]{1,0:T(8,128)(2,1)S(1)}, u32[]{:S(2)}, u32[]{:S(2)}) collective-permute-start(bf16[64,576]{1,0:T(8,128)(2,1)S(1)} %select.3.refs_0_), channel_id=1, source_target_pairs={{0,8},{1,9},{2,10},{3,11},{4,12},{5,13},{6,14},{7,15},{8,0},{9,1},... | collective-permute-start | bytes 221192 | tf_op jit(solution)/shard_map/ppermute | solution.py:230
  5.8 1.5 %collective-permute-start.4 = (bf16[64,576]{1,0:T(8,128)(2,1)S(1)}, bf16[64,576]{1,0:T(8,128)(2,1)S(1)}, u32[]{:S(2)}, u32[]{:S(2)}) collective-permute-start(bf16[64,576]{1,0:T(8,128)(2,1)S(1)} %select.3.refs_0_), channel_id=1, source_target_pairs={{0,2},{1,3},{2,0},{3,1},{4,6},{5,7},{6,4},{7,5},{8,10},{9,11},{10,... | collective-permute-start | bytes 221192 | tf_op jit(solution)/shard_map/ppermute | solution.py:230
  7.3 1.5 %collective-permute-start.1 = (bf16[64,576]{1,0:T(8,128)(2,1)S(1)}, bf16[64,576]{1,0:T(8,128)(2,1)S(1)}, u32[]{:S(2)}, u32[]{:S(2)}) collective-permute-start(bf16[64,576]{1,0:T(8,128)(2,1)S(1)} %select.3.refs_0_), channel_id=1, source_target_pairs={{0,6},{1,7},{2,4},{3,5},{4,2},{5,3},{6,0},{7,1},{8,14},{9,15},{10,... | collective-permute-start | bytes 221192 | tf_op jit(solution)/shard_map/ppermute | solution.py:230
  8.8 0.4 collective-permute-start.2
  9.3 1.3 %collective-permute-done.3.refs_0_ = bf16[64,576]{1,0:T(8,128)(2,1)S(1)} collective-permute-done((bf16[64,576]{1,0:T(8,128)(2,1)S(1)}, bf16[64,576]{1,0:T(8,128)(2,1)S(1)}, u32[]{:S(2)}, u32[]{:S(2)}) %collective-permute-start.3) | collective-permute-done | bytes 73760 | tf_op jit(solution)/shard_map/ppermute | solution.py:230
  10.6 3.4 %collective-permute-start.6 = (bf16[64,576]{1,0:T(8,128)(2,1)S(1)}, bf16[64,576]{1,0:T(8,128)(2,1)S(1)}, u32[]{:S(2)}, u32[]{:S(2)}) collective-permute-start(bf16[64,576]{1,0:T(8,128)(2,1)S(1)} %collective-permute-done.3.refs_0_), channel_id=1, source_target_pairs={{0,6},{1,7},{2,4},{3,5},{4,2},{5,3},{6,0},{7,1},{8,14},{9,15},{10,... | collective-permute-start | bytes 221192 | tf_op jit(solution)/shard_map/ppermute | solution.py:230
  13.9 0.4 collective-permute-start.7
  14.5 0.2 dynamic-slice_bitcast_fusion.refs_5_
  14.8 3.4 %attend.2 = (bf16[64,640]{1,0:T(8,128)(2,1)S(1)}, bf16[64,640]{1,0:T(8,128)(2,1)S(1)}, bf16[64,640]{1,0:T(8,128)(2,1)S(1)}, bf16[64,640]{1,0:T(8,128)(2,1)S(1)}) custom-call(s32[2,128]{1,0:T(2,128)S(1)} %broadcast_in_dim.2.lengths_ref, s32[2,4]{1,0:T(2,128)S(1)} %copy-done.3, bf16[64,576]{1,0:T(8,128)(2,1)S(1)} %select.3.refs_0_, ...), custom_call_target="tpu_custom_call" | custom-call | flops 2281701376 | bytes 4718592 | tf_op jit(solution)/shard_map/attend/pallas_call | solution.py:99
  18.2 0.2 collective-permute-done.7.refs_2_
  18.4 0.5 collective-permute-done.8.refs_3_
  18.8 3.4 %attend.3 = (bf16[64,640]{1,0:T(8,128)(2,1)S(1)}, bf16[64,640]{1,0:T(8,128)(2,1)S(1)}, bf16[64,640]{1,0:T(8,128)(2,1)S(1)}, bf16[64,640]{1,0:T(8,128)(2,1)S(1)}) custom-call(s32[2,128]{1,0:T(2,128)S(1)} %broadcast_in_dim.2.lengths_ref, s32[2,4]{1,0:T(2,128)S(1)} %copy-done.3, bf16[64,576]{1,0:T(8,128)(2,1)S(1)} %collective-permute-done.3.refs_0_, ...), custom_call_target="tpu_custom_call" | custom-call | flops 2281701376 | bytes 4718592 | tf_op jit(solution)/shard_map/attend/pallas_call | solution.py:99
  22.2 2.4 %collective-permute-start.10 = (bf16[64,640]{1,0:T(8,128)(2,1)S(1)}, bf16[64,640]{1,0:T(8,128)(2,1)S(1)}, u32[]{:S(2)}, u32[]{:S(2)}) collective-permute-start(bf16[64,640]{1,0:T(8,128)(2,1)S(1)} %get-tuple-element.57), channel_id=1, source_target_pairs={{0,6},{1,7},{2,4},{3,5},{4,2},{5,3},{6,0},{7,1},{8,14},{9,15},{10,... | collective-permute-start | bytes 245768 | tf_op jit(solution)/shard_map/ppermute | solution.py:230
  24.6 0.7 %collective-permute-start.11 = (bf16[64,640]{1,0:T(8,128)(2,1)S(1)}, bf16[64,640]{1,0:T(8,128)(2,1)S(1)}, u32[]{:S(2)}, u32[]{:S(2)}) collective-permute-start(bf16[64,640]{1,0:T(8,128)(2,1)S(1)} %get-tuple-element.58), channel_id=1, source_target_pairs={{0,2},{1,3},{2,0},{3,1},{4,6},{5,7},{6,4},{7,5},{8,10},{9,11},{10,... | collective-permute-start | bytes 245768 | tf_op jit(solution)/shard_map/ppermute | solution.py:230
  25.3 0.5 collective-permute-start.9
  25.8 2.3 %collective-permute-start.13 = (bf16[64,640]{1,0:T(8,128)(2,1)S(1)}, bf16[64,640]{1,0:T(8,128)(2,1)S(1)}, u32[]{:S(2)}, u32[]{:S(2)}) collective-permute-start(bf16[64,640]{1,0:T(8,128)(2,1)S(1)} %get-tuple-element.60), channel_id=1, source_target_pairs={{0,6},{1,7},{2,4},{3,5},{4,2},{5,3},{6,0},{7,1},{8,14},{9,15},{10,... | collective-permute-start | bytes 245768 | tf_op jit(solution)/shard_map/ppermute | solution.py:230
  28.1 0.5 collective-permute-start.14
  28.5 1.3 %collective-permute-start.15 = (bf16[64,640]{1,0:T(8,128)(2,1)S(1)}, bf16[64,640]{1,0:T(8,128)(2,1)S(1)}, u32[]{:S(2)}, u32[]{:S(2)}) collective-permute-start(bf16[64,640]{1,0:T(8,128)(2,1)S(1)} %get-tuple-element.62), channel_id=1, source_target_pairs={{0,2},{1,3},{2,0},{3,1},{4,6},{5,7},{6,4},{7,5},{8,10},{9,11},{10,... | collective-permute-start | bytes 245768 | tf_op jit(solution)/shard_map/ppermute | solution.py:230
  29.8 0.2 collective-permute-done.11.refs_3_
  30.0 0.3 combine.1
  30.3 2.4 %collective-permute-start.12 = (bf16[64,640]{1,0:T(8,128)(2,1)S(1)}, bf16[64,640]{1,0:T(8,128)(2,1)S(1)}, u32[]{:S(2)}, u32[]{:S(2)}) collective-permute-start(bf16[64,640]{1,0:T(8,128)(2,1)S(1)} %combine.1), channel_id=1, source_target_pairs={{0,8},{1,9},{2,10},{3,11},{4,12},{5,13},{6,14},{7,15},{8,0},{9,1},... | collective-permute-start | bytes 245768 | tf_op jit(solution)/shard_map/ppermute | solution.py:230
  32.7 0.3 collective-permute-done.15.refs_4_
  33.0 2.7 %collective-permute-done.12.refs_0_ = bf16[64,640]{1,0:T(8,128)(2,1)S(1)} collective-permute-done((bf16[64,640]{1,0:T(8,128)(2,1)S(1)}, bf16[64,640]{1,0:T(8,128)(2,1)S(1)}, u32[]{:S(2)}, u32[]{:S(2)}) %collective-permute-start.12) | collective-permute-done | bytes 81952 | tf_op jit(solution)/shard_map/ppermute | solution.py:230
  35.7 0.3 merge.1
  36.0 1.2 %collective-permute-done.16.got_ref = bf16[32,512]{1,0:T(8,128)(2,1)S(1)} collective-permute-done((bf16[32,512]{1,0:T(8,128)(2,1)S(1)}, bf16[32,512]{1,0:T(8,128)(2,1)S(1)}, u32[]{:S(2)}, u32[]{:S(2)}) %collective-permute-start.16) | collective-permute-done | bytes 32800 | tf_op jit(solution)/shard_map/ppermute | solution.py:230
  37.2 2.3 %project.1 = bf16[16,8,448]{2,1,0:T(8,128)(2,1)S(1)} custom-call(bf16[32,512]{1,0:T(8,128)(2,1)S(1)} %get-tuple-element.63.own_ref, bf16[32,512]{1,0:T(8,128)(2,1)S(1)} %collective-permute-done.16.got_ref, bf16[8,512,128]{2,1,0:T(8,128)(2,1)S(1)} %copy-done.1, bf16[1024,7168]{1,0:T(8,128)(2,1)S(1)} %copy-done), custom_call_target="tpu_custom_call" | custom-call | tf_op jit(solution)/shard_map/project/pallas_call | solution.py:197
  39.5 12.2 %all_to_all.5.in_ref = bf16[16,8,448]{2,1,0:T(8,128)(2,1)S(1)} all-to-all(bf16[16,8,448]{2,1,0:T(8,128)(2,1)S(1)} %project.1), channel_id=1, replica_groups=mesh['grp'=2,'ctx'=16] {'ctx'}, dimensions={0} | all-to-all | bytes 229376 | tf_op jit(solution)/shard_map/all_to_all | solution.py:262
  51.7 0.6 %finish.1 = bf16[2,4,448]{2,1,0:T(4,128)(2,1)} custom-call(bf16[16,8,448]{2,1,0:T(8,128)(2,1)S(1)} %all_to_all.5.in_ref), custom_call_target="tpu_custom_call" | custom-call | tf_op jit(solution)/shard_map/finish/pallas_call | solution.py:216
  (23 shorter events, 0.3 us)
Async XLA Ops:
  0.0 14.7 %copy-start.4 = (s32[2]{0:T(128)S(1)}, s32[2]{0:T(128)}, u32[]{:S(2)}) copy-start(s32[2]{0:T(128)} %param.8) | copy-start | bytes 28
  0.0 14.8 %copy-start.3 = (s32[2,4]{1,0:T(2,128)S(1)}, s32[2,4]{1,0:T(2,128)}, u32[]{:S(2)}) copy-start(s32[2,4]{1,0:T(2,128)} %mask_ref.3) | copy-start | bytes 100
  0.0 1.6 %collective-permute-start = (bf16[2,4,8,576]{3,2,1,0:T(8,128)(2,1)}, bf16[2,4,8,576]{3,2,1,0:T(8,128)(2,1)S(1)}, u32[]{:S(2)}, u32[]{:S(2)}) collective-permute-start(bf16[2,4,8,576]{3,2,1,0:T(8,128)(2,1)} %param.6), channel_id=1, source_target_pairs={{0,1},{1,0},{2,3},{3,2},{4,5},{5,4},{6,7},{7,6},{8,9},{9,8},{10,11... | collective-permute-start | bytes 221192 | tf_op jit(solution)/shard_map/ppermute | solution.py:230
  0.5 14.3 %copy-start.2 = (bf16[2,2048,576]{1,2,0:T(8,128)(2,1)S(1)}, bf16[2,2048,576]{1,2,0:T(8,128)(2,1)}, u32[]{:S(2)}) copy-start(bf16[2,2048,576]{1,2,0:T(8,128)(2,1)} %param.7) | copy-start | bytes 14155780
  1.6 12.8 %collective-permute-start.5 = (bf16[2,576,2048]{2,1,0:T(8,128)(2,1)}, bf16[2,576,2048]{2,1,0:T(8,128)(2,1)S(1)}, u32[]{:S(2)}, u32[]{:S(2)}) collective-permute-start(bf16[2,576,2048]{2,1,0:T(8,128)(2,1)} %bitcast.5), channel_id=1, source_target_pairs={{0,1},{1,0},{2,3},{3,2},{4,5},{5,4},{6,7},{7,6},{8,9},{9,8},{10,11... | collective-permute-start | bytes 14155784 | tf_op jit(solution)/shard_map/ppermute | solution.py:230
  2.0 8.6 %collective-permute-start.3 = (bf16[64,576]{1,0:T(8,128)(2,1)S(1)}, bf16[64,576]{1,0:T(8,128)(2,1)S(1)}, u32[]{:S(2)}, u32[]{:S(2)}) collective-permute-start(bf16[64,576]{1,0:T(8,128)(2,1)S(1)} %select.3.refs_0_), channel_id=1, source_target_pairs={{0,8},{1,9},{2,10},{3,11},{4,12},{5,13},{6,14},{7,15},{8,0},{9,1},... | collective-permute-start | bytes 221192 | tf_op jit(solution)/shard_map/ppermute | solution.py:230
  5.8 4.8 %collective-permute-start.4 = (bf16[64,576]{1,0:T(8,128)(2,1)S(1)}, bf16[64,576]{1,0:T(8,128)(2,1)S(1)}, u32[]{:S(2)}, u32[]{:S(2)}) collective-permute-start(bf16[64,576]{1,0:T(8,128)(2,1)S(1)} %select.3.refs_0_), channel_id=1, source_target_pairs={{0,2},{1,3},{2,0},{3,1},{4,6},{5,7},{6,4},{7,5},{8,10},{9,11},{10,... | collective-permute-start | bytes 221192 | tf_op jit(solution)/shard_map/ppermute | solution.py:230
  7.3 7.4 %collective-permute-start.1 = (bf16[64,576]{1,0:T(8,128)(2,1)S(1)}, bf16[64,576]{1,0:T(8,128)(2,1)S(1)}, u32[]{:S(2)}, u32[]{:S(2)}) collective-permute-start(bf16[64,576]{1,0:T(8,128)(2,1)S(1)} %select.3.refs_0_), channel_id=1, source_target_pairs={{0,6},{1,7},{2,4},{3,5},{4,2},{5,3},{6,0},{7,1},{8,14},{9,15},{10,... | collective-permute-start | bytes 221192 | tf_op jit(solution)/shard_map/ppermute | solution.py:230
  8.8 5.9 %collective-permute-start.2 = (bf16[64,576]{1,0:T(8,128)(2,1)S(1)}, bf16[64,576]{1,0:T(8,128)(2,1)S(1)}, u32[]{:S(2)}, u32[]{:S(2)}) collective-permute-start(bf16[64,576]{1,0:T(8,128)(2,1)S(1)} %select.3.refs_0_), channel_id=1, source_target_pairs={{0,4},{1,5},{2,6},{3,7},{4,0},{5,1},{6,2},{7,3},{8,12},{9,13},{10,... | collective-permute-start | bytes 221192 | tf_op jit(solution)/shard_map/ppermute | solution.py:230
  10.6 7.6 %collective-permute-start.6 = (bf16[64,576]{1,0:T(8,128)(2,1)S(1)}, bf16[64,576]{1,0:T(8,128)(2,1)S(1)}, u32[]{:S(2)}, u32[]{:S(2)}) collective-permute-start(bf16[64,576]{1,0:T(8,128)(2,1)S(1)} %collective-permute-done.3.refs_0_), channel_id=1, source_target_pairs={{0,6},{1,7},{2,4},{3,5},{4,2},{5,3},{6,0},{7,1},{8,14},{9,15},{10,... | collective-permute-start | bytes 221192 | tf_op jit(solution)/shard_map/ppermute | solution.py:230
  13.9 4.4 %collective-permute-start.7 = (bf16[64,576]{1,0:T(8,128)(2,1)S(1)}, bf16[64,576]{1,0:T(8,128)(2,1)S(1)}, u32[]{:S(2)}, u32[]{:S(2)}) collective-permute-start(bf16[64,576]{1,0:T(8,128)(2,1)S(1)} %collective-permute-done.3.refs_0_), channel_id=1, source_target_pairs={{0,4},{1,5},{2,6},{3,7},{4,0},{5,1},{6,2},{7,3},{8,12},{9,13},{10,... | collective-permute-start | bytes 221192 | tf_op jit(solution)/shard_map/ppermute | solution.py:230
  14.4 4.4 %collective-permute-start.8 = (bf16[64,576]{1,0:T(8,128)(2,1)S(1)}, bf16[64,576]{1,0:T(8,128)(2,1)S(1)}, u32[]{:S(2)}, u32[]{:S(2)}) collective-permute-start(bf16[64,576]{1,0:T(8,128)(2,1)S(1)} %collective-permute-done.3.refs_0_), channel_id=1, source_target_pairs={{0,2},{1,3},{2,0},{3,1},{4,6},{5,7},{6,4},{7,5},{8,10},{9,11},{10,... | collective-permute-start | bytes 221192 | tf_op jit(solution)/shard_map/ppermute | solution.py:230
  14.8 22.4 %copy-start = (bf16[1024,7168]{1,0:T(8,128)(2,1)S(1)}, bf16[1024,7168]{1,0:T(8,128)(2,1)}, u32[]{:S(2)}) copy-start(bf16[1024,7168]{1,0:T(8,128)(2,1)} %weight_ref.1) | copy-start | bytes 44040196
  18.2 19.1 %copy-start.1 = (bf16[8,512,128]{2,1,0:T(8,128)(2,1)S(1)}, bf16[8,512,128]{2,1,0:T(8,128)(2,1)}, u32[]{:S(2)}) copy-start(bf16[8,512,128]{2,1,0:T(8,128)(2,1)} %up_ref.1) | copy-start | bytes 3145732
  22.2 6.3 %collective-permute-start.10 = (bf16[64,640]{1,0:T(8,128)(2,1)S(1)}, bf16[64,640]{1,0:T(8,128)(2,1)S(1)}, u32[]{:S(2)}, u32[]{:S(2)}) collective-permute-start(bf16[64,640]{1,0:T(8,128)(2,1)S(1)} %get-tuple-element.57), channel_id=1, source_target_pairs={{0,6},{1,7},{2,4},{3,5},{4,2},{5,3},{6,0},{7,1},{8,14},{9,15},{10,... | collective-permute-start | bytes 245768 | tf_op jit(solution)/shard_map/ppermute | solution.py:230
  24.6 5.4 %collective-permute-start.11 = (bf16[64,640]{1,0:T(8,128)(2,1)S(1)}, bf16[64,640]{1,0:T(8,128)(2,1)S(1)}, u32[]{:S(2)}, u32[]{:S(2)}) collective-permute-start(bf16[64,640]{1,0:T(8,128)(2,1)S(1)} %get-tuple-element.58), channel_id=1, source_target_pairs={{0,2},{1,3},{2,0},{3,1},{4,6},{5,7},{6,4},{7,5},{8,10},{9,11},{10,... | collective-permute-start | bytes 245768 | tf_op jit(solution)/shard_map/ppermute | solution.py:230
  25.3 4.7 %collective-permute-start.9 = (bf16[64,640]{1,0:T(8,128)(2,1)S(1)}, bf16[64,640]{1,0:T(8,128)(2,1)S(1)}, u32[]{:S(2)}, u32[]{:S(2)}) collective-permute-start(bf16[64,640]{1,0:T(8,128)(2,1)S(1)} %get-tuple-element.56), channel_id=1, source_target_pairs={{0,4},{1,5},{2,6},{3,7},{4,0},{5,1},{6,2},{7,3},{8,12},{9,13},{10,... | collective-permute-start | bytes 245768 | tf_op jit(solution)/shard_map/ppermute | solution.py:230
  25.8 6.9 %collective-permute-start.13 = (bf16[64,640]{1,0:T(8,128)(2,1)S(1)}, bf16[64,640]{1,0:T(8,128)(2,1)S(1)}, u32[]{:S(2)}, u32[]{:S(2)}) collective-permute-start(bf16[64,640]{1,0:T(8,128)(2,1)S(1)} %get-tuple-element.60), channel_id=1, source_target_pairs={{0,6},{1,7},{2,4},{3,5},{4,2},{5,3},{6,0},{7,1},{8,14},{9,15},{10,... | collective-permute-start | bytes 245768 | tf_op jit(solution)/shard_map/ppermute | solution.py:230
  28.1 4.6 %collective-permute-start.14 = (bf16[64,640]{1,0:T(8,128)(2,1)S(1)}, bf16[64,640]{1,0:T(8,128)(2,1)S(1)}, u32[]{:S(2)}, u32[]{:S(2)}) collective-permute-start(bf16[64,640]{1,0:T(8,128)(2,1)S(1)} %get-tuple-element.61), channel_id=1, source_target_pairs={{0,4},{1,5},{2,6},{3,7},{4,0},{5,1},{6,2},{7,3},{8,12},{9,13},{10,... | collective-permute-start | bytes 245768 | tf_op jit(solution)/shard_map/ppermute | solution.py:230
  28.5 4.4 %collective-permute-start.15 = (bf16[64,640]{1,0:T(8,128)(2,1)S(1)}, bf16[64,640]{1,0:T(8,128)(2,1)S(1)}, u32[]{:S(2)}, u32[]{:S(2)}) collective-permute-start(bf16[64,640]{1,0:T(8,128)(2,1)S(1)} %get-tuple-element.62), channel_id=1, source_target_pairs={{0,2},{1,3},{2,0},{3,1},{4,6},{5,7},{6,4},{7,5},{8,10},{9,11},{10,... | collective-permute-start | bytes 245768 | tf_op jit(solution)/shard_map/ppermute | solution.py:230
  30.3 5.4 %collective-permute-start.12 = (bf16[64,640]{1,0:T(8,128)(2,1)S(1)}, bf16[64,640]{1,0:T(8,128)(2,1)S(1)}, u32[]{:S(2)}, u32[]{:S(2)}) collective-permute-start(bf16[64,640]{1,0:T(8,128)(2,1)S(1)} %combine.1), channel_id=1, source_target_pairs={{0,8},{1,9},{2,10},{3,11},{4,12},{5,13},{6,14},{7,15},{8,0},{9,1},... | collective-permute-start | bytes 245768 | tf_op jit(solution)/shard_map/ppermute | solution.py:230
  36.0 1.3 %collective-permute-start.16 = (bf16[32,512]{1,0:T(8,128)(2,1)S(1)}, bf16[32,512]{1,0:T(8,128)(2,1)S(1)}, u32[]{:S(2)}, u32[]{:S(2)}) collective-permute-start(bf16[32,512]{1,0:T(8,128)(2,1)S(1)} %get-tuple-element.64), channel_id=1, source_target_pairs={{0,1},{1,0},{2,3},{3,2},{4,5},{5,4},{6,7},{7,6},{8,9},{9,8},{10,11... | collective-permute-start | bytes 98312 | tf_op jit(solution)/shard_map/ppermute | solution.py:230

commit v7 on v6

--- a/solution.py
+++ b/solution.py
@@ -11,7 +11,9 @@
 SOFTMAX_SCALE = 192.0 ** (-0.5)
 LOG2_SCALE = SOFTMAX_SCALE * math.log2(math.e)
 SCORE_FLOOR = -1e30
+PEAK_FLOOR = -(2.0**96)
 STAT_LANES = 128
+STAT_ROWS = 8
 MIB = 1024 * 1024
 HINT = 20 * MIB
 
@@ -65,25 +67,33 @@
         position = start + lax.broadcasted_iota(jnp.int32, (1, width), 1)
         return jnp.where(position < horizon, tile * LOG2_SCALE, SCORE_FLOOR)
 
-    peak = jnp.full((rows, 1), 0.1 * SCORE_FLOOR, jnp.float32)
+    peak = jnp.full((rows, 1), PEAK_FLOOR, jnp.float32)
     denominator = jnp.zeros((rows, 1), jnp.float32)
     numerator = jnp.zeros((rows, latent), jnp.float32)
-    tile = score(0)
-    for step in range(steps):
-        following = score(step + 1) if step + 1 < steps else None
-        higher = jnp.maximum(peak, jnp.max(tile, axis=1, keepdims=True))
-        if step == steps - 1:
+    half = steps // 2
+    tiles = [score(step) for step in range(half)]
+    for side in range(2):
+        following = []
+        higher = peak
+        for tile in tiles:
+            higher = jnp.maximum(higher, jnp.max(tile, axis=1, keepdims=True))
+        if side == 1:
             higher = sum(split_low(higher))
-        weights = jnp.exp2(tile - higher)
         ratio = jnp.exp2(peak - higher)
-        denominator = denominator * ratio + jnp.sum(weights, axis=1, keepdims=True)
-        numerator = numerator * ratio + lax.dot_general(
-            weights.astype(jnp.bfloat16),
-            keys(step, latent),
-            (((1,), (1,)), ((), ())),
-            preferred_element_type=jnp.float32,
-        )
-        peak, tile = higher, following
+        denominator *= ratio
+        numerator *= ratio
+        for i in range(half):
+            if side == 0:
+                following.append(score(half + i))
+            weights = jnp.exp2(tiles[i] - higher)
+            denominator += jnp.sum(weights, axis=1, keepdims=True)
+            numerator += lax.dot_general(
+                weights.astype(jnp.bfloat16),
+                keys(side * half + i, latent),
+                (((1,), (1,)), ((), ())),
+                preferred_element_type=jnp.float32,
+            )
+        peak, tiles = higher, following
     mask = mask_ref[pl.ds(lax.rem(me, 2), 1), :].astype(jnp.float32)
     numerator *= sum(jnp.where(draft == j, mask[:, j : j + 1], 0.0) for j in range(spec))
     chunk = rows // chunks
@@ -112,14 +122,18 @@
 def merged(in_refs, latent):
     peaks, denominators = [], []
     for ref in in_refs:
-        stats = ref[:, latent:].astype(jnp.float32)
+        rows = in_refs[-1].shape[0]
+        if ref.shape[1] == latent:
+            stats = ref[rows:, :STAT_LANES].astype(jnp.float32).T[:rows]
+        else:
+            stats = ref[:, latent:].astype(jnp.float32)
         peaks.append(stats[:, 0:1] + stats[:, 1:2])
         denominators.append(stats[:, 2:3] + stats[:, 3:4])
     largest = functools.reduce(jnp.maximum, peaks)
     upper, lower = 0.0, 0.0
     for ref, peak, denominator in zip(in_refs, peaks, denominators):
         factor = jnp.exp2(peak - largest)
-        upper += factor * ref[:, :latent].astype(jnp.float32)
+        upper += factor * ref[: peak.shape[0], :latent].astype(jnp.float32)
         lower += factor * denominator
     return largest, lower, upper
 
@@ -134,14 +148,28 @@
     ref[:, latent:] = stats.astype(jnp.bfloat16)
 
 
+def store_packed(ref, latent, peak, denominator, numerator):
+    rows = numerator.shape[0]
+    peak_high, peak_low = split_low(peak)
+    denom_high, denom_low = split_low(denominator)
+    lane = lax.broadcasted_iota(jnp.int32, (rows, STAT_LANES), 1)
+    stats = jnp.where(lane == 0, peak_high, jnp.where(lane == 1, peak_low, 0.0))
+    stats = jnp.where(lane == 2, denom_high, jnp.where(lane == 3, denom_low, stats))
+    blank = jnp.zeros((STAT_LANES - rows, STAT_LANES), jnp.float32)
+    stats = jnp.concatenate([stats, blank], axis=0).T[:STAT_ROWS]
+    ref[:rows] = numerator.astype(jnp.bfloat16)
+    ref[rows:] = jnp.zeros((STAT_ROWS, latent), jnp.bfloat16)
+    ref[rows:, :STAT_LANES] = stats.astype(jnp.bfloat16)
+
+
 def combine_kernel(parts, latent, *refs):
-    store_part(refs[parts], latent, *merged(refs[:parts], latent))
+    store_packed(refs[parts], latent, *merged(refs[:parts], latent))
 
 
 def combine(parts, latent):
     return pl.pallas_call(
         functools.partial(combine_kernel, len(parts), latent),
-        out_shape=jax.ShapeDtypeStruct(parts[0].shape, jnp.bfloat16),
+        out_shape=jax.ShapeDtypeStruct((parts[0].shape[0] + STAT_ROWS, latent), jnp.bfloat16),
         compiler_params=pltpu.CompilerParams(vmem_limit_bytes=8 * MIB),
         name="combine",
     )(*parts)
@@ -157,7 +185,7 @@
 
 
 def merge(parts, latent):
-    rows = parts[0].shape[0]
+    rows = parts[-1].shape[0]
     return pl.pallas_call(
         functools.partial(merge_kernel, len(parts), latent),
         out_shape=[jax.ShapeDtypeStruct((rows // 2, latent), jnp.bfloat16)] * 2,
@@ -193,7 +221,7 @@
 def project(own, got, value_up, weight, spec, owners):
     heads = own.shape[0] // spec
     columns = weight.shape[1] // owners
-    group = next(g for g in (2, 1, 4, 8, 16, owners) if (g * columns) % 128 == 0)
+    group = next(g for g in (8, 4, 2, 1, 16, owners) if (g * columns) % 128 == 0)
     return pl.pallas_call(
         functools.partial(project_kernel, heads, group),
         out_shape=jax.ShapeDtypeStruct((owners, 2 * spec, columns), jnp.bfloat16),

time: 52.5 us -> 52.4 us (level)
  no operation moved by 1% of the time
where the time goes in v7:
time: 52.4 us; the launch traced here: 52.2 us
  starting transfers between devices  22 us (42%)
  blocking collectives  12.2 us (23%)
  Pallas kernels  10.2 us (19%)
  waiting for transfers between devices  6.52 us (12%)
  local copies, waits for them, and re-layouts  1.18 us (2%)
    ppermute x17, starting transfers between devices, swap(): return lax.ppermute(x, 'ctx', [(i, i ^ bits) for i in range(n)])  22 us
    all_to_all x1, blocking collectives, on_device(): received = lax.all_to_all(outs, 'ctx', 0, 0, tiled=True)  12.2 us
    pallas_call x2, Pallas kernels, attend(): pl.pallas_call(functools.partial(attend_kernel, chunks, spec, heads, late...  6.68 us
    ppermute x17, waiting for transfers between devices, swap(): return lax.ppermute(x, 'ctx', [(i, i ^ bits) for i in range(n)])  6.52 us
    pallas_call x1, Pallas kernels, project(): pl.pallas_call(functools.partial(project_kernel, heads, group), out_shape...  2.27 us
  transfers between devices with their start and end apart: 17, of which 8 were waited for; matrix products, arithmetic and copies ran while one was open for 2% of the time, Pallas kernels for 7%

profile of v7, /device:TPU:0, one launch (start us, length us, event | category | flops | bytes accessed | tf_op | source)
XLA Modules:
  0.0 52.2 jit_solution(2197491571681189550)
XLA Ops:
  0.0 0.5 collective-permute-start
  0.5 0.9 %dynamic-slice_bitcast_fusion.1.own_ref = bf16[4,8,576]{2,1,0:T(8,128)(2,1)S(1)} fusion(bf16[2,4,8,576]{3,2,1,0:T(8,128)(2,1)} %param.6, s32[]{:T(128)S(6)} %select_n.6), kind=kLoop, calls=%fused_computation.1 | loop fusion | bytes 73732 | tf_op jit(solution)/shard_map/jit(dynamic_index_in_dim)/squeeze | solution.py:262
  1.4 0.2 collective-permute-done.got_ref
  1.6 0.4 collective-permute-start.5
  2.0 3.8 %collective-permute-start.3 = (bf16[64,576]{1,0:T(8,128)(2,1)S(1)}, bf16[64,576]{1,0:T(8,128)(2,1)S(1)}, u32[]{:S(2)}, u32[]{:S(2)}) collective-permute-start(bf16[64,576]{1,0:T(8,128)(2,1)S(1)} %select.3.refs_0_), channel_id=1, source_target_pairs={{0,8},{1,9},{2,10},{3,11},{4,12},{5,13},{6,14},{7,15},{8,0},{9,1},... | collective-permute-start | bytes 221192 | tf_op jit(solution)/shard_map/ppermute | solution.py:258
  5.8 1.5 %collective-permute-start.4 = (bf16[64,576]{1,0:T(8,128)(2,1)S(1)}, bf16[64,576]{1,0:T(8,128)(2,1)S(1)}, u32[]{:S(2)}, u32[]{:S(2)}) collective-permute-start(bf16[64,576]{1,0:T(8,128)(2,1)S(1)} %select.3.refs_0_), channel_id=1, source_target_pairs={{0,2},{1,3},{2,0},{3,1},{4,6},{5,7},{6,4},{7,5},{8,10},{9,11},{10,... | collective-permute-start | bytes 221192 | tf_op jit(solution)/shard_map/ppermute | solution.py:258
  7.3 1.5 %collective-permute-start.1 = (bf16[64,576]{1,0:T(8,128)(2,1)S(1)}, bf16[64,576]{1,0:T(8,128)(2,1)S(1)}, u32[]{:S(2)}, u32[]{:S(2)}) collective-permute-start(bf16[64,576]{1,0:T(8,128)(2,1)S(1)} %select.3.refs_0_), channel_id=1, source_target_pairs={{0,6},{1,7},{2,4},{3,5},{4,2},{5,3},{6,0},{7,1},{8,14},{9,15},{10,... | collective-permute-start | bytes 221192 | tf_op jit(solution)/shard_map/ppermute | solution.py:258
  8.8 0.4 collective-permute-start.2
  9.3 1.3 %collective-permute-done.3.refs_0_ = bf16[64,576]{1,0:T(8,128)(2,1)S(1)} collective-permute-done((bf16[64,576]{1,0:T(8,128)(2,1)S(1)}, bf16[64,576]{1,0:T(8,128)(2,1)S(1)}, u32[]{:S(2)}, u32[]{:S(2)}) %collective-permute-start.3) | collective-permute-done | bytes 73760 | tf_op jit(solution)/shard_map/ppermute | solution.py:258
  10.6 3.4 %collective-permute-start.6 = (bf16[64,576]{1,0:T(8,128)(2,1)S(1)}, bf16[64,576]{1,0:T(8,128)(2,1)S(1)}, u32[]{:S(2)}, u32[]{:S(2)}) collective-permute-start(bf16[64,576]{1,0:T(8,128)(2,1)S(1)} %collective-permute-done.3.refs_0_), channel_id=1, source_target_pairs={{0,6},{1,7},{2,4},{3,5},{4,2},{5,3},{6,0},{7,1},{8,14},{9,15},{10,... | collective-permute-start | bytes 221192 | tf_op jit(solution)/shard_map/ppermute | solution.py:258
  13.9 0.4 collective-permute-start.7
  14.5 0.2 dynamic-slice_bitcast_fusion.refs_5_
  14.8 3.3 %attend.2 = (bf16[64,640]{1,0:T(8,128)(2,1)S(1)}, bf16[64,640]{1,0:T(8,128)(2,1)S(1)}, bf16[64,640]{1,0:T(8,128)(2,1)S(1)}, bf16[64,640]{1,0:T(8,128)(2,1)S(1)}) custom-call(s32[2,128]{1,0:T(2,128)S(1)} %broadcast_in_dim.2.lengths_ref, s32[2,4]{1,0:T(2,128)S(1)} %copy-done.3, bf16[64,576]{1,0:T(8,128)(2,1)S(1)} %select.3.refs_0_, ...), custom_call_target="tpu_custom_call" | custom-call | flops 2281701376 | bytes 4718592 | tf_op jit(solution)/shard_map/attend/pallas_call | solution.py:109
  18.1 0.2 collective-permute-done.7.refs_2_
  18.4 0.5 collective-permute-done.8.refs_3_
  18.8 3.4 %attend.3 = (bf16[64,640]{1,0:T(8,128)(2,1)S(1)}, bf16[64,640]{1,0:T(8,128)(2,1)S(1)}, bf16[64,640]{1,0:T(8,128)(2,1)S(1)}, bf16[64,640]{1,0:T(8,128)(2,1)S(1)}) custom-call(s32[2,128]{1,0:T(2,128)S(1)} %broadcast_in_dim.2.lengths_ref, s32[2,4]{1,0:T(2,128)S(1)} %copy-done.3, bf16[64,576]{1,0:T(8,128)(2,1)S(1)} %collective-permute-done.3.refs_0_, ...), custom_call_target="tpu_custom_call" | custom-call | flops 2281701376 | bytes 4718592 | tf_op jit(solution)/shard_map/attend/pallas_call | solution.py:109
  22.2 2.3 %collective-permute-start.10 = (bf16[64,640]{1,0:T(8,128)(2,1)S(1)}, bf16[64,640]{1,0:T(8,128)(2,1)S(1)}, u32[]{:S(2)}, u32[]{:S(2)}) collective-permute-start(bf16[64,640]{1,0:T(8,128)(2,1)S(1)} %get-tuple-element.57), channel_id=1, source_target_pairs={{0,6},{1,7},{2,4},{3,5},{4,2},{5,3},{6,0},{7,1},{8,14},{9,15},{10,... | collective-permute-start | bytes 245768 | tf_op jit(solution)/shard_map/ppermute | solution.py:258
  24.5 0.8 %collective-permute-start.11 = (bf16[64,640]{1,0:T(8,128)(2,1)S(1)}, bf16[64,640]{1,0:T(8,128)(2,1)S(1)}, u32[]{:S(2)}, u32[]{:S(2)}) collective-permute-start(bf16[64,640]{1,0:T(8,128)(2,1)S(1)} %get-tuple-element.58), channel_id=1, source_target_pairs={{0,2},{1,3},{2,0},{3,1},{4,6},{5,7},{6,4},{7,5},{8,10},{9,11},{10,... | collective-permute-start | bytes 245768 | tf_op jit(solution)/shard_map/ppermute | solution.py:258
  25.3 0.4 collective-permute-start.9
  25.7 2.2 %collective-permute-start.13 = (bf16[64,640]{1,0:T(8,128)(2,1)S(1)}, bf16[64,640]{1,0:T(8,128)(2,1)S(1)}, u32[]{:S(2)}, u32[]{:S(2)}) collective-permute-start(bf16[64,640]{1,0:T(8,128)(2,1)S(1)} %get-tuple-element.60), channel_id=1, source_target_pairs={{0,6},{1,7},{2,4},{3,5},{4,2},{5,3},{6,0},{7,1},{8,14},{9,15},{10,... | collective-permute-start | bytes 245768 | tf_op jit(solution)/shard_map/ppermute | solution.py:258
  28.0 0.5 collective-permute-start.14
  28.5 1.3 %collective-permute-start.15 = (bf16[64,640]{1,0:T(8,128)(2,1)S(1)}, bf16[64,640]{1,0:T(8,128)(2,1)S(1)}, u32[]{:S(2)}, u32[]{:S(2)}) collective-permute-start(bf16[64,640]{1,0:T(8,128)(2,1)S(1)} %get-tuple-element.62), channel_id=1, source_target_pairs={{0,2},{1,3},{2,0},{3,1},{4,6},{5,7},{6,4},{7,5},{8,10},{9,11},{10,... | collective-permute-start | bytes 245768 | tf_op jit(solution)/shard_map/ppermute | solution.py:258
  29.7 0.2 collective-permute-done.11.refs_3_
  30.0 0.3 combine.1
  30.3 2.4 %collective-permute-start.12 = (bf16[72,512]{1,0:T(8,128)(2,1)S(1)}, bf16[72,512]{1,0:T(8,128)(2,1)S(1)}, u32[]{:S(2)}, u32[]{:S(2)}) collective-permute-start(bf16[72,512]{1,0:T(8,128)(2,1)S(1)} %combine.1), channel_id=1, source_target_pairs={{0,8},{1,9},{2,10},{3,11},{4,12},{5,13},{6,14},{7,15},{8,0},{9,1},... | collective-permute-start | bytes 221192 | tf_op jit(solution)/shard_map/ppermute | solution.py:258
  32.7 0.3 collective-permute-done.15.refs_4_
  32.9 2.6 %collective-permute-done.12.refs_0_ = bf16[72,512]{1,0:T(8,128)(2,1)S(1)} collective-permute-done((bf16[72,512]{1,0:T(8,128)(2,1)S(1)}, bf16[72,512]{1,0:T(8,128)(2,1)S(1)}, u32[]{:S(2)}, u32[]{:S(2)}) %collective-permute-start.12) | collective-permute-done | bytes 73760 | tf_op jit(solution)/shard_map/ppermute | solution.py:258
  35.5 0.3 merge.1
  36.0 1.2 %collective-permute-done.16.got_ref = bf16[32,512]{1,0:T(8,128)(2,1)S(1)} collective-permute-done((bf16[32,512]{1,0:T(8,128)(2,1)S(1)}, bf16[32,512]{1,0:T(8,128)(2,1)S(1)}, u32[]{:S(2)}, u32[]{:S(2)}) %collective-permute-start.16) | collective-permute-done | bytes 32800 | tf_op jit(solution)/shard_map/ppermute | solution.py:258
  37.2 2.3 %project.1 = bf16[16,8,448]{2,1,0:T(8,128)(2,1)S(1)} custom-call(bf16[32,512]{1,0:T(8,128)(2,1)S(1)} %get-tuple-element.63.own_ref, bf16[32,512]{1,0:T(8,128)(2,1)S(1)} %collective-permute-done.16.got_ref, bf16[8,512,128]{2,1,0:T(8,128)(2,1)S(1)} %copy-done.1, bf16[1024,7168]{1,0:T(8,128)(2,1)S(1)} %copy-done), custom_call_target="tpu_custom_call" | custom-call | tf_op jit(solution)/shard_map/project/pallas_call | solution.py:225
  39.4 12.2 %all_to_all.5.in_ref = bf16[16,8,448]{2,1,0:T(8,128)(2,1)S(1)} all-to-all(bf16[16,8,448]{2,1,0:T(8,128)(2,1)S(1)} %project.1), channel_id=1, replica_groups=mesh['grp'=2,'ctx'=16] {'ctx'}, dimensions={0} | all-to-all | bytes 229376 | tf_op jit(solution)/shard_map/all_to_all | solution.py:290
  51.6 0.6 %finish.1 = bf16[2,4,448]{2,1,0:T(4,128)(2,1)} custom-call(bf16[16,8,448]{2,1,0:T(8,128)(2,1)S(1)} %all_to_all.5.in_ref), custom_call_target="tpu_custom_call" | custom-call | tf_op jit(solution)/shard_map/finish/pallas_call | solution.py:244
  (23 shorter events, 0.3 us)
Async XLA Ops:
  0.0 14.7 %copy-start.4 = (s32[2]{0:T(128)S(1)}, s32[2]{0:T(128)}, u32[]{:S(2)}) copy-start(s32[2]{0:T(128)} %param.8) | copy-start | bytes 28
  0.0 14.8 %copy-start.3 = (s32[2,4]{1,0:T(2,128)S(1)}, s32[2,4]{1,0:T(2,128)}, u32[]{:S(2)}) copy-start(s32[2,4]{1,0:T(2,128)} %mask_ref.3) | copy-start | bytes 100
  0.0 1.6 %collective-permute-start = (bf16[2,4,8,576]{3,2,1,0:T(8,128)(2,1)}, bf16[2,4,8,576]{3,2,1,0:T(8,128)(2,1)S(1)}, u32[]{:S(2)}, u32[]{:S(2)}) collective-permute-start(bf16[2,4,8,576]{3,2,1,0:T(8,128)(2,1)} %param.6), channel_id=1, source_target_pairs={{0,1},{1,0},{2,3},{3,2},{4,5},{5,4},{6,7},{7,6},{8,9},{9,8},{10,11... | collective-permute-start | bytes 221192 | tf_op jit(solution)/shard_map/ppermute | solution.py:258
  0.5 14.3 %copy-start.2 = (bf16[2,2048,576]{1,2,0:T(8,128)(2,1)S(1)}, bf16[2,2048,576]{1,2,0:T(8,128)(2,1)}, u32[]{:S(2)}) copy-start(bf16[2,2048,576]{1,2,0:T(8,128)(2,1)} %param.7) | copy-start | bytes 14155780
  1.6 12.8 %collective-permute-start.5 = (bf16[2,576,2048]{2,1,0:T(8,128)(2,1)}, bf16[2,576,2048]{2,1,0:T(8,128)(2,1)S(1)}, u32[]{:S(2)}, u32[]{:S(2)}) collective-permute-start(bf16[2,576,2048]{2,1,0:T(8,128)(2,1)} %bitcast.5), channel_id=1, source_target_pairs={{0,1},{1,0},{2,3},{3,2},{4,5},{5,4},{6,7},{7,6},{8,9},{9,8},{10,11... | collective-permute-start | bytes 14155784 | tf_op jit(solution)/shard_map/ppermute | solution.py:258
  2.0 8.6 %collective-permute-start.3 = (bf16[64,576]{1,0:T(8,128)(2,1)S(1)}, bf16[64,576]{1,0:T(8,128)(2,1)S(1)}, u32[]{:S(2)}, u32[]{:S(2)}) collective-permute-start(bf16[64,576]{1,0:T(8,128)(2,1)S(1)} %select.3.refs_0_), channel_id=1, source_target_pairs={{0,8},{1,9},{2,10},{3,11},{4,12},{5,13},{6,14},{7,15},{8,0},{9,1},... | collective-permute-start | bytes 221192 | tf_op jit(solution)/shard_map/ppermute | solution.py:258
  5.8 4.8 %collective-permute-start.4 = (bf16[64,576]{1,0:T(8,128)(2,1)S(1)}, bf16[64,576]{1,0:T(8,128)(2,1)S(1)}, u32[]{:S(2)}, u32[]{:S(2)}) collective-permute-start(bf16[64,576]{1,0:T(8,128)(2,1)S(1)} %select.3.refs_0_), channel_id=1, source_target_pairs={{0,2},{1,3},{2,0},{3,1},{4,6},{5,7},{6,4},{7,5},{8,10},{9,11},{10,... | collective-permute-start | bytes 221192 | tf_op jit(solution)/shard_map/ppermute | solution.py:258
  7.3 7.4 %collective-permute-start.1 = (bf16[64,576]{1,0:T(8,128)(2,1)S(1)}, bf16[64,576]{1,0:T(8,128)(2,1)S(1)}, u32[]{:S(2)}, u32[]{:S(2)}) collective-permute-start(bf16[64,576]{1,0:T(8,128)(2,1)S(1)} %select.3.refs_0_), channel_id=1, source_target_pairs={{0,6},{1,7},{2,4},{3,5},{4,2},{5,3},{6,0},{7,1},{8,14},{9,15},{10,... | collective-permute-start | bytes 221192 | tf_op jit(solution)/shard_map/ppermute | solution.py:258
  8.8 5.9 %collective-permute-start.2 = (bf16[64,576]{1,0:T(8,128)(2,1)S(1)}, bf16[64,576]{1,0:T(8,128)(2,1)S(1)}, u32[]{:S(2)}, u32[]{:S(2)}) collective-permute-start(bf16[64,576]{1,0:T(8,128)(2,1)S(1)} %select.3.refs_0_), channel_id=1, source_target_pairs={{0,4},{1,5},{2,6},{3,7},{4,0},{5,1},{6,2},{7,3},{8,12},{9,13},{10,... | collective-permute-start | bytes 221192 | tf_op jit(solution)/shard_map/ppermute | solution.py:258
  10.6 7.5 %collective-permute-start.6 = (bf16[64,576]{1,0:T(8,128)(2,1)S(1)}, bf16[64,576]{1,0:T(8,128)(2,1)S(1)}, u32[]{:S(2)}, u32[]{:S(2)}) collective-permute-start(bf16[64,576]{1,0:T(8,128)(2,1)S(1)} %collective-permute-done.3.refs_0_), channel_id=1, source_target_pairs={{0,6},{1,7},{2,4},{3,5},{4,2},{5,3},{6,0},{7,1},{8,14},{9,15},{10,... | collective-permute-start | bytes 221192 | tf_op jit(solution)/shard_map/ppermute | solution.py:258
  13.9 4.4 %collective-permute-start.7 = (bf16[64,576]{1,0:T(8,128)(2,1)S(1)}, bf16[64,576]{1,0:T(8,128)(2,1)S(1)}, u32[]{:S(2)}, u32[]{:S(2)}) collective-permute-start(bf16[64,576]{1,0:T(8,128)(2,1)S(1)} %collective-permute-done.3.refs_0_), channel_id=1, source_target_pairs={{0,4},{1,5},{2,6},{3,7},{4,0},{5,1},{6,2},{7,3},{8,12},{9,13},{10,... | collective-permute-start | bytes 221192 | tf_op jit(solution)/shard_map/ppermute | solution.py:258
  14.4 4.4 %collective-permute-start.8 = (bf16[64,576]{1,0:T(8,128)(2,1)S(1)}, bf16[64,576]{1,0:T(8,128)(2,1)S(1)}, u32[]{:S(2)}, u32[]{:S(2)}) collective-permute-start(bf16[64,576]{1,0:T(8,128)(2,1)S(1)} %collective-permute-done.3.refs_0_), channel_id=1, source_target_pairs={{0,2},{1,3},{2,0},{3,1},{4,6},{5,7},{6,4},{7,5},{8,10},{9,11},{10,... | collective-permute-start | bytes 221192 | tf_op jit(solution)/shard_map/ppermute | solution.py:258
  14.8 22.4 %copy-start = (bf16[1024,7168]{1,0:T(8,128)(2,1)S(1)}, bf16[1024,7168]{1,0:T(8,128)(2,1)}, u32[]{:S(2)}) copy-start(bf16[1024,7168]{1,0:T(8,128)(2,1)} %weight_ref.1) | copy-start | bytes 44040196
  18.1 19.0 %copy-start.1 = (bf16[8,512,128]{2,1,0:T(8,128)(2,1)S(1)}, bf16[8,512,128]{2,1,0:T(8,128)(2,1)}, u32[]{:S(2)}) copy-start(bf16[8,512,128]{2,1,0:T(8,128)(2,1)} %up_ref.1) | copy-start | bytes 3145732
  22.2 6.3 %collective-permute-start.10 = (bf16[64,640]{1,0:T(8,128)(2,1)S(1)}, bf16[64,640]{1,0:T(8,128)(2,1)S(1)}, u32[]{:S(2)}, u32[]{:S(2)}) collective-permute-start(bf16[64,640]{1,0:T(8,128)(2,1)S(1)} %get-tuple-element.57), channel_id=1, source_target_pairs={{0,6},{1,7},{2,4},{3,5},{4,2},{5,3},{6,0},{7,1},{8,14},{9,15},{10,... | collective-permute-start | bytes 245768 | tf_op jit(solution)/shard_map/ppermute | solution.py:258
  24.5 5.5 %collective-permute-start.11 = (bf16[64,640]{1,0:T(8,128)(2,1)S(1)}, bf16[64,640]{1,0:T(8,128)(2,1)S(1)}, u32[]{:S(2)}, u32[]{:S(2)}) collective-permute-start(bf16[64,640]{1,0:T(8,128)(2,1)S(1)} %get-tuple-element.58), channel_id=1, source_target_pairs={{0,2},{1,3},{2,0},{3,1},{4,6},{5,7},{6,4},{7,5},{8,10},{9,11},{10,... | collective-permute-start | bytes 245768 | tf_op jit(solution)/shard_map/ppermute | solution.py:258
  25.3 4.7 %collective-permute-start.9 = (bf16[64,640]{1,0:T(8,128)(2,1)S(1)}, bf16[64,640]{1,0:T(8,128)(2,1)S(1)}, u32[]{:S(2)}, u32[]{:S(2)}) collective-permute-start(bf16[64,640]{1,0:T(8,128)(2,1)S(1)} %get-tuple-element.56), channel_id=1, source_target_pairs={{0,4},{1,5},{2,6},{3,7},{4,0},{5,1},{6,2},{7,3},{8,12},{9,13},{10,... | collective-permute-start | bytes 245768 | tf_op jit(solution)/shard_map/ppermute | solution.py:258
  25.7 6.9 %collective-permute-start.13 = (bf16[64,640]{1,0:T(8,128)(2,1)S(1)}, bf16[64,640]{1,0:T(8,128)(2,1)S(1)}, u32[]{:S(2)}, u32[]{:S(2)}) collective-permute-start(bf16[64,640]{1,0:T(8,128)(2,1)S(1)} %get-tuple-element.60), channel_id=1, source_target_pairs={{0,6},{1,7},{2,4},{3,5},{4,2},{5,3},{6,0},{7,1},{8,14},{9,15},{10,... | collective-permute-start | bytes 245768 | tf_op jit(solution)/shard_map/ppermute | solution.py:258
  28.0 4.7 %collective-permute-start.14 = (bf16[64,640]{1,0:T(8,128)(2,1)S(1)}, bf16[64,640]{1,0:T(8,128)(2,1)S(1)}, u32[]{:S(2)}, u32[]{:S(2)}) collective-permute-start(bf16[64,640]{1,0:T(8,128)(2,1)S(1)} %get-tuple-element.61), channel_id=1, source_target_pairs={{0,4},{1,5},{2,6},{3,7},{4,0},{5,1},{6,2},{7,3},{8,12},{9,13},{10,... | collective-permute-start | bytes 245768 | tf_op jit(solution)/shard_map/ppermute | solution.py:258
  28.5 4.4 %collective-permute-start.15 = (bf16[64,640]{1,0:T(8,128)(2,1)S(1)}, bf16[64,640]{1,0:T(8,128)(2,1)S(1)}, u32[]{:S(2)}, u32[]{:S(2)}) collective-permute-start(bf16[64,640]{1,0:T(8,128)(2,1)S(1)} %get-tuple-element.62), channel_id=1, source_target_pairs={{0,2},{1,3},{2,0},{3,1},{4,6},{5,7},{6,4},{7,5},{8,10},{9,11},{10,... | collective-permute-start | bytes 245768 | tf_op jit(solution)/shard_map/ppermute | solution.py:258
  30.3 5.3 %collective-permute-start.12 = (bf16[72,512]{1,0:T(8,128)(2,1)S(1)}, bf16[72,512]{1,0:T(8,128)(2,1)S(1)}, u32[]{:S(2)}, u32[]{:S(2)}) collective-permute-start(bf16[72,512]{1,0:T(8,128)(2,1)S(1)} %combine.1), channel_id=1, source_target_pairs={{0,8},{1,9},{2,10},{3,11},{4,12},{5,13},{6,14},{7,15},{8,0},{9,1},... | collective-permute-start | bytes 221192 | tf_op jit(solution)/shard_map/ppermute | solution.py:258
  35.9 1.3 %collective-permute-start.16 = (bf16[32,512]{1,0:T(8,128)(2,1)S(1)}, bf16[32,512]{1,0:T(8,128)(2,1)S(1)}, u32[]{:S(2)}, u32[]{:S(2)}) collective-permute-start(bf16[32,512]{1,0:T(8,128)(2,1)S(1)} %get-tuple-element.64), channel_id=1, source_target_pairs={{0,1},{1,0},{2,3},{3,2},{4,5},{5,4},{6,7},{7,6},{8,9},{9,8},{10,11... | collective-permute-start | bytes 98312 | tf_op jit(solution)/shard_map/ppermute | solution.py:258

commit v8 on v6

--- a/solution.py
+++ b/solution.py
@@ -204,23 +204,6 @@
     )(own, got, value_up, weight)
 
 
-def finish_kernel(in_ref, out_ref):
-    total = jnp.sum(in_ref[...].astype(jnp.float32), axis=0)
-    spec = out_ref.shape[1]
-    for r in range(out_ref.shape[0]):
-        out_ref[r] = total[r * spec : (r + 1) * spec].astype(out_ref.dtype)
-
-
-def finish(parts, requests):
-    _, rows, columns = parts.shape
-    return pl.pallas_call(
-        finish_kernel,
-        out_shape=jax.ShapeDtypeStruct((requests, rows // requests, columns), jnp.bfloat16),
-        compiler_params=pltpu.CompilerParams(vmem_limit_bytes=8 * MIB),
-        name="finish",
-    )(parts)
-
-
 def on_device(n, queries, latent_cache, lengths, draft_mask, value_up, output_weight):
     requests, spec, heads, feature = queries.shape
     latent = value_up.shape[1]
@@ -260,7 +243,8 @@
     own, give = merge(parts, latent)
     outs = project(own, swap(give, 1), value_up, output_weight, spec, n)
     received = lax.all_to_all(outs, "ctx", 0, 0, tiled=True)
-    return finish(received, requests)
+    total = jnp.sum(received.astype(jnp.float32), axis=0).astype(jnp.bfloat16)
+    return total.reshape(requests, spec, -1)
 
 
 def solution(mesh):

time: 52.5 us -> 52.5 us (level)
  local copies, waits for them, and re-layouts: 1.18 us -> 1.79 us
  Pallas kernels: 10.2 us -> 9.6 us
    pallas_call x1 -> x0, Pallas kernels: 0.62 us -> none  [finish(): pl.pallas_call(finish_kernel, out_shape=jax.ShapeDtypeStruct((requests, r...]
    reshape x0 -> x1, local copies, waits for them, and re-layouts: none -> 0.61 us  [on_device(): return total.reshape(requests, spec, -1)]
where the time goes in v8:
time: 52.5 us; the launch traced here: 52.3 us
  starting transfers between devices  22.1 us (42%)
  blocking collectives  12.2 us (23%)
  Pallas kernels  9.6 us (18%)
  waiting for transfers between devices  6.56 us (12%)
  local copies, waits for them, and re-layouts  1.79 us (3%)
    ppermute x17, starting transfers between devices, swap(): return lax.ppermute(x, 'ctx', [(i, i ^ bits) for i in range(n)])  22.1 us
    all_to_all x1, blocking collectives, on_device(): received = lax.all_to_all(outs, 'ctx', 0, 0, tiled=True)  12.2 us
    pallas_call x2, Pallas kernels, attend(): pl.pallas_call(functools.partial(attend_kernel, chunks, spec, heads, late...  6.74 us
    ppermute x17, waiting for transfers between devices, swap(): return lax.ppermute(x, 'ctx', [(i, i ^ bits) for i in range(n)])  6.56 us
    pallas_call x1, Pallas kernels, project(): pl.pallas_call(functools.partial(project_kernel, heads, group), out_shape...  2.27 us
  transfers between devices with their start and end apart: 17, of which 8 were waited for; matrix products, arithmetic and copies ran while one was open for 2% of the time, Pallas kernels for 7%

profile of v8, /device:TPU:0, one launch (start us, length us, event | category | flops | bytes accessed | tf_op | source)
XLA Modules:
  0.0 52.3 jit_solution(1682969706802438184)
XLA Ops:
  0.0 0.5 collective-permute-start
  0.5 0.9 %dynamic-slice_bitcast_fusion.1.own_ref = bf16[4,8,576]{2,1,0:T(8,128)(2,1)S(1)} fusion(bf16[2,4,8,576]{3,2,1,0:T(8,128)(2,1)} %param.6, s32[]{:T(128)S(6)} %select_n.6), kind=kLoop, calls=%fused_computation.1 | loop fusion | bytes 73732 | tf_op jit(solution)/shard_map/jit(dynamic_index_in_dim)/squeeze | solution.py:217
  1.4 0.2 collective-permute-done.got_ref
  1.6 0.4 collective-permute-start.5
  2.0 3.8 %collective-permute-start.3 = (bf16[64,576]{1,0:T(8,128)(2,1)S(1)}, bf16[64,576]{1,0:T(8,128)(2,1)S(1)}, u32[]{:S(2)}, u32[]{:S(2)}) collective-permute-start(bf16[64,576]{1,0:T(8,128)(2,1)S(1)} %select.3.refs_0_), channel_id=1, source_target_pairs={{0,8},{1,9},{2,10},{3,11},{4,12},{5,13},{6,14},{7,15},{8,0},{9,1},... | collective-permute-start | bytes 221192 | tf_op jit(solution)/shard_map/ppermute | solution.py:213
  5.8 1.5 %collective-permute-start.4 = (bf16[64,576]{1,0:T(8,128)(2,1)S(1)}, bf16[64,576]{1,0:T(8,128)(2,1)S(1)}, u32[]{:S(2)}, u32[]{:S(2)}) collective-permute-start(bf16[64,576]{1,0:T(8,128)(2,1)S(1)} %select.3.refs_0_), channel_id=1, source_target_pairs={{0,2},{1,3},{2,0},{3,1},{4,6},{5,7},{6,4},{7,5},{8,10},{9,11},{10,... | collective-permute-start | bytes 221192 | tf_op jit(solution)/shard_map/ppermute | solution.py:213
  7.3 1.5 %collective-permute-start.1 = (bf16[64,576]{1,0:T(8,128)(2,1)S(1)}, bf16[64,576]{1,0:T(8,128)(2,1)S(1)}, u32[]{:S(2)}, u32[]{:S(2)}) collective-permute-start(bf16[64,576]{1,0:T(8,128)(2,1)S(1)} %select.3.refs_0_), channel_id=1, source_target_pairs={{0,6},{1,7},{2,4},{3,5},{4,2},{5,3},{6,0},{7,1},{8,14},{9,15},{10,... | collective-permute-start | bytes 221192 | tf_op jit(solution)/shard_map/ppermute | solution.py:213
  8.8 0.4 collective-permute-start.2
  9.3 1.3 %collective-permute-done.3.refs_0_ = bf16[64,576]{1,0:T(8,128)(2,1)S(1)} collective-permute-done((bf16[64,576]{1,0:T(8,128)(2,1)S(1)}, bf16[64,576]{1,0:T(8,128)(2,1)S(1)}, u32[]{:S(2)}, u32[]{:S(2)}) %collective-permute-start.3) | collective-permute-done | bytes 73760 | tf_op jit(solution)/shard_map/ppermute | solution.py:213
  10.6 3.4 %collective-permute-start.6 = (bf16[64,576]{1,0:T(8,128)(2,1)S(1)}, bf16[64,576]{1,0:T(8,128)(2,1)S(1)}, u32[]{:S(2)}, u32[]{:S(2)}) collective-permute-start(bf16[64,576]{1,0:T(8,128)(2,1)S(1)} %collective-permute-done.3.refs_0_), channel_id=1, source_target_pairs={{0,6},{1,7},{2,4},{3,5},{4,2},{5,3},{6,0},{7,1},{8,14},{9,15},{10,... | collective-permute-start | bytes 221192 | tf_op jit(solution)/shard_map/ppermute | solution.py:213
  13.9 0.4 collective-permute-start.7
  14.5 0.2 dynamic-slice_bitcast_fusion.refs_5_
  14.8 3.4 %attend.2 = (bf16[64,640]{1,0:T(8,128)(2,1)S(1)}, bf16[64,640]{1,0:T(8,128)(2,1)S(1)}, bf16[64,640]{1,0:T(8,128)(2,1)S(1)}, bf16[64,640]{1,0:T(8,128)(2,1)S(1)}) custom-call(s32[2,128]{1,0:T(2,128)S(1)} %broadcast_in_dim.2.lengths_ref, s32[2,4]{1,0:T(2,128)S(1)} %copy-done.3, bf16[64,576]{1,0:T(8,128)(2,1)S(1)} %select.3.refs_0_, ...), custom_call_target="tpu_custom_call" | custom-call | flops 2281701376 | bytes 4718592 | tf_op jit(solution)/shard_map/attend/pallas_call | solution.py:99
  18.2 0.2 collective-permute-done.7.refs_2_
  18.4 0.5 collective-permute-done.8.refs_3_
  18.8 3.4 %attend.3 = (bf16[64,640]{1,0:T(8,128)(2,1)S(1)}, bf16[64,640]{1,0:T(8,128)(2,1)S(1)}, bf16[64,640]{1,0:T(8,128)(2,1)S(1)}, bf16[64,640]{1,0:T(8,128)(2,1)S(1)}) custom-call(s32[2,128]{1,0:T(2,128)S(1)} %broadcast_in_dim.2.lengths_ref, s32[2,4]{1,0:T(2,128)S(1)} %copy-done.3, bf16[64,576]{1,0:T(8,128)(2,1)S(1)} %collective-permute-done.3.refs_0_, ...), custom_call_target="tpu_custom_call" | custom-call | flops 2281701376 | bytes 4718592 | tf_op jit(solution)/shard_map/attend/pallas_call | solution.py:99
  22.2 2.4 %collective-permute-start.10 = (bf16[64,640]{1,0:T(8,128)(2,1)S(1)}, bf16[64,640]{1,0:T(8,128)(2,1)S(1)}, u32[]{:S(2)}, u32[]{:S(2)}) collective-permute-start(bf16[64,640]{1,0:T(8,128)(2,1)S(1)} %get-tuple-element.57), channel_id=1, source_target_pairs={{0,6},{1,7},{2,4},{3,5},{4,2},{5,3},{6,0},{7,1},{8,14},{9,15},{10,... | collective-permute-start | bytes 245768 | tf_op jit(solution)/shard_map/ppermute | solution.py:213
  24.6 0.7 %collective-permute-start.11 = (bf16[64,640]{1,0:T(8,128)(2,1)S(1)}, bf16[64,640]{1,0:T(8,128)(2,1)S(1)}, u32[]{:S(2)}, u32[]{:S(2)}) collective-permute-start(bf16[64,640]{1,0:T(8,128)(2,1)S(1)} %get-tuple-element.58), channel_id=1, source_target_pairs={{0,2},{1,3},{2,0},{3,1},{4,6},{5,7},{6,4},{7,5},{8,10},{9,11},{10,... | collective-permute-start | bytes 245768 | tf_op jit(solution)/shard_map/ppermute | solution.py:213
  25.3 0.5 collective-permute-start.9
  25.8 2.3 %collective-permute-start.13 = (bf16[64,640]{1,0:T(8,128)(2,1)S(1)}, bf16[64,640]{1,0:T(8,128)(2,1)S(1)}, u32[]{:S(2)}, u32[]{:S(2)}) collective-permute-start(bf16[64,640]{1,0:T(8,128)(2,1)S(1)} %get-tuple-element.60), channel_id=1, source_target_pairs={{0,6},{1,7},{2,4},{3,5},{4,2},{5,3},{6,0},{7,1},{8,14},{9,15},{10,... | collective-permute-start | bytes 245768 | tf_op jit(solution)/shard_map/ppermute | solution.py:213
  28.1 0.5 collective-permute-start.14
  28.5 1.3 %collective-permute-start.15 = (bf16[64,640]{1,0:T(8,128)(2,1)S(1)}, bf16[64,640]{1,0:T(8,128)(2,1)S(1)}, u32[]{:S(2)}, u32[]{:S(2)}) collective-permute-start(bf16[64,640]{1,0:T(8,128)(2,1)S(1)} %get-tuple-element.62), channel_id=1, source_target_pairs={{0,2},{1,3},{2,0},{3,1},{4,6},{5,7},{6,4},{7,5},{8,10},{9,11},{10,... | collective-permute-start | bytes 245768 | tf_op jit(solution)/shard_map/ppermute | solution.py:213
  29.8 0.2 collective-permute-done.11.refs_3_
  30.0 0.3 combine.1
  30.3 2.4 %collective-permute-start.12 = (bf16[64,640]{1,0:T(8,128)(2,1)S(1)}, bf16[64,640]{1,0:T(8,128)(2,1)S(1)}, u32[]{:S(2)}, u32[]{:S(2)}) collective-permute-start(bf16[64,640]{1,0:T(8,128)(2,1)S(1)} %combine.1), channel_id=1, source_target_pairs={{0,8},{1,9},{2,10},{3,11},{4,12},{5,13},{6,14},{7,15},{8,0},{9,1},... | collective-permute-start | bytes 245768 | tf_op jit(solution)/shard_map/ppermute | solution.py:213
  32.7 0.3 collective-permute-done.15.refs_4_
  33.0 2.7 %collective-permute-done.12.refs_0_ = bf16[64,640]{1,0:T(8,128)(2,1)S(1)} collective-permute-done((bf16[64,640]{1,0:T(8,128)(2,1)S(1)}, bf16[64,640]{1,0:T(8,128)(2,1)S(1)}, u32[]{:S(2)}, u32[]{:S(2)}) %collective-permute-start.12) | collective-permute-done | bytes 81952 | tf_op jit(solution)/shard_map/ppermute | solution.py:213
  35.7 0.3 merge.1
  36.0 1.2 %collective-permute-done.16.got_ref = bf16[32,512]{1,0:T(8,128)(2,1)S(1)} collective-permute-done((bf16[32,512]{1,0:T(8,128)(2,1)S(1)}, bf16[32,512]{1,0:T(8,128)(2,1)S(1)}, u32[]{:S(2)}, u32[]{:S(2)}) %collective-permute-start.16) | collective-permute-done | bytes 32800 | tf_op jit(solution)/shard_map/ppermute | solution.py:213
  37.2 2.3 %project.1 = bf16[16,8,448]{2,1,0:T(8,128)(2,1)S(1)} custom-call(bf16[32,512]{1,0:T(8,128)(2,1)S(1)} %get-tuple-element.63.own_ref, bf16[32,512]{1,0:T(8,128)(2,1)S(1)} %collective-permute-done.16.got_ref, bf16[8,512,128]{2,1,0:T(8,128)(2,1)S(1)} %copy-done.1, bf16[1024,7168]{1,0:T(8,128)(2,1)S(1)} %copy-done), custom_call_target="tpu_custom_call" | custom-call | tf_op jit(solution)/shard_map/project/pallas_call | solution.py:197
  39.5 12.2 %all_to_all.5 = bf16[16,8,448]{2,1,0:T(8,128)(2,1)S(1)} all-to-all(bf16[16,8,448]{2,1,0:T(8,128)(2,1)S(1)} %project.1), channel_id=1, replica_groups=mesh['grp'=2,'ctx'=16] {'ctx'}, dimensions={0} | all-to-all | bytes 229376 | tf_op jit(solution)/shard_map/all_to_all | solution.py:245
  51.7 0.6 %reshape.4 = bf16[2,4,448]{2,1,0:T(4,128)(2,1)} reshape(bf16[8,448]{1,0:T(8,128)(2,1)S(1)} %reduce_sum.12) | data formatting | bytes 14336 | tf_op jit(solution)/shard_map/reshape | solution.py:247
  (24 shorter events, 0.3 us)
Async XLA Ops:
  0.0 14.7 %copy-start.4 = (s32[2]{0:T(128)S(1)}, s32[2]{0:T(128)}, u32[]{:S(2)}) copy-start(s32[2]{0:T(128)} %param.8) | copy-start | bytes 28
  0.0 14.8 %copy-start.3 = (s32[2,4]{1,0:T(2,128)S(1)}, s32[2,4]{1,0:T(2,128)}, u32[]{:S(2)}) copy-start(s32[2,4]{1,0:T(2,128)} %mask_ref.3) | copy-start | bytes 100
  0.0 1.6 %collective-permute-start = (bf16[2,4,8,576]{3,2,1,0:T(8,128)(2,1)}, bf16[2,4,8,576]{3,2,1,0:T(8,128)(2,1)S(1)}, u32[]{:S(2)}, u32[]{:S(2)}) collective-permute-start(bf16[2,4,8,576]{3,2,1,0:T(8,128)(2,1)} %param.6), channel_id=1, source_target_pairs={{0,1},{1,0},{2,3},{3,2},{4,5},{5,4},{6,7},{7,6},{8,9},{9,8},{10,11... | collective-permute-start | bytes 221192 | tf_op jit(solution)/shard_map/ppermute | solution.py:213
  0.5 14.3 %copy-start.2 = (bf16[2,2048,576]{1,2,0:T(8,128)(2,1)S(1)}, bf16[2,2048,576]{1,2,0:T(8,128)(2,1)}, u32[]{:S(2)}) copy-start(bf16[2,2048,576]{1,2,0:T(8,128)(2,1)} %param.7) | copy-start | bytes 14155780
  1.6 12.8 %collective-permute-start.5 = (bf16[2,576,2048]{2,1,0:T(8,128)(2,1)}, bf16[2,576,2048]{2,1,0:T(8,128)(2,1)S(1)}, u32[]{:S(2)}, u32[]{:S(2)}) collective-permute-start(bf16[2,576,2048]{2,1,0:T(8,128)(2,1)} %bitcast.5), channel_id=1, source_target_pairs={{0,1},{1,0},{2,3},{3,2},{4,5},{5,4},{6,7},{7,6},{8,9},{9,8},{10,11... | collective-permute-start | bytes 14155784 | tf_op jit(solution)/shard_map/ppermute | solution.py:213
  2.0 8.6 %collective-permute-start.3 = (bf16[64,576]{1,0:T(8,128)(2,1)S(1)}, bf16[64,576]{1,0:T(8,128)(2,1)S(1)}, u32[]{:S(2)}, u32[]{:S(2)}) collective-permute-start(bf16[64,576]{1,0:T(8,128)(2,1)S(1)} %select.3.refs_0_), channel_id=1, source_target_pairs={{0,8},{1,9},{2,10},{3,11},{4,12},{5,13},{6,14},{7,15},{8,0},{9,1},... | collective-permute-start | bytes 221192 | tf_op jit(solution)/shard_map/ppermute | solution.py:213
  5.8 4.8 %collective-permute-start.4 = (bf16[64,576]{1,0:T(8,128)(2,1)S(1)}, bf16[64,576]{1,0:T(8,128)(2,1)S(1)}, u32[]{:S(2)}, u32[]{:S(2)}) collective-permute-start(bf16[64,576]{1,0:T(8,128)(2,1)S(1)} %select.3.refs_0_), channel_id=1, source_target_pairs={{0,2},{1,3},{2,0},{3,1},{4,6},{5,7},{6,4},{7,5},{8,10},{9,11},{10,... | collective-permute-start | bytes 221192 | tf_op jit(solution)/shard_map/ppermute | solution.py:213
  7.3 7.4 %collective-permute-start.1 = (bf16[64,576]{1,0:T(8,128)(2,1)S(1)}, bf16[64,576]{1,0:T(8,128)(2,1)S(1)}, u32[]{:S(2)}, u32[]{:S(2)}) collective-permute-start(bf16[64,576]{1,0:T(8,128)(2,1)S(1)} %select.3.refs_0_), channel_id=1, source_target_pairs={{0,6},{1,7},{2,4},{3,5},{4,2},{5,3},{6,0},{7,1},{8,14},{9,15},{10,... | collective-permute-start | bytes 221192 | tf_op jit(solution)/shard_map/ppermute | solution.py:213
  8.8 5.9 %collective-permute-start.2 = (bf16[64,576]{1,0:T(8,128)(2,1)S(1)}, bf16[64,576]{1,0:T(8,128)(2,1)S(1)}, u32[]{:S(2)}, u32[]{:S(2)}) collective-permute-start(bf16[64,576]{1,0:T(8,128)(2,1)S(1)} %select.3.refs_0_), channel_id=1, source_target_pairs={{0,4},{1,5},{2,6},{3,7},{4,0},{5,1},{6,2},{7,3},{8,12},{9,13},{10,... | collective-permute-start | bytes 221192 | tf_op jit(solution)/shard_map/ppermute | solution.py:213
  10.6 7.6 %collective-permute-start.6 = (bf16[64,576]{1,0:T(8,128)(2,1)S(1)}, bf16[64,576]{1,0:T(8,128)(2,1)S(1)}, u32[]{:S(2)}, u32[]{:S(2)}) collective-permute-start(bf16[64,576]{1,0:T(8,128)(2,1)S(1)} %collective-permute-done.3.refs_0_), channel_id=1, source_target_pairs={{0,6},{1,7},{2,4},{3,5},{4,2},{5,3},{6,0},{7,1},{8,14},{9,15},{10,... | collective-permute-start | bytes 221192 | tf_op jit(solution)/shard_map/ppermute | solution.py:213
  13.9 4.4 %collective-permute-start.7 = (bf16[64,576]{1,0:T(8,128)(2,1)S(1)}, bf16[64,576]{1,0:T(8,128)(2,1)S(1)}, u32[]{:S(2)}, u32[]{:S(2)}) collective-permute-start(bf16[64,576]{1,0:T(8,128)(2,1)S(1)} %collective-permute-done.3.refs_0_), channel_id=1, source_target_pairs={{0,4},{1,5},{2,6},{3,7},{4,0},{5,1},{6,2},{7,3},{8,12},{9,13},{10,... | collective-permute-start | bytes 221192 | tf_op jit(solution)/shard_map/ppermute | solution.py:213
  14.4 4.4 %collective-permute-start.8 = (bf16[64,576]{1,0:T(8,128)(2,1)S(1)}, bf16[64,576]{1,0:T(8,128)(2,1)S(1)}, u32[]{:S(2)}, u32[]{:S(2)}) collective-permute-start(bf16[64,576]{1,0:T(8,128)(2,1)S(1)} %collective-permute-done.3.refs_0_), channel_id=1, source_target_pairs={{0,2},{1,3},{2,0},{3,1},{4,6},{5,7},{6,4},{7,5},{8,10},{9,11},{10,... | collective-permute-start | bytes 221192 | tf_op jit(solution)/shard_map/ppermute | solution.py:213
  14.8 22.4 %copy-start = (bf16[1024,7168]{1,0:T(8,128)(2,1)S(1)}, bf16[1024,7168]{1,0:T(8,128)(2,1)}, u32[]{:S(2)}) copy-start(bf16[1024,7168]{1,0:T(8,128)(2,1)} %weight_ref.1) | copy-start | bytes 44040196
  18.2 19.1 %copy-start.1 = (bf16[8,512,128]{2,1,0:T(8,128)(2,1)S(1)}, bf16[8,512,128]{2,1,0:T(8,128)(2,1)}, u32[]{:S(2)}) copy-start(bf16[8,512,128]{2,1,0:T(8,128)(2,1)} %up_ref.1) | copy-start | bytes 3145732
  22.2 6.3 %collective-permute-start.10 = (bf16[64,640]{1,0:T(8,128)(2,1)S(1)}, bf16[64,640]{1,0:T(8,128)(2,1)S(1)}, u32[]{:S(2)}, u32[]{:S(2)}) collective-permute-start(bf16[64,640]{1,0:T(8,128)(2,1)S(1)} %get-tuple-element.57), channel_id=1, source_target_pairs={{0,6},{1,7},{2,4},{3,5},{4,2},{5,3},{6,0},{7,1},{8,14},{9,15},{10,... | collective-permute-start | bytes 245768 | tf_op jit(solution)/shard_map/ppermute | solution.py:213
  24.6 5.4 %collective-permute-start.11 = (bf16[64,640]{1,0:T(8,128)(2,1)S(1)}, bf16[64,640]{1,0:T(8,128)(2,1)S(1)}, u32[]{:S(2)}, u32[]{:S(2)}) collective-permute-start(bf16[64,640]{1,0:T(8,128)(2,1)S(1)} %get-tuple-element.58), channel_id=1, source_target_pairs={{0,2},{1,3},{2,0},{3,1},{4,6},{5,7},{6,4},{7,5},{8,10},{9,11},{10,... | collective-permute-start | bytes 245768 | tf_op jit(solution)/shard_map/ppermute | solution.py:213
  25.3 4.7 %collective-permute-start.9 = (bf16[64,640]{1,0:T(8,128)(2,1)S(1)}, bf16[64,640]{1,0:T(8,128)(2,1)S(1)}, u32[]{:S(2)}, u32[]{:S(2)}) collective-permute-start(bf16[64,640]{1,0:T(8,128)(2,1)S(1)} %get-tuple-element.56), channel_id=1, source_target_pairs={{0,4},{1,5},{2,6},{3,7},{4,0},{5,1},{6,2},{7,3},{8,12},{9,13},{10,... | collective-permute-start | bytes 245768 | tf_op jit(solution)/shard_map/ppermute | solution.py:213
  25.8 6.9 %collective-permute-start.13 = (bf16[64,640]{1,0:T(8,128)(2,1)S(1)}, bf16[64,640]{1,0:T(8,128)(2,1)S(1)}, u32[]{:S(2)}, u32[]{:S(2)}) collective-permute-start(bf16[64,640]{1,0:T(8,128)(2,1)S(1)} %get-tuple-element.60), channel_id=1, source_target_pairs={{0,6},{1,7},{2,4},{3,5},{4,2},{5,3},{6,0},{7,1},{8,14},{9,15},{10,... | collective-permute-start | bytes 245768 | tf_op jit(solution)/shard_map/ppermute | solution.py:213
  28.1 4.6 %collective-permute-start.14 = (bf16[64,640]{1,0:T(8,128)(2,1)S(1)}, bf16[64,640]{1,0:T(8,128)(2,1)S(1)}, u32[]{:S(2)}, u32[]{:S(2)}) collective-permute-start(bf16[64,640]{1,0:T(8,128)(2,1)S(1)} %get-tuple-element.61), channel_id=1, source_target_pairs={{0,4},{1,5},{2,6},{3,7},{4,0},{5,1},{6,2},{7,3},{8,12},{9,13},{10,... | collective-permute-start | bytes 245768 | tf_op jit(solution)/shard_map/ppermute | solution.py:213
  28.5 4.4 %collective-permute-start.15 = (bf16[64,640]{1,0:T(8,128)(2,1)S(1)}, bf16[64,640]{1,0:T(8,128)(2,1)S(1)}, u32[]{:S(2)}, u32[]{:S(2)}) collective-permute-start(bf16[64,640]{1,0:T(8,128)(2,1)S(1)} %get-tuple-element.62), channel_id=1, source_target_pairs={{0,2},{1,3},{2,0},{3,1},{4,6},{5,7},{6,4},{7,5},{8,10},{9,11},{10,... | collective-permute-start | bytes 245768 | tf_op jit(solution)/shard_map/ppermute | solution.py:213
  30.3 5.4 %collective-permute-start.12 = (bf16[64,640]{1,0:T(8,128)(2,1)S(1)}, bf16[64,640]{1,0:T(8,128)(2,1)S(1)}, u32[]{:S(2)}, u32[]{:S(2)}) collective-permute-start(bf16[64,640]{1,0:T(8,128)(2,1)S(1)} %combine.1), channel_id=1, source_target_pairs={{0,8},{1,9},{2,10},{3,11},{4,12},{5,13},{6,14},{7,15},{8,0},{9,1},... | collective-permute-start | bytes 245768 | tf_op jit(solution)/shard_map/ppermute | solution.py:213
  36.0 1.3 %collective-permute-start.16 = (bf16[32,512]{1,0:T(8,128)(2,1)S(1)}, bf16[32,512]{1,0:T(8,128)(2,1)S(1)}, u32[]{:S(2)}, u32[]{:S(2)}) collective-permute-start(bf16[32,512]{1,0:T(8,128)(2,1)S(1)} %get-tuple-element.64), channel_id=1, source_target_pairs={{0,1},{1,0},{2,3},{3,2},{4,5},{5,4},{6,7},{7,6},{8,9},{9,8},{10,11... | collective-permute-start | bytes 98312 | tf_op jit(solution)/shard_map/ppermute | solution.py:213
